TPU v7x, 32 devices: a whole 2x2x4 slice. The times are simulated.
32 devices in a mesh: grp: 2 (over y), ffn: 4 (over z), hid: 4 (over x, core).
Axes of the slice: x: 2, y: 2, z: 4, core: 2. Of those that a mesh axis runs over, the one named last changes fastest.
Arguments:
- tokens: bfloat16 [4096, 18432], P(('grp', 'ffn'), 'hid'), parts along dimension 0, may hold values from -6 to 6
- query_weight: bfloat16 [18432, 8192], P('hid', 'ffn'), may hold values from -0.046875 to 0.046875
- kv_weight: bfloat16 [18432, 512], P('hid', 'ffn'), may hold values from -0.046875 to 0.046875
Outputs:
- attended: bfloat16 [4096, 8192], P(('grp', 'hid'), 'ffn'), parts along dimension 0
There are 2 independent parts, one for each index of `grp`. A program takes and returns all parts, laid end to end along the dimension named above; an argument that names none is the same for every part. Nothing has to cross between parts.
All inputs are finite; a program needn't handle non-finite values.
Results may differ from a plain program's by a relative error of at most 0.0089.
Values may be sent and summed in bfloat16 or wider, within the bound.
No kernel may reach another device: no remote copies, remote signals or barrier semaphores. Data moves between devices by JAX's collectives and lax.ppermute only.
A program may use at most 192 MiB of HBM per device.

v0:
```python
import jax
import jax.numpy as jnp
from jax import lax
from jax.sharding import PartitionSpec as P

HEAD_DIM = 256
SEQ = 1024


def shards(tokens, query_weight, kv_weight):
    local_rows = tokens.shape[0]
    total_rows = local_rows * lax.axis_size("ffn")
    query_count = total_rows // lax.axis_size("hid")
    heads_here = query_weight.shape[1] // HEAD_DIM
    kv_block = lax.all_gather(kv_weight, "ffn", axis=1, tiled=True)
    kv_partial = jnp.dot(tokens, kv_block, preferred_element_type=jnp.float32)
    kv_summed = lax.psum(kv_partial, "hid")
    shared = lax.all_gather(kv_summed.astype(jnp.bfloat16), "ffn", axis=0, tiled=True)
    keys = shared[:, :HEAD_DIM]
    values = shared[:, HEAD_DIM:]
    query_partial = jnp.dot(
        lax.all_gather(tokens, "ffn", axis=0, tiled=True),
        query_weight,
        preferred_element_type=jnp.float32,
    )
    query_summed = lax.psum_scatter(query_partial, "hid", scatter_dimension=0, tiled=True)
    queries = query_summed.astype(jnp.bfloat16)
    first_row = lax.axis_index("hid") * query_count
    query_pos = first_row + jnp.arange(query_count, dtype=jnp.int32)
    key_pos = jnp.arange(total_rows, dtype=jnp.int32)
    same_prompt = query_pos[:, None] // SEQ == key_pos[None, :] // SEQ
    visible = same_prompt & (key_pos[None, :] <= query_pos[:, None])
    scale = HEAD_DIM ** (-0.5)
    split_heads = queries.reshape(query_count, heads_here, HEAD_DIM)
    scores = (
        jnp.einsum("qhd,kd->hqk", split_heads, keys, preferred_element_type=jnp.float32) * scale
    )
    weights = jnp.where(visible[None, :, :], jnp.exp(scores), jnp.float32(0.0))
    probs = (weights / jnp.sum(weights, axis=2, keepdims=True)).astype(jnp.bfloat16)
    mixed = jnp.einsum("hqk,kd->qhd", probs, values, preferred_element_type=jnp.float32)
    return mixed.reshape(query_count, heads_here * HEAD_DIM).astype(jnp.bfloat16)


def solution(mesh):
    return jax.shard_map(
        shards,
        mesh=mesh,
        in_specs=(P(("grp", "ffn"), "hid"), P("hid", "ffn"), P("hid", "ffn")),
        out_specs=P(("grp", "hid"), "ffn"),
        check_vma=False,
    )
```

profile of v0, /device:TPU:1, one launch (start us, length us, event | category | flops | bytes accessed | tf_op | source)
XLA Modules:
  0.0 637.7 jit_solution(4194464372003260013)
XLA Ops:
  6.5 0.0 all-gather.8.cloned.1.call-start
  6.5 0.7 all-gather.8.cloned.1.call-update
  7.3 0.0 all-gather.4.cloned.1.call-start
  7.3 0.7 all-gather.4.cloned.1.call-update
  8.0 0.0 reduce-scatter.2.cloned.1.call-start
  8.1 325.6 %all-gather.8.cloned.1.call-done = bf16[2048,4608]{1,0:T(8,128)(2,1)} async-done(((bf16[512,4608]{1,0:T(8,128)(2,1)}), bf16[2048,4608]{1,0:T(8,128)(2,1)}) %all-gather.8.cloned.1.call-update) | async-done | bytes 18874384 | tf_op jit(solution)/shard_map/all_gather | solution.py:22
  333.7 47.8 %fusion.16 = f32[2048,2048]{1,0:T(8,128)} fusion(bf16[2048,4608]{1,0:T(8,128)(2,1)} %all-gather.8.cloned.1.call-done, bf16[4608,2048]{1,0:T(8,128)(2,1)} %param.4), kind=kOutput, calls=%fused_computation.31 | convolution fusion | flops 38654705664 | bytes 54525952 | tf_op jit(solution)/shard_map/dot_general | solution.py:21
  381.5 0.0 reduce-scatter.2.cloned.1.call-update
  381.5 0.0 all-gather.6.cloned.1.call-start
  381.6 41.8 %all-gather.4.cloned.1.call-done = bf16[4608,512]{1,0:T(8,128)(2,1)} async-done(((bf16[4608,128]{1,0:T(8,128)(2,1)}), bf16[4608,512]{1,0:T(8,128)(2,1)}) %all-gather.4.cloned.1.call-update) | async-done | bytes 4718608 | tf_op jit(solution)/shard_map/all_gather | solution.py:15
  423.4 5.9 fusion.15
  429.3 27.5 %all-reduce.1 = bf16[512,512]{1,0:T(8,128)(2,1)} all-reduce(f32[512,512]{1,0:T(8,128)S(1)} %fusion.15), channel_id=1, replica_groups=mesh['grp'=2,'ffn'=4,'hid'=4] {'hid'}, use_global_device_ids=true, to_apply=%region_0.0 | all-reduce | flops 262144 | bytes 1572864 | tf_op jit(solution)/shard_map/psum | solution.py:17
  456.8 0.0 all-gather.6.cloned.1.call-update
  456.9 1.0 fusion.2
  457.8 92.5 %reduce-scatter.2.cloned.1.call-done = f32[512,2048]{1,0:T(8,128)} async-done(((f32[2048,2048]{1,0:T(8,128)}), f32[512,2048]{1,0:T(8,128)}) %reduce-scatter.2.cloned.1.call-update) | async-done | bytes 4194320 | tf_op jit(solution)/shard_map/reduce_scatter | solution.py:26
  550.3 2.5 convert_element_type.19
  552.8 45.0 %all-gather.6.cloned.1.call-done = bf16[2048,512]{1,0:T(8,128)(2,1)} async-done(((bf16[512,512]{1,0:T(8,128)(2,1)}), bf16[2048,512]{1,0:T(8,128)(2,1)}) %all-gather.6.cloned.1.call-update) | async-done | bytes 2097168 | tf_op jit(solution)/shard_map/all_gather | solution.py:18
  597.8 15.7 %fusion = (f32[8,512]{1,0:T(8,128)S(1)}, f32[2048,512,8]{1,0,2:T(8,128)}) fusion(pred[512,2048]{0,1:T(8,128)(4,1)S(1)} %fusion.2, bf16[64,8,8,256]{3,2,1,0:T(8,128)(2,1)S(1)} %bitcast.30, bf16[2048,512]{1,0:T(8,128)(2,1)} %all-gather.6.cloned.1.call-done), kind=kOutput, calls=%fused_computation.2 | convolution fusion | flops 4320129024 | bytes 37765120 | tf_op jit(solution)/shard_map/qhd,kd->hqk/dot_general | solution.py:36
  613.5 15.3 %fusion.6 = bf16[256,8,512]{2,0,1:T(8,128)(2,1)S(1)} fusion(f32[2048,512,8]{1,0,2:T(8,128)} %get-tuple-element.6, f32[8,512]{1,0:T(8,128)S(1)} %get-tuple-element.5, pred[512,2048]{0,1:T(8,128)(4,1)S(1)} %fusion.2, bf16[2048,512]{1,0:T(8,128)(2,1)} %all-gather.6.cloned.1.call-done), kind=kOutput, calls=%fused_computation.9 | convolution fusion | flops 4329570304 | bytes 37765120 | tf_op jit(solution)/shard_map/hqk,kd->qhd/dot_general | solution.py:40
  628.8 2.4 copy.7
  (2 shorter events, 0.0 us)
Async XLA Ops:
  6.5 327.1 %all-gather.8.cloned.1.call-start = ((), (), s32[]{:S(2)}) async-start(), calls=%async_computation.3 | async-start | bytes 23592960 | tf_op jit(solution)/shard_map/all_gather | solution.py:22
  7.3 416.1 %all-gather.4.cloned.1.call-start = ((), (), s32[]{:S(2)}) async-start(), calls=%async_computation.1 | async-start | bytes 5898240 | tf_op jit(solution)/shard_map/all_gather | solution.py:15
  8.0 542.3 %reduce-scatter.2.cloned.1.call-start = ((), (), s32[]{:S(2)}) async-start(), calls=%async_computation.4 | async-start | bytes 20971520 | tf_op jit(solution)/shard_map/reduce_scatter | solution.py:26
  381.5 216.3 %all-gather.6.cloned.1.call-start = ((), (), s32[]{:S(2)}) async-start(), calls=%async_computation.2 | async-start | bytes 2621440 | tf_op jit(solution)/shard_map/all_gather | solution.py:18
Sparse Core Ops, SparseCore 0:
  8.9 324.6 all-gather.7
  335.2 88.0 all-gather.3
  425.9 124.3 reduce-scatter.1
  551.8 45.9 all-gather.5
where the time goes:
time: 639 us; the launch traced here: 638 us
  waiting for transfers between devices  506 us (79%)
  matrix products  84.7 us (13%)
  blocking collectives  27.5 us (4%)
  between operations  13.2 us (2%)
    all_gather x1, waiting for transfers between devices, shards(): lax.all_gather(tokens, 'ffn', axis=0, tiled=True)  326 us
    reduce_scatter x1, waiting for transfers between devices, shards(): lax.psum_scatter(query_partial, 'hid', scatter_dimension=0, tiled=True)  92.5 us
    dot_general x1, matrix products, shards(): jnp.dot(lax.all_gather(tokens, 'ffn', axis=0, tiled=True), query_weight,...  47.8 us
    all_gather x1, waiting for transfers between devices, shards(): lax.all_gather(kv_summed.astype(jnp.bfloat16), 'ffn', axis=0, tiled=True)  45 us
    all_gather x1, waiting for transfers between devices, shards(): kv_block = lax.all_gather(kv_weight, 'ffn', axis=1, tiled=True)  41.8 us
    psum x1, blocking collectives, shards(): kv_summed = lax.psum(kv_partial, 'hid')  27.5 us
    dot_general x1, matrix products, shards(): jnp.einsum('qhd,kd->hqk', split_heads, keys, preferred_element_type=jnp.f...  15.7 us
    dot_general x1, matrix products, shards(): jnp.einsum('hqk,kd->qhd', probs, values, preferred_element_type=jnp.float32)  15.3 us
  transfers between devices with their start and end apart: 4, of which 4 were waited for; matrix products, arithmetic and copies ran while one was open for 9% of the time, Pallas kernels for 0%

commit v1 on v0

--- a/solution.py
+++ b/solution.py
@@ -1,13 +1,18 @@
+import functools
+
 import jax
 import jax.numpy as jnp
 from jax import lax
+from jax.experimental import pallas as pl
+from jax.experimental.pallas import tpu as pltpu
 from jax.sharding import PartitionSpec as P
 
 HEAD_DIM = 256
 SEQ = 1024
-
-
-def shards(tokens, query_weight, kv_weight):
+F32, BF16 = jnp.float32, jnp.bfloat16
+
+
+def general(tokens, query_weight, kv_weight):
     local_rows = tokens.shape[0]
     total_rows = local_rows * lax.axis_size("ffn")
     query_count = total_rows // lax.axis_size("hid")
@@ -41,9 +46,419 @@
     return mixed.reshape(query_count, heads_here * HEAD_DIM).astype(jnp.bfloat16)
 
 
+def attention_kernel(rows, where_ref, q_ref, kv_ref, o_ref):
+    tile = rows // 2
+    later = where_ref[0]
+    scale = HEAD_DIM ** (-0.5) * 1.4426950408889634
+    row = lax.broadcasted_iota(jnp.int32, (tile, tile), 0)
+    col = lax.broadcasted_iota(jnp.int32, (tile, tile), 1)
+    seen = col <= row
+
+    def strip(first, count):
+        q = q_ref[pl.ds(first * tile, tile), :]
+        keys = kv_ref[: count * tile, :HEAD_DIM]
+        values = kv_ref[: count * tile, HEAD_DIM:]
+        s = lax.dot_general(q, keys, (((1,), (1,)), ((), ())), preferred_element_type=F32)
+        last = jnp.where(seen, s[:, (count - 1) * tile :], -jnp.inf)
+        s = last if count == 1 else jnp.concatenate([s[:, : (count - 1) * tile], last], axis=1)
+        top = jnp.max(s, axis=1, keepdims=True)
+        w = jnp.exp2((s - top) * scale)
+        total = jnp.sum(w, axis=1, keepdims=True)
+        mixed = jnp.dot(w.astype(BF16), values, preferred_element_type=F32)
+        o_ref[pl.ds(first * tile, tile), :] = (mixed / total).astype(BF16)
+
+    @pl.when(later == 0)
+    def _():
+        strip(0, 1)
+        strip(1, 2)
+
+    @pl.when(later == 1)
+    def _():
+        strip(0, 3)
+        strip(1, 4)
+
+
+def attention(later, queries, shared):
+    rows, width = queries.shape
+    return pl.pallas_call(
+        functools.partial(attention_kernel, rows),
+        out_shape=jax.ShapeDtypeStruct(queries.shape, BF16),
+        grid_spec=pltpu.PrefetchScalarGridSpec(
+            num_scalar_prefetch=1,
+            grid=(width // HEAD_DIM,),
+            in_specs=[
+                pl.BlockSpec((rows, HEAD_DIM), lambda i, _: (0, i)),
+                pl.BlockSpec(shared.shape, lambda i, _: (0, 0)),
+            ],
+            out_specs=pl.BlockSpec((rows, HEAD_DIM), lambda i, _: (0, i)),
+        ),
+        compiler_params=pltpu.CompilerParams(vmem_limit_bytes=32 * 2**20),
+        cost_estimate=pl.CostEstimate(flops=6 * 10**9, bytes_accessed=5 * 10**6, transcendentals=3 * 10**6),
+    )(later.reshape(1).astype(jnp.int32), queries, shared)
+
+
+MID = [(1, 2), (2, 1)]
+INTO = [(0, 1), (3, 2)]
+OUT = [(1, 0), (2, 3)]
+ORDER = ((0, 1, 2, 3), (1, 2, 1, 2), (2, 0, 3, 1), (3, 3, 0, 0))
+
+
+def gate(xs, deps):
+    deps = [x for x in deps if x is not None]
+    return lax.optimization_barrier((tuple(xs), tuple(deps)))[0]
+
+
+class Steps:
+    def __init__(self):
+        self.last, self.before, self.now, self.arrived = None, [], [], []
+
+    def step(self):
+        self.before, self.now = self.now, []
+
+    def start(self, move, x):
+        (x,) = gate((x,), (self.last,))
+        self.now.append(move(x))
+        return self.now[-1]
+
+    def land(self):
+        self.arrived = self.before
+
+    def run(self, work, *xs):
+        xs = gate(xs, [self.last] + self.arrived)
+        out = work(*xs)
+        self.last, self.arrived = jax.tree.leaves(out)[0], []
+        return out
+
+
+def to_core(x, blocks):
+    pairs = []
+    for z, block in enumerate(blocks):
+        core = block % 2
+        pairs += [(z * 4 + chip * 2 + 1 - core, z * 4 + chip * 2 + core) for chip in range(2)]
+    return lax.ppermute(x, ("ffn", "hid"), pairs)
+
+
+def to_chip(x, blocks):
+    pairs = [(z * 4 + (block ^ 2), z * 4 + block) for z, block in enumerate(blocks)]
+    return lax.ppermute(x, ("ffn", "hid"), pairs)
+
+
+def to_end(x, blocks):
+    pairs = [(z * 4 + blocks[z], end * 4 + blocks[z]) for z, end in OUT]
+    return lax.ppermute(x, ("ffn", "hid"), pairs)
+
+
+def gathered(x):
+    z = lax.axis_index("ffn")
+    got = [x] + [lax.ppermute(x, "ffn", [(i, i ^ k) for i in range(4)]) for k in (1, 2, 3)]
+    columns = []
+    for i in range(4):
+        column = got[0]
+        for k in (1, 2, 3):
+            column = jnp.where((z ^ i) == k, got[k], column)
+        columns.append(column)
+    return jnp.concatenate(columns, 1)
+
+
+TILE = 512
+
+
+def product_kernel(terms, sums, kinds, heads, sp_ref, *refs):
+    refs = list(refs)
+    loaded = []
+    for pieces, weights in terms:
+        xs = [[refs.pop(0) for _ in range(n)] for n in pieces]
+        if weights == "help":
+            ws = [refs.pop(0) for _ in range(8)]
+            loaded.append((xs, ws, None))
+        else:
+            ws = [refs.pop(0) for _ in weights]
+            loaded.append((xs, ws, [refs.pop(0) for _ in weights]))
+    outs = [[refs.pop(0) for _ in kinds] for _ in sums]
+    kept = refs
+    j = pl.program_id(0)
+    inner = sp_ref[0] == 1
+
+    @pl.when(j == 0)
+    def _():
+        for (xs, _, _), keep in zip(loaded, kept):
+            at = 0
+            for piece in xs:
+                m = piece[0].shape[0]
+                x = piece[0][...]
+                if len(piece) == 2:
+                    x = jnp.where(inner, x, piece[1][...])
+                keep[pl.ds(at, m), :] = x
+                at += m
+
+    def total(chosen, part):
+        acc = None
+        for i in chosen:
+            _, ws, kvs = loaded[i]
+            at = 0
+            for k, w in enumerate(ws):
+                if part == "heads":
+                    w = w[...]
+                else:
+                    w = w[:, : heads[1]] if kvs is None else kvs[k][...]
+                x = kept[i][:, at : at + w.shape[0]]
+                at += w.shape[0]
+                y = jnp.dot(x, w, preferred_element_type=F32)
+                acc = y if acc is None else acc + y
+        return acc
+
+    @pl.when(j < heads[0])
+    def _():
+        for chosen, out in zip(sums, outs):
+            acc = total(chosen, "heads")
+            for o in out:
+                o[...] = acc.astype(o.dtype)
+
+    @pl.when(j == heads[0])
+    def _():
+        for chosen, out in zip(sums, outs):
+            acc = total(chosen, "kv")
+            for o in out:
+                o[:, : heads[1]] = acc.astype(o.dtype)
+
+
+def product(sp, query_weight, kv_weight, terms, sums, kinds=(F32, BF16)):
+    width, kv_width = query_weight.shape[1], kv_weight.shape[1]
+    tiles = width // TILE
+    args, specs, shape, scratch, flops = [], [], [], [], 0
+
+    def own(at, size, columns, which):
+        def index(j, sp):
+            return (at if isinstance(at, int) else pl.multiple_of(sp[at[0]], 128), jnp.minimum(j, tiles - 1) * TILE if which else 0)
+
+        return pl.BlockSpec((pl.Element(size), pl.Element(columns)), index)
+
+    for pieces, weights in terms:
+        for piece in pieces:
+            for x in piece:
+                args.append(x)
+                specs.append(pl.BlockSpec(x.shape, lambda j, sp: (0, 0)))
+        rows = sum(piece[0].shape[0] for piece in pieces)
+        depth = pieces[0][0].shape[1]
+        scratch.append(pltpu.VMEM((rows, depth), BF16))
+        flops += 2 * rows * depth * (width + kv_width)
+        if isinstance(weights[0], tuple):
+            args += [query_weight] * len(weights) + [kv_weight] * len(weights)
+            specs += [own(at, size, TILE, True) for at, size in weights]
+            specs += [own(at, size, kv_width, False) for at, size in weights]
+            shape.append((tuple(len(p) for p in pieces), tuple(weights)))
+        else:
+            args += list(weights)
+            specs += [pl.BlockSpec((w.shape[0], TILE), lambda j, sp: (0, j)) for w in weights]
+            shape.append((tuple(len(p) for p in pieces), "help"))
+    rows = [scratch[chosen[0]].shape[0] for chosen in sums]
+    out = pl.pallas_call(
+        functools.partial(product_kernel, shape, sums, kinds, (tiles, kv_width)),
+        out_shape=[jax.ShapeDtypeStruct((m, width + kv_width), k) for m in rows for k in kinds],
+        grid_spec=pltpu.PrefetchScalarGridSpec(
+            num_scalar_prefetch=1,
+            grid=(tiles + 1,),
+            in_specs=specs,
+            out_specs=[pl.BlockSpec((m, TILE), lambda j, sp: (0, j)) for m in rows for _ in kinds],
+            scratch_shapes=scratch,
+        ),
+        compiler_params=pltpu.CompilerParams(vmem_limit_bytes=48 * 2**20),
+        cost_estimate=pl.CostEstimate(
+            flops=flops // 2, bytes_accessed=flops // 1000, transcendentals=0
+        ),
+    )(sp, *args)
+    out = [tuple(out[i : i + len(kinds)]) for i in range(0, len(out), len(kinds))]
+    return out[0] if len(out) == 1 else out
+
+
+def along(axis, pairs):
+    return lambda x: lax.ppermute(x, axis, pairs)
+
+
+def staged(tokens, query_weight, kv_weight):
+    rows, depth = tokens.shape
+    width = query_weight.shape[1]
+    z, hid, grp = (lax.axis_index(name) for name in ("ffn", "hid", "grp"))
+    inner = (z == 1) | (z == 2)
+    part = depth * 2 // 9 // 128 * 128
+    first = depth - 2 * part
+    halves = ((0, rows // 2), (rows // 2, rows // 2))
+    mid, into, out = along("ffn", MID), along("ffn", INTO), along("ffn", OUT)
+    across = along("grp", [(0, 1), (1, 0)])
+    core = [functools.partial(to_core, blocks=blocks) for blocks in ORDER]
+    far = [functools.partial(to_chip, blocks=blocks) for blocks in ORDER]
+    home = [functools.partial(to_end, blocks=blocks) for blocks in ORDER]
+
+    own_at, far_at = first + grp * part, first + (1 - grp) * part
+    sp = jnp.stack([inner.astype(jnp.int32), own_at, far_at]).astype(jnp.int32)
+    weights1 = ((0, first),)
+    weights2 = (((1,), part), ((2,), part))
+
+    def both(x):
+        return x, x.astype(BF16)
+
+    def added(x, y):
+        return both(x + y.astype(F32))
+
+    def rounded(x, y):
+        return (x + y.astype(F32)).astype(BF16)
+
+    def make(terms, sums=((0, 1),)):
+        return product(sp, query_weight, kv_weight, terms, sums)
+
+    quarter = part // 4
+
+    def weights_at(i):
+        return jnp.concatenate(
+            [
+                lax.dynamic_slice_in_dim(w, own_at + i * quarter, quarter, 0)
+                for w in (query_weight, kv_weight)
+            ],
+            1,
+        )
+
+    s = Steps()
+    t1 = [tokens[a : a + m, :first] for a, m in halves]
+    t2 = [
+        jnp.concatenate(
+            [lax.dynamic_slice(tokens, (a, at), (m, part)) for at in (own_at, far_at)], 1
+        )
+        for a, m in halves
+    ]
+
+    b1 = [s.start(mid, t1[0])]
+    e1 = [s.start(out, t1[0])]
+    w_in = [s.start(into, weights_at(0))]
+    q_a, q_a16 = s.run(lambda x: make([([(x,)], ((0, depth),))], ((0,),)), tokens)
+    s.step()
+    b1.append(s.start(mid, t1[1]))
+    e1.append(s.start(out, t1[1]))
+    w_in.append(s.start(into, weights_at(1)))
+    c_a = s.start(core[0], q_a16)
+    s.land()
+    w_far = [s.start(across, w_in[0])]
+    f1 = [s.start(out, b1[0])]
+    mark = s.run(lambda x, y: x[:16, :128] + y[:16, :128], b1[0], w_in[0])
+    s.step()
+    b2 = [s.start(mid, t2[0])]
+    w_in.append(s.start(into, weights_at(2)))
+    s.land()
+    w_far.append(s.start(across, w_in[1]))
+    f1.append(s.start(out, b1[1]))
+    q_a, q_a16 = s.run(added, q_a, c_a)
+    s.step()
+    b2.append(s.start(mid, t2[1]))
+    w_in.append(s.start(into, weights_at(3)))
+    x_a = s.start(far[0], q_a16)
+    s.land()
+    w_far.append(s.start(across, w_in[2]))
+    mark = s.run(lambda x, y: x[:16, :128] + y[:16, :128], b1[1], w_in[2])
+    s.step()
+    c1 = [s.start(into, t1[0])]
+    s.land()
+    w_far.append(s.start(across, w_in[3]))
+    q_b, q_b16 = s.run(
+        lambda *x: make([([(x[0], x[2]), (x[1], x[3])], weights1), ([(x[4],), (x[5],)], weights2)]),
+        *b1, *e1, *b2,
+    )
+    s.step()
+    c1.append(s.start(into, t1[1]))
+    c_b = s.start(core[1], q_b16)
+    s.land()
+    d1 = [s.start(mid, c1[0])]
+    help_ab = s.run(
+        lambda *x: make(
+            [([(x[0],), (x[1],)], x[4:]), ([(x[2],), (x[3],)], x[4:])], ((0,), (1,))
+        ),
+        *t2, *b2, *w_in, *w_far,
+    )
+    (h_a, h_a16), (h_b, h_b16) = help_ab
+    s.step()
+    c2 = [s.start(into, t2[0])]
+    c_ha = s.start(core[0], h_a16)
+    c_hb = s.start(core[1], h_b16)
+    s.land()
+    d1.append(s.start(mid, c1[1]))
+    q_b, q_b16 = s.run(added, q_b, c_b)
+    s.step()
+    c2.append(s.start(into, t2[1]))
+    x_b = s.start(far[1], q_b16)
+    s.land()
+    d2 = [s.start(mid, c2[0])]
+    g1 = [s.start(out, d1[0])]
+    h_a, h_a16 = s.run(added, h_a, c_ha)
+    h_b, h_b16 = s.run(added, h_b, c_hb)
+    s.step()
+    x_ha = s.start(far[0], h_a16)
+    x_hb = s.start(far[1], h_b16)
+    s.land()
+    d2.append(s.start(mid, c2[1]))
+    g1.append(s.start(out, d1[1]))
+
+    def last(*x):
+        return make(
+            [([(x[0], x[1])], weights1), ([(x[2],)], weights2), ([(x[2],)], x[3:])], ((2,), (0, 1))
+        )
+
+    (h_d0, h_d016), (q_d0, q_d016) = s.run(last, d1[0], g1[0], d2[0], *w_in, *w_far)
+    q_c, q_c16 = s.run(
+        lambda *x: make([([(x[0], x[2]), (x[1], x[3])], weights1), ([(x[4],), (x[5],)], weights2)]),
+        *c1, *f1, *c2,
+    )
+    s.step()
+    c_hd0 = s.start(core[3], h_d016)
+    c_d0 = s.start(core[3], q_d016)
+    c_c = s.start(core[2], q_c16)
+    s.land()
+    (h_d1, h_d116), (q_d1, q_d116) = s.run(last, d1[1], g1[1], d2[1], *w_in, *w_far)
+    h_a = s.run(rounded, h_a, x_ha)
+    h_b = s.run(rounded, h_b, x_hb)
+    s.step()
+    c_hd1 = s.start(core[3], h_d116)
+    c_d1 = s.start(core[3], q_d116)
+    o_ha = s.start(home[0], h_a)
+    o_hb = s.start(home[1], h_b)
+    s.land()
+    h_d0, h_d016 = s.run(added, h_d0, c_hd0)
+    q_d0, q_d016 = s.run(added, q_d0, c_d0)
+    q_c, q_c16 = s.run(added, q_c, c_c)
+    s.step()
+    x_hd0 = s.start(far[3], h_d016)
+    x_d0 = s.start(far[3], q_d016)
+    x_c = s.start(far[2], q_c16)
+    h_d1, h_d116 = added(h_d1, c_hd1)
+    q_d1, q_d116 = added(q_d1, c_d1)
+    x_hd1 = far[3](h_d116)
+    x_d1 = far[3](q_d116)
+    o_hd0 = home[3](rounded(h_d0, x_hd0))
+    o_hd1 = home[3](rounded(h_d1, x_hd1))
+
+    late = [
+        (q + x.astype(F32) + o.astype(F32)).astype(BF16)
+        for q, x, o in ((q_d0, x_d0, o_hd0), (q_d1, x_d1, o_hd1))
+    ]
+    block = jnp.concatenate(late, 0)
+    stages = (
+        q_a + x_a.astype(F32),
+        q_b + x_b.astype(F32) + o_ha.astype(F32),
+        q_c + x_c.astype(F32) + o_hb.astype(F32),
+    )
+    for stage, order in zip(stages, ORDER):
+        here = sum(jnp.where(z == i, b, 0) for i, b in enumerate(order)) == hid
+        block = jnp.where(here, stage.astype(BF16), block)
+    kv_mine = gathered(block[:, width:])
+    kv_other = lax.ppermute(kv_mine, "hid", [(i, i ^ 1) for i in range(4)])
+    which = hid % 2
+    shared = jnp.concatenate(
+        [jnp.where(which == 0, kv_mine, kv_other), jnp.where(which == 0, kv_other, kv_mine)], 0
+    )
+    return attention(which, block[:, :width], shared)
+
+
 def solution(mesh):
+    fits = mesh.shape["ffn"] == 4 and mesh.shape["hid"] == 4 and mesh.shape["grp"] == 2
     return jax.shard_map(
-        shards,
+        staged if fits else general,
         mesh=mesh,
         in_specs=(P(("grp", "ffn"), "hid"), P("hid", "ffn"), P("hid", "ffn")),
         out_specs=P(("grp", "hid"), "ffn"),

time: 639 us -> 493 us (0.77)
  waiting for transfers between devices: 506 us -> 178 us
  starting transfers between devices: 0.12 us -> 134 us
  Pallas kernels: 0 us -> 115 us
  matrix products: 84.7 us -> 0 us
  other arithmetic: 3.47 us -> 50.8 us
  blocking collectives: 27.5 us -> 0 us
  between operations: 13.2 us -> 0.82 us
  local copies, waits for them, and re-layouts: 2.38 us -> 12.8 us
    all_gather x3 -> x0, waiting for transfers between devices: 412 us -> none  [the longest x1 326 us: shards(): lax.all_gather(tokens, 'ffn', axis=0, tiled=True)]
    ppermute x0 -> x52, waiting for transfers between devices: none -> 178 us  [the longest x26 110 us: along(): return lambda x: lax.ppermute(x, axis, pairs)]
    ppermute x0 -> x52, starting transfers between devices: none -> 134 us  [the longest x26 66.3 us: along(): return lambda x: lax.ppermute(x, axis, pairs)]
    pallas_call x0 -> x7, Pallas kernels: none -> 115 us  [the longest x6 103 us: product(): pl.pallas_call(functools.partial(product_kernel, shape, sums, kinds, (til...]
    reduce_scatter x1 -> x0, waiting for transfers between devices: 92.5 us -> none  [shards(): lax.psum_scatter(query_partial, 'hid', scatter_dimension=0, tiled=True)]
    dot_general x4 -> x0, matrix products: 84.7 us -> none  [the longest x1 47.8 us: shards(): jnp.dot(lax.all_gather(tokens, 'ffn', axis=0, tiled=True), query_weight,...]
    convert_element_type x1 -> x15, other arithmetic: 2.5 us -> 38.1 us  [the longest x9 22.2 us: both(): return (x, x.astype(BF16))]
    psum x1 -> x0, blocking collectives: 27.5 us -> none  [shards(): kv_summed = lax.psum(kv_partial, 'hid')]
  transfers between devices with their start and end apart: 4 -> 52, of which waited for: 4 -> 17; matrix products, arithmetic and copies ran while one was open for 9% -> 8% of each run, Pallas kernels for 0% -> 18%
where the time goes in v1:
time: 493 us; the launch traced here: 492 us
  waiting for transfers between devices  178 us (36%)
  starting transfers between devices  134 us (27%)
  Pallas kernels  115 us (23%)
  other arithmetic  50.8 us (10%)
  local copies, waits for them, and re-layouts  12.8 us (3%)
    ppermute x26, waiting for transfers between devices, along(): return lambda x: lax.ppermute(x, axis, pairs)  110 us
    pallas_call x6, Pallas kernels, product(): pl.pallas_call(functools.partial(product_kernel, shape, sums, kinds, (til...  103 us
    ppermute x26, starting transfers between devices, along(): return lambda x: lax.ppermute(x, axis, pairs)  66.3 us
    ppermute x9, waiting for transfers between devices, to_chip(): return lax.ppermute(x, ('ffn', 'hid'), pairs)  62.7 us
    convert_element_type x9, other arithmetic, both(): return (x, x.astype(BF16))  22.2 us
    ppermute x9, starting transfers between devices, to_core(): return lax.ppermute(x, ('ffn', 'hid'), pairs)  20.5 us
    ppermute x9, starting transfers between devices, to_chip(): return lax.ppermute(x, ('ffn', 'hid'), pairs)  19.8 us
    ppermute x1, starting transfers between devices, staged(): kv_other = lax.ppermute(kv_mine, 'hid', [(i, i ^ 1) for i in range(4)])  17.3 us
  transfers between devices with their start and end apart: 52, of which 17 were waited for; matrix products, arithmetic and copies ran while one was open for 8% of the time, Pallas kernels for 18%

profile of v1, /device:TPU:1, one launch (start us, length us, event | category | flops | bytes accessed | tf_op | source)
XLA Modules:
  0.0 491.6 jit_solution(1736628745165244607)
XLA Ops:
  0.0 3.4 fusion.12
  3.4 1.7 collective-permute-start.1
  6.4 4.2 constant_dynamic-slice_fusion.1
  11.8 6.6 %collective-permute-start.2 = (bf16[256,2176]{1,0:T(8,128)(2,1)}, bf16[256,2176]{1,0:T(8,128)(2,1)S(1)}, u32[]{:S(2)}, u32[]{:S(2)}) collective-permute-start(bf16[256,2176]{1,0:T(8,128)(2,1)} %pad_maximum_fusion.1), channel_id=1, source_target_pairs={{0,4},{12,8},{1,5},{13,9},{2,6},{14,10},{3,7},{15,11},{16,20},{28,... | collective-permute-start | bytes 3342344 | tf_op jit(solution)/shard_map/ppermute | solution.py:275
  18.5 17.7 %shard_map.37 = (f32[512,2176]{1,0:T(8,128)}, bf16[512,2176]{1,0:T(8,128)(2,1)}) custom-call(s32[3]{0:T(128)S(1)} %pad_add_fusion.sp_ref, bf16[512,4608]{1,0:T(8,128)(2,1)} %refs_0_, bf16[4608,2048]{1,0:T(8,128)(2,1)} %refs_6_.3, bf16[4608,128]{1,0:T(8,128)(2,1)S(1)} %copy-done), custom_call_target="tpu_custom_call" | custom-call | flops 5133828096 | bytes 10267656 | tf_op jit(solution)/shard_map/pallas_call | solution.py:255
  38.8 4.6 collective-permute-start.5
  43.4 1.7 collective-permute-start
  46.4 18.9 %collective-permute-done.7.refs_3_.refs_13_.refs_11_ = bf16[256,2176]{1,0:T(8,128)(2,1)S(1)} collective-permute-done((bf16[256,2176]{1,0:T(8,128)(2,1)S(1)}, bf16[256,2176]{1,0:T(8,128)(2,1)S(1)}, u32[]{:S(2)}, u32[]{:S(2)}) %collective-permute-start.7) | collective-permute-done | bytes 1114144 | tf_op jit(solution)/shard_map/ppermute | solution.py:275
  68.0 1.8 constant_dynamic-slice_fusion.11
  69.9 5.5 %collective-permute-start.4 = (bf16[256,2176]{1,0:T(8,128)(2,1)S(1)}, bf16[256,2176]{1,0:T(8,128)(2,1)S(1)}, u32[]{:S(2)}, u32[]{:S(2)}) collective-permute-start(bf16[256,2176]{1,0:T(8,128)(2,1)S(1)} %copy-done.22), channel_id=1, source_target_pairs={{0,4},{12,8},{1,5},{13,9},{2,6},{14,10},{3,7},{15,11},{16,20},{28,... | collective-permute-start | bytes 3342344 | tf_op jit(solution)/shard_map/ppermute | solution.py:275
  76.2 14.8 %collective-permute-done.8.refs_6_.refs_16_.refs_14_ = bf16[256,2176]{1,0:T(8,128)(2,1)} collective-permute-done((bf16[256,2176]{1,0:T(8,128)(2,1)S(1)}, bf16[256,2176]{1,0:T(8,128)(2,1)}, u32[]{:S(2)}, u32[]{:S(2)}) %collective-permute-start.8) | collective-permute-done | bytes 1114144 | tf_op jit(solution)/shard_map/ppermute | solution.py:275
  91.0 11.5 %collective-permute-done.9.refs_1_ = bf16[256,2560]{1,0:T(8,128)(2,1)} collective-permute-done((bf16[256,2560]{1,0:T(8,128)(2,1)}, bf16[256,2560]{1,0:T(8,128)(2,1)}, u32[]{:S(2)}, u32[]{:S(2)}) %collective-permute-start.9) | collective-permute-done | bytes 1310752 | tf_op jit(solution)/shard_map/ppermute | solution.py:275
  102.5 4.2 fusion.11
  106.7 2.1 collective-permute-start.16
  111.7 5.1 %collective-permute-start.15 = (bf16[256,2176]{1,0:T(8,128)(2,1)S(1)}, bf16[256,2176]{1,0:T(8,128)(2,1)}, u32[]{:S(2)}, u32[]{:S(2)}) collective-permute-start(bf16[256,2176]{1,0:T(8,128)(2,1)S(1)} %pad_maximum_fusion.3), channel_id=1, source_target_pairs={{0,4},{12,8},{1,5},{13,9},{2,6},{14,10},{3,7},{15,11},{16,20},{28,... | collective-permute-start | bytes 3342344 | tf_op jit(solution)/shard_map/ppermute | solution.py:275
  116.9 14.5 %collective-permute-done.11.refs_7_.refs_17_.refs_15_ = bf16[256,2176]{1,0:T(8,128)(2,1)S(1)} collective-permute-done((bf16[256,2176]{1,0:T(8,128)(2,1)S(1)}, bf16[256,2176]{1,0:T(8,128)(2,1)S(1)}, u32[]{:S(2)}, u32[]{:S(2)}) %collective-permute-start.11) | collective-permute-done | bytes 1114144 | tf_op jit(solution)/shard_map/ppermute | solution.py:275
  132.1 6.5 %collective-permute-done.12.refs_3_ = bf16[256,2560]{1,0:T(8,128)(2,1)S(1)} collective-permute-done((bf16[256,2560]{1,0:T(8,128)(2,1)}, bf16[256,2560]{1,0:T(8,128)(2,1)S(1)}, u32[]{:S(2)}, u32[]{:S(2)}) %collective-permute-start.12) | collective-permute-done | bytes 1310752 | tf_op jit(solution)/shard_map/ppermute | solution.py:275
  140.3 14.8 %collective-permute-done.17.refs_8_.refs_18_.refs_16_ = bf16[256,2176]{1,0:T(8,128)(2,1)S(1)} collective-permute-done((bf16[256,2176]{1,0:T(8,128)(2,1)S(1)}, bf16[256,2176]{1,0:T(8,128)(2,1)S(1)}, u32[]{:S(2)}, u32[]{:S(2)}) %collective-permute-start.17) | collective-permute-done | bytes 1114144 | tf_op jit(solution)/shard_map/ppermute | solution.py:275
  155.2 18.5 %shard_map.38 = (f32[512,2176]{1,0:T(8,128)}, bf16[512,2176]{1,0:T(8,128)(2,1)}) custom-call(s32[3]{0:T(128)S(1)} %pad_add_fusion.sp_ref, bf16[256,2560]{1,0:T(8,128)(2,1)} %collective-permute-done.1.refs_0_, bf16[256,2560]{1,0:T(8,128)(2,1)} %collective-permute-done.3.refs_1_, bf16[256,2560]{1,0:T(8,128)(2,1)} %collective-permute-done.refs_2_, ...), custom_call_target="tpu_custom_call" | custom-call | flops 5133828096 | bytes 10267656 | tf_op jit(solution)/shard_map/pallas_call | solution.py:255
  175.8 13.4 %collective-permute-start.18 = (bf16[256,2560]{1,0:T(8,128)(2,1)}, bf16[256,2560]{1,0:T(8,128)(2,1)}, u32[]{:S(2)}, u32[]{:S(2)}) collective-permute-start(bf16[256,2560]{1,0:T(8,128)(2,1)} %get-tuple-element.160), channel_id=1, source_target_pairs={{0,4},{12,8},{1,5},{13,9},{2,6},{14,10},{3,7},{15,11},{16,20},{28,... | collective-permute-start | bytes 3932168 | tf_op jit(solution)/shard_map/ppermute | solution.py:275
  190.2 15.9 %shard_map.39 = (f32[512,2176]{1,0:T(8,128)}, bf16[512,2176]{1,0:T(8,128)(2,1)}, f32[512,2176]{1,0:T(8,128)}, bf16[512,2176]{1,0:T(8,128)(2,1)}) custom-call(s32[3]{0:T(128)S(1)} %pad_add_fusion.sp_ref, bf16[256,2048]{1,0:T(8,128)(2,1)S(1)} %pad_maximum_fusion.4.refs_0_, bf16[256,2048]{1,0:T(8,128)(2,1)S(1)} %pad_maximum_fusion.5.refs_1_, ...), custom_call_target="tpu_custom_call" | custom-call | flops 4563402752 | bytes 9126805 | tf_op jit(solution)/shard_map/pallas_call | solution.py:255
  206.1 4.7 collective-permute-start.27
  210.9 1.6 collective-permute-start.26
  212.4 1.6 collective-permute-done.18.refs_2_
  214.0 1.7 collective-permute-start.28
  215.8 7.6 %collective-permute-start.20 = (bf16[256,2048]{1,0:T(8,128)(2,1)S(1)}, bf16[256,2048]{1,0:T(8,128)(2,1)S(1)}, u32[]{:S(2)}, u32[]{:S(2)}) collective-permute-start(bf16[256,2048]{1,0:T(8,128)(2,1)S(1)} %pad_maximum_fusion.4.refs_0_), channel_id=1, source_target_pairs={{0,4},{12,8},{1,5},{13,9},{2,6},{14,10},{3,7},{15,11},{16,20},{28,... | collective-permute-start | bytes 3145736 | tf_op jit(solution)/shard_map/ppermute | solution.py:275
  223.4 5.0 %fusion.8 = (bf16[512,2176]{1,0:T(8,128)(2,1)S(1)}, f32[512,2176]{1,0:T(8,128)}) fusion(f32[512,2176]{1,0:T(8,128)} %get-tuple-element.179, bf16[512,2176]{1,0:T(8,128)(2,1)S(1)} %collective-permute-done.21), kind=kLoop, calls=%fused_computation.55 | loop fusion | flops 3342336 | bytes 13369344 | tf_op jit(solution)/shard_map/convert_element_type | solution.py:298
  228.4 15.5 %collective-permute-done.20.refs_6_ = bf16[256,2048]{1,0:T(8,128)(2,1)S(1)} collective-permute-done((bf16[256,2048]{1,0:T(8,128)(2,1)S(1)}, bf16[256,2048]{1,0:T(8,128)(2,1)S(1)}, u32[]{:S(2)}, u32[]{:S(2)}) %collective-permute-start.20) | collective-permute-done | bytes 1048608 | tf_op jit(solution)/shard_map/ppermute | solution.py:275
  246.0 5.5 %collective-permute-start.23 = (bf16[256,2048]{1,0:T(8,128)(2,1)S(1)}, bf16[256,2048]{1,0:T(8,128)(2,1)S(1)}, u32[]{:S(2)}, u32[]{:S(2)}) collective-permute-start(bf16[256,2048]{1,0:T(8,128)(2,1)S(1)} %pad_maximum_fusion.5.refs_1_), channel_id=1, source_target_pairs={{0,4},{12,8},{1,5},{13,9},{2,6},{14,10},{3,7},{15,11},{16,20},{28,... | collective-permute-start | bytes 3145736 | tf_op jit(solution)/shard_map/ppermute | solution.py:275
  251.5 1.4 collective-permute-start.29
  253.0 2.6 fusion.9
  255.6 3.5 fusion.10
  259.1 2.0 collective-permute-start.34
  261.1 1.4 collective-permute-start.33
  262.6 8.4 %collective-permute-done.23.refs_7_ = bf16[256,2048]{1,0:T(8,128)(2,1)S(1)} collective-permute-done((bf16[256,2048]{1,0:T(8,128)(2,1)S(1)}, bf16[256,2048]{1,0:T(8,128)(2,1)S(1)}, u32[]{:S(2)}, u32[]{:S(2)}) %collective-permute-start.23) | collective-permute-done | bytes 1048608 | tf_op jit(solution)/shard_map/ppermute | solution.py:275
  272.2 3.4 collective-permute-done.24.refs_1_
  276.7 18.4 %collective-permute-done.29 = bf16[512,2176]{1,0:T(8,128)(2,1)} collective-permute-done((bf16[512,2176]{1,0:T(8,128)(2,1)S(1)}, bf16[512,2176]{1,0:T(8,128)(2,1)}, u32[]{:S(2)}, u32[]{:S(2)}) %collective-permute-start.29) | collective-permute-done | bytes 2228256 | tf_op jit(solution)/shard_map/ppermute | solution.py:143
  295.2 16.4 %shard_map.40 = (f32[256,2176]{1,0:T(8,128)}, bf16[256,2176]{1,0:T(8,128)(2,1)S(1)}, f32[256,2176]{1,0:T(8,128)}, bf16[256,2176]{1,0:T(8,128)(2,1)S(1)}) custom-call(s32[3]{0:T(128)S(1)} %pad_add_fusion.sp_ref, bf16[256,2560]{1,0:T(8,128)(2,1)} %copy-done.18, bf16[256,2560]{1,0:T(8,128)(2,1)} %copy-done.20, bf16[4608,2048]{1,0:T(8,128)(2,1)} %refs_6_.3, ...), custom_call_target="tpu_custom_call" | custom-call | flops 3707764736 | bytes 7415529 | tf_op jit(solution)/shard_map/pallas_call | solution.py:255
  311.6 18.1 %shard_map.41 = (f32[512,2176]{1,0:T(8,128)}, bf16[512,2176]{1,0:T(8,128)(2,1)}) custom-call(s32[3]{0:T(128)S(1)} %pad_add_fusion.sp_ref, bf16[256,2560]{1,0:T(8,128)(2,1)S(1)} %collective-permute-done.13.refs_0_, bf16[256,2560]{1,0:T(8,128)(2,1)} %collective-permute-done.9.refs_1_, bf16[256,2560]{1,0:T(8,128)(2,1)} %collective-permute-done.18.refs_2_, ...), custom_call_target="tpu_custom_call" | custom-call | flops 5133828096 | bytes 10267656 | tf_op jit(solution)/shard_map/pallas_call | solution.py:255
  330.7 16.3 %shard_map.42 = (f32[256,2176]{1,0:T(8,128)}, bf16[256,2176]{1,0:T(8,128)(2,1)S(1)}, f32[256,2176]{1,0:T(8,128)}, bf16[256,2176]{1,0:T(8,128)(2,1)S(1)}) custom-call(s32[3]{0:T(128)S(1)} %pad_add_fusion.sp_ref, bf16[256,2560]{1,0:T(8,128)(2,1)} %collective-permute-done.28.refs_0_, bf16[256,2560]{1,0:T(8,128)(2,1)} %copy-done.21, bf16[4608,2048]{1,0:T(8,128)(2,1)} %refs_6_.3, ...), custom_call_target="tpu_custom_call" | custom-call | flops 3707764736 | bytes 7415529 | tf_op jit(solution)/shard_map/pallas_call | solution.py:255
  347.0 4.8 add_convert_fusion.4
  351.8 4.9 add_convert_fusion.3
  358.0 3.2 collective-permute-start.30
  366.2 2.4 collective-permute-start.44
  369.8 1.9 collective-permute-start.46
  372.0 2.0 fusion.5
  374.0 3.2 fusion.7
  378.6 18.4 %collective-permute-done.46 = bf16[256,2176]{1,0:T(8,128)(2,1)S(1)} collective-permute-done((bf16[256,2176]{1,0:T(8,128)(2,1)}, bf16[256,2176]{1,0:T(8,128)(2,1)S(1)}, u32[]{:S(2)}, u32[]{:S(2)}) %collective-permute-start.46) | collective-permute-done | bytes 1114144 | tf_op jit(solution)/shard_map/ppermute | solution.py:143
  397.5 1.7 collective-permute-start.47
  400.4 2.1 collective-permute-start.38
  402.5 18.3 %collective-permute-done.41 = bf16[256,2176]{1,0:T(8,128)(2,1)S(1)} collective-permute-done((bf16[256,2176]{1,0:T(8,128)(2,1)S(1)}, bf16[256,2176]{1,0:T(8,128)(2,1)S(1)}, u32[]{:S(2)}, u32[]{:S(2)}) %collective-permute-start.41) | collective-permute-done | bytes 1114144 | tf_op jit(solution)/shard_map/ppermute | solution.py:143
  420.8 2.0 collective-permute-start.37
  424.0 5.2 %collective-permute-start.40 = (bf16[256,2176]{1,0:T(8,128)(2,1)}, bf16[256,2176]{1,0:T(8,128)(2,1)}, u32[]{:S(2)}, u32[]{:S(2)}) collective-permute-start(bf16[256,2176]{1,0:T(8,128)(2,1)} %get-tuple-element.250), channel_id=1, source_target_pairs={{1,3},{5,7},{10,8},{14,12},{17,19},{21,23},{26,24},{30,28}} | collective-permute-start | bytes 3342344 | tf_op jit(solution)/shard_map/ppermute | solution.py:143
  429.2 1.7 collective-permute-start.42
  430.9 2.5 add_convert_fusion.5
  433.4 7.5 %collective-permute-done.40 = bf16[256,2176]{1,0:T(8,128)(2,1)} collective-permute-done((bf16[256,2176]{1,0:T(8,128)(2,1)}, bf16[256,2176]{1,0:T(8,128)(2,1)}, u32[]{:S(2)}, u32[]{:S(2)}) %collective-permute-start.40) | collective-permute-done | bytes 1114144 | tf_op jit(solution)/shard_map/ppermute | solution.py:143
  440.9 2.0 add_convert_fusion.7
  443.0 8.9 %fusion = bf16[512,2176]{1,0:T(8,128)(2,1)S(1)} fusion(bf16[512,2176]{1,0:T(8,128)(2,1)} %collective-permute-done.38, f32[512,2176]{1,0:T(8,128)} %get-tuple-element.262, bf16[512,2176]{1,0:T(8,128)(2,1)} %collective-permute-done.37, bf16[512,2176]{1,0:T(8,128)(2,1)} %collective-permute-done.39, f32[512,2176]{1,0:T(8,128)} %get-tuple-element.264, ...), kind=kLoop, calls=%fused_computation.10 | loop fusion | flops 22282240 | bytes 28966916 | tf_op jit(solution)/shard_map/jit(_where)/select_n | solution.py:448
  452.1 3.5 collective-permute-start.50
  455.5 2.3 collective-permute-done.48
  457.8 1.8 collective-permute-done.49
  460.5 17.3 %collective-permute-start.51 = (bf16[512,512]{1,0:T(8,128)(2,1)}, bf16[512,512]{1,0:T(8,128)(2,1)S(1)}, u32[]{:S(2)}, u32[]{:S(2)}) collective-permute-start(bf16[512,512]{1,0:T(8,128)(2,1)} %pad_maximum_fusion.7), channel_id=1, source_target_pairs={{0,1},{1,0},{2,3},{3,2},{4,5},{5,4},{6,7},{7,6},{8,9},{9,8},{10,11... | collective-permute-start | bytes 1572872 | tf_op jit(solution)/shard_map/ppermute | solution.py:450
  478.1 1.5 collective-permute-done.51
  479.9 11.6 %shard_map.43 = bf16[512,2048]{1,0:T(8,128)(2,1)} custom-call(s32[1]{0:T(128)} %bitcast.where_ref, bf16[512,2048]{1,0:T(8,128)(2,1)S(1)} %slice.32.q_ref, bf16[1024,512]{1,0:T(8,128)(2,1)S(1)} %pad_maximum_fusion.6.kv_ref), custom_call_target="tpu_custom_call" | custom-call | flops 6000000000 | bytes 5000000 | tf_op jit(solution)/shard_map/pallas_call | solution.py:83
  (147 shorter events, 37.1 us)
Async XLA Ops:
  3.4 41.7 %collective-permute-start.1 = (bf16[256,2560]{1,0:T(8,128)(2,1)}, bf16[256,2560]{1,0:T(8,128)(2,1)}, u32[]{:S(2)}, u32[]{:S(2)}) collective-permute-start(bf16[256,2560]{1,0:T(8,128)(2,1)} %get-tuple-element.148), channel_id=1, source_target_pairs={{4,8},{8,4},{5,9},{9,5},{6,10},{10,6},{7,11},{11,7},{20,24},{24,20... | collective-permute-start | bytes 3932168 | tf_op jit(solution)/shard_map/ppermute | solution.py:275
  5.1 61.5 %collective-permute-start.3 = (bf16[256,2560]{1,0:T(8,128)(2,1)}, bf16[256,2560]{1,0:T(8,128)(2,1)}, u32[]{:S(2)}, u32[]{:S(2)}) collective-permute-start(bf16[256,2560]{1,0:T(8,128)(2,1)} %get-tuple-element.148), channel_id=1, source_target_pairs={{4,0},{8,12},{5,1},{9,13},{6,2},{10,14},{7,3},{11,15},{20,16},{24,... | collective-permute-start | bytes 3932168 | tf_op jit(solution)/shard_map/ppermute | solution.py:275
  11.8 31.6 %collective-permute-start.2 = (bf16[256,2176]{1,0:T(8,128)(2,1)}, bf16[256,2176]{1,0:T(8,128)(2,1)S(1)}, u32[]{:S(2)}, u32[]{:S(2)}) collective-permute-start(bf16[256,2176]{1,0:T(8,128)(2,1)} %pad_maximum_fusion.1), channel_id=1, source_target_pairs={{0,4},{12,8},{1,5},{13,9},{2,6},{14,10},{3,7},{15,11},{16,20},{28,... | collective-permute-start | bytes 3342344 | tf_op jit(solution)/shard_map/ppermute | solution.py:275
  37.5 27.9 %collective-permute-start.7 = (bf16[256,2176]{1,0:T(8,128)(2,1)S(1)}, bf16[256,2176]{1,0:T(8,128)(2,1)S(1)}, u32[]{:S(2)}, u32[]{:S(2)}) collective-permute-start(bf16[256,2176]{1,0:T(8,128)(2,1)S(1)} %get-tuple-element.138), channel_id=1, source_target_pairs={{0,4},{12,8},{1,5},{13,9},{2,6},{14,10},{3,7},{15,11},{16,20},{28,... | collective-permute-start | bytes 3342344 | tf_op jit(solution)/shard_map/ppermute | solution.py:275
  38.8 52.2 %collective-permute-start.5 = (bf16[512,2176]{1,0:T(8,128)(2,1)}, bf16[512,2176]{1,0:T(8,128)(2,1)}, u32[]{:S(2)}, u32[]{:S(2)}) collective-permute-start(bf16[512,2176]{1,0:T(8,128)(2,1)} %get-tuple-element.137), channel_id=1, source_target_pairs={{1,0},{3,2},{4,5},{6,7},{9,8},{11,10},{12,13},{14,15},{17,16},{19,... | collective-permute-start | bytes 6684680 | tf_op jit(solution)/shard_map/ppermute | solution.py:138
  43.4 26.5 %collective-permute-start = (bf16[256,2560]{1,0:T(8,128)(2,1)}, bf16[256,2560]{1,0:T(8,128)(2,1)}, u32[]{:S(2)}, u32[]{:S(2)}) collective-permute-start(bf16[256,2560]{1,0:T(8,128)(2,1)} %get-tuple-element.160), channel_id=1, source_target_pairs={{4,8},{8,4},{5,9},{9,5},{6,10},{10,6},{7,11},{11,7},{20,24},{24,20... | collective-permute-start | bytes 3932168 | tf_op jit(solution)/shard_map/ppermute | solution.py:275
  45.1 30.3 %collective-permute-start.6 = (bf16[256,2560]{1,0:T(8,128)(2,1)}, bf16[256,2560]{1,0:T(8,128)(2,1)}, u32[]{:S(2)}, u32[]{:S(2)}) collective-permute-start(bf16[256,2560]{1,0:T(8,128)(2,1)} %get-tuple-element.160), channel_id=1, source_target_pairs={{4,0},{8,12},{5,1},{9,13},{6,2},{10,14},{7,3},{11,15},{20,16},{24,... | collective-permute-start | bytes 3932168 | tf_op jit(solution)/shard_map/ppermute | solution.py:275
  65.3 43.4 %copy-start.2 = (bf16[256,2176]{1,0:T(8,128)(2,1)}, bf16[256,2176]{1,0:T(8,128)(2,1)S(1)}, u32[]{:S(2)}) copy-start(bf16[256,2176]{1,0:T(8,128)(2,1)S(1)} %collective-permute-done.7.refs_3_.refs_13_.refs_11_) | copy-start | bytes 3342340
  65.3 37.1 %collective-permute-start.9 = (bf16[256,2560]{1,0:T(8,128)(2,1)}, bf16[256,2560]{1,0:T(8,128)(2,1)}, u32[]{:S(2)}, u32[]{:S(2)}) collective-permute-start(bf16[256,2560]{1,0:T(8,128)(2,1)} %collective-permute-done.1.refs_0_), channel_id=1, source_target_pairs={{4,0},{8,12},{5,1},{9,13},{6,2},{10,14},{7,3},{11,15},{20,16},{24,... | collective-permute-start | bytes 3932168 | tf_op jit(solution)/shard_map/ppermute | solution.py:275
  66.6 24.4 %collective-permute-start.8 = (bf16[256,2176]{1,0:T(8,128)(2,1)S(1)}, bf16[256,2176]{1,0:T(8,128)(2,1)}, u32[]{:S(2)}, u32[]{:S(2)}) collective-permute-start(bf16[256,2176]{1,0:T(8,128)(2,1)S(1)} %collective-permute-done.2.refs_2_.refs_12_.refs_10_), channel_id=1, source_target_pairs={{0,16},{16,0},{1,17},{17,1},{2,18},{18,2},{3,19},{19,3},{4,20},{20... | collective-permute-start | bytes 3342344 | tf_op jit(solution)/shard_map/ppermute | solution.py:275
  68.0 34.5 %copy-start.12 = (f32[512,2176]{1,0:T(8,128)S(1)}, f32[512,2176]{1,0:T(8,128)}, u32[]{:S(2)}) copy-start(f32[512,2176]{1,0:T(8,128)} %get-tuple-element.141) | copy-start | bytes 13369348
  69.9 41.4 %copy-start.14 = (bf16[256,2048]{1,0:T(8,128)(2,1)S(1)}, bf16[256,2048]{1,0:T(8,128)(2,1)}, u32[]{:S(2)}) copy-start(bf16[256,2048]{1,0:T(8,128)(2,1)} %get-tuple-element.271) | copy-start | bytes 3145732
  69.9 41.5 %collective-permute-start.4 = (bf16[256,2176]{1,0:T(8,128)(2,1)S(1)}, bf16[256,2176]{1,0:T(8,128)(2,1)S(1)}, u32[]{:S(2)}, u32[]{:S(2)}) collective-permute-start(bf16[256,2176]{1,0:T(8,128)(2,1)S(1)} %copy-done.22), channel_id=1, source_target_pairs={{0,4},{12,8},{1,5},{13,9},{2,6},{14,10},{3,7},{15,11},{16,20},{28,... | collective-permute-start | bytes 3342344 | tf_op jit(solution)/shard_map/ppermute | solution.py:275
  75.5 36.3 %collective-permute-start.10 = (bf16[256,2048]{1,0:T(8,128)(2,1)S(1)}, bf16[256,2048]{1,0:T(8,128)(2,1)S(1)}, u32[]{:S(2)}, u32[]{:S(2)}) collective-permute-start(bf16[256,2048]{1,0:T(8,128)(2,1)S(1)} %pad_maximum_fusion.4.refs_0_), channel_id=1, source_target_pairs={{4,8},{8,4},{5,9},{9,5},{6,10},{10,6},{7,11},{11,7},{20,24},{24,20... | collective-permute-start | bytes 3145736 | tf_op jit(solution)/shard_map/ppermute | solution.py:275
  106.7 48.5 %collective-permute-start.16 = (bf16[512,2176]{1,0:T(8,128)(2,1)S(1)}, bf16[512,2176]{1,0:T(8,128)(2,1)}, u32[]{:S(2)}, u32[]{:S(2)}) collective-permute-start(bf16[512,2176]{1,0:T(8,128)(2,1)S(1)} %get-tuple-element.151), channel_id=1, source_target_pairs={{2,0},{7,5},{8,10},{13,15},{18,16},{23,21},{24,26},{29,31}} | collective-permute-start | bytes 6684680 | tf_op jit(solution)/shard_map/ppermute | solution.py:143
  108.8 22.6 %collective-permute-start.11 = (bf16[256,2176]{1,0:T(8,128)(2,1)S(1)}, bf16[256,2176]{1,0:T(8,128)(2,1)S(1)}, u32[]{:S(2)}, u32[]{:S(2)}) collective-permute-start(bf16[256,2176]{1,0:T(8,128)(2,1)S(1)} %collective-permute-done.7.refs_3_.refs_13_.refs_11_), channel_id=1, source_target_pairs={{0,16},{16,0},{1,17},{17,1},{2,18},{18,2},{3,19},{19,3},{4,20},{20... | collective-permute-start | bytes 3342344 | tf_op jit(solution)/shard_map/ppermute | solution.py:275
  110.0 28.7 %collective-permute-start.12 = (bf16[256,2560]{1,0:T(8,128)(2,1)}, bf16[256,2560]{1,0:T(8,128)(2,1)S(1)}, u32[]{:S(2)}, u32[]{:S(2)}) collective-permute-start(bf16[256,2560]{1,0:T(8,128)(2,1)} %collective-permute-done.refs_2_), channel_id=1, source_target_pairs={{4,0},{8,12},{5,1},{9,13},{6,2},{10,14},{7,3},{11,15},{20,16},{24,... | collective-permute-start | bytes 3932168 | tf_op jit(solution)/shard_map/ppermute | solution.py:275
  111.4 62.3 %copy-start.4 = (bf16[256,2176]{1,0:T(8,128)(2,1)}, bf16[256,2176]{1,0:T(8,128)(2,1)S(1)}, u32[]{:S(2)}) copy-start(bf16[256,2176]{1,0:T(8,128)(2,1)S(1)} %collective-permute-done.4.refs_4_.refs_14_.refs_12_) | copy-start | bytes 3342340
  111.4 43.7 %collective-permute-start.17 = (bf16[256,2176]{1,0:T(8,128)(2,1)S(1)}, bf16[256,2176]{1,0:T(8,128)(2,1)S(1)}, u32[]{:S(2)}, u32[]{:S(2)}) collective-permute-start(bf16[256,2176]{1,0:T(8,128)(2,1)S(1)} %collective-permute-done.4.refs_4_.refs_14_.refs_12_), channel_id=1, source_target_pairs={{0,16},{16,0},{1,17},{17,1},{2,18},{18,2},{3,19},{19,3},{4,20},{20... | collective-permute-start | bytes 3342344 | tf_op jit(solution)/shard_map/ppermute | solution.py:275
  111.7 28.3 %collective-permute-start.15 = (bf16[256,2176]{1,0:T(8,128)(2,1)S(1)}, bf16[256,2176]{1,0:T(8,128)(2,1)}, u32[]{:S(2)}, u32[]{:S(2)}) collective-permute-start(bf16[256,2176]{1,0:T(8,128)(2,1)S(1)} %pad_maximum_fusion.3), channel_id=1, source_target_pairs={{0,4},{12,8},{1,5},{13,9},{2,6},{14,10},{3,7},{15,11},{16,20},{28,... | collective-permute-start | bytes 3342344 | tf_op jit(solution)/shard_map/ppermute | solution.py:275
  131.4 42.3 %copy-start.5 = (bf16[256,2176]{1,0:T(8,128)(2,1)}, bf16[256,2176]{1,0:T(8,128)(2,1)S(1)}, u32[]{:S(2)}) copy-start(bf16[256,2176]{1,0:T(8,128)(2,1)S(1)} %collective-permute-done.11.refs_7_.refs_17_.refs_15_) | copy-start | bytes 3342340
  131.4 8.9 %collective-permute-start.14 = (bf16[256,2048]{1,0:T(8,128)(2,1)S(1)}, bf16[256,2048]{1,0:T(8,128)(2,1)S(1)}, u32[]{:S(2)}, u32[]{:S(2)}) collective-permute-start(bf16[256,2048]{1,0:T(8,128)(2,1)S(1)} %pad_maximum_fusion.5.refs_1_), channel_id=1, source_target_pairs={{4,8},{8,4},{5,9},{9,5},{6,10},{10,6},{7,11},{11,7},{20,24},{24,20... | collective-permute-start | bytes 3145736 | tf_op jit(solution)/shard_map/ppermute | solution.py:275
  138.7 36.3 %collective-permute-start.13 = (bf16[256,2560]{1,0:T(8,128)(2,1)}, bf16[256,2560]{1,0:T(8,128)(2,1)S(1)}, u32[]{:S(2)}, u32[]{:S(2)}) collective-permute-start(bf16[256,2560]{1,0:T(8,128)(2,1)} %get-tuple-element.148), channel_id=1, source_target_pairs={{0,4},{12,8},{1,5},{13,9},{2,6},{14,10},{3,7},{15,11},{16,20},{28,... | collective-permute-start | bytes 3932168 | tf_op jit(solution)/shard_map/ppermute | solution.py:275
  140.1 49.1 %collective-permute-start.19 = (bf16[256,2176]{1,0:T(8,128)(2,1)}, bf16[256,2176]{1,0:T(8,128)(2,1)S(1)}, u32[]{:S(2)}, u32[]{:S(2)}) collective-permute-start(bf16[256,2176]{1,0:T(8,128)(2,1)} %collective-permute-done.15.refs_5_.refs_15_.refs_13_), channel_id=1, source_target_pairs={{0,16},{16,0},{1,17},{17,1},{2,18},{18,2},{3,19},{19,3},{4,20},{20... | collective-permute-start | bytes 3342344 | tf_op jit(solution)/shard_map/ppermute | solution.py:275
  155.2 18.5 %copy-start.6 = (bf16[256,2176]{1,0:T(8,128)(2,1)}, bf16[256,2176]{1,0:T(8,128)(2,1)S(1)}, u32[]{:S(2)}) copy-start(bf16[256,2176]{1,0:T(8,128)(2,1)S(1)} %collective-permute-done.17.refs_8_.refs_18_.refs_16_) | copy-start | bytes 3342340
  173.7 49.7 %collective-permute-start.21 = (bf16[512,2176]{1,0:T(8,128)(2,1)}, bf16[512,2176]{1,0:T(8,128)(2,1)S(1)}, u32[]{:S(2)}, u32[]{:S(2)}) collective-permute-start(bf16[512,2176]{1,0:T(8,128)(2,1)} %get-tuple-element.177), channel_id=1, source_target_pairs={{0,1},{2,3},{5,4},{7,6},{8,9},{10,11},{13,12},{15,14},{16,17},{18,... | collective-permute-start | bytes 6684680 | tf_op jit(solution)/shard_map/ppermute | solution.py:138
  175.0 40.8 %collective-permute-start.22 = (bf16[256,2560]{1,0:T(8,128)(2,1)S(1)}, bf16[256,2560]{1,0:T(8,128)(2,1)S(1)}, u32[]{:S(2)}, u32[]{:S(2)}) collective-permute-start(bf16[256,2560]{1,0:T(8,128)(2,1)S(1)} %collective-permute-done.13.refs_0_), channel_id=1, source_target_pairs={{4,8},{8,4},{5,9},{9,5},{6,10},{10,6},{7,11},{11,7},{20,24},{24,20... | collective-permute-start | bytes 3932168 | tf_op jit(solution)/shard_map/ppermute | solution.py:275
  175.8 38.3 %collective-permute-start.18 = (bf16[256,2560]{1,0:T(8,128)(2,1)}, bf16[256,2560]{1,0:T(8,128)(2,1)}, u32[]{:S(2)}, u32[]{:S(2)}) collective-permute-start(bf16[256,2560]{1,0:T(8,128)(2,1)} %get-tuple-element.160), channel_id=1, source_target_pairs={{0,4},{12,8},{1,5},{13,9},{2,6},{14,10},{3,7},{15,11},{16,20},{28,... | collective-permute-start | bytes 3932168 | tf_op jit(solution)/shard_map/ppermute | solution.py:275
  206.1 39.8 %collective-permute-start.27 = (bf16[512,2176]{1,0:T(8,128)(2,1)}, bf16[512,2176]{1,0:T(8,128)(2,1)S(1)}, u32[]{:S(2)}, u32[]{:S(2)}) collective-permute-start(bf16[512,2176]{1,0:T(8,128)(2,1)} %get-tuple-element.188), channel_id=1, source_target_pairs={{1,0},{3,2},{4,5},{6,7},{9,8},{11,10},{12,13},{14,15},{17,16},{19,... | collective-permute-start | bytes 6684680 | tf_op jit(solution)/shard_map/ppermute | solution.py:138
  210.8 42.1 %slice-start.6 = ((s8[4456448]{0:T(1024)(128)(4,1)}), s8[4194304]{0:T(1024)(128)(4,1)S(1)}, s32[]{:S(2)}) async-start(s8[4456448]{0:T(1024)(128)(4,1)} %bitcast.10), calls=%async_computation.6 | async-start | bytes 8388608
  210.9 42.1 %slice-start.7 = ((s8[4456448]{0:T(1024)(128)(4,1)}), s8[262144]{0:T(1024)(128)(4,1)S(1)}, s32[]{:S(2)}) async-start(s8[4456448]{0:T(1024)(128)(4,1)} %bitcast.10), calls=%async_computation.7 | async-start | bytes 524288
  210.9 40.6 %collective-permute-start.26 = (bf16[512,2176]{1,0:T(8,128)(2,1)}, bf16[512,2176]{1,0:T(8,128)(2,1)S(1)}, u32[]{:S(2)}, u32[]{:S(2)}) collective-permute-start(bf16[512,2176]{1,0:T(8,128)(2,1)} %get-tuple-element.186), channel_id=1, source_target_pairs={{0,1},{2,3},{5,4},{7,6},{8,9},{10,11},{13,12},{15,14},{16,17},{18,... | collective-permute-start | bytes 6684680 | tf_op jit(solution)/shard_map/ppermute | solution.py:138
  214.0 38.9 %collective-permute-start.28 = (bf16[256,2560]{1,0:T(8,128)(2,1)}, bf16[256,2560]{1,0:T(8,128)(2,1)}, u32[]{:S(2)}, u32[]{:S(2)}) collective-permute-start(bf16[256,2560]{1,0:T(8,128)(2,1)} %collective-permute-done.18.refs_2_), channel_id=1, source_target_pairs={{4,8},{8,4},{5,9},{9,5},{6,10},{10,6},{7,11},{11,7},{20,24},{24,20... | collective-permute-start | bytes 3932168 | tf_op jit(solution)/shard_map/ppermute | solution.py:275
  215.8 28.1 %collective-permute-start.20 = (bf16[256,2048]{1,0:T(8,128)(2,1)S(1)}, bf16[256,2048]{1,0:T(8,128)(2,1)S(1)}, u32[]{:S(2)}, u32[]{:S(2)}) collective-permute-start(bf16[256,2048]{1,0:T(8,128)(2,1)S(1)} %pad_maximum_fusion.4.refs_0_), channel_id=1, source_target_pairs={{0,4},{12,8},{1,5},{13,9},{2,6},{14,10},{3,7},{15,11},{16,20},{28,... | collective-permute-start | bytes 3145736 | tf_op jit(solution)/shard_map/ppermute | solution.py:275
  223.4 21.2 %copy-start.19 = (bf16[256,2560]{1,0:T(8,128)(2,1)S(1)}, bf16[256,2560]{1,0:T(8,128)(2,1)}, u32[]{:S(2)}) copy-start(bf16[256,2560]{1,0:T(8,128)(2,1)} %copy-done.18) | copy-start | bytes 3932164
  223.4 32.2 %slice-start.4 = ((s8[4456448]{0:T(1024)(128)(4,1)}), s8[4194304]{0:T(1024)(128)(4,1)S(1)}, s32[]{:S(2)}) async-start(s8[4456448]{0:T(1024)(128)(4,1)} %bitcast.8), calls=%async_computation.4 | async-start | bytes 8388608
  243.9 17.2 %collective-permute-start.25 = (bf16[256,2048]{1,0:T(8,128)(2,1)S(1)}, bf16[256,2048]{1,0:T(8,128)(2,1)S(1)}, u32[]{:S(2)}, u32[]{:S(2)}) collective-permute-start(bf16[256,2048]{1,0:T(8,128)(2,1)S(1)} %collective-permute-done.20.refs_6_), channel_id=1, source_target_pairs={{4,8},{8,4},{5,9},{9,5},{6,10},{10,6},{7,11},{11,7},{20,24},{24,20... | collective-permute-start | bytes 3145736 | tf_op jit(solution)/shard_map/ppermute | solution.py:275
  244.6 31.0 %collective-permute-start.24 = (bf16[256,2560]{1,0:T(8,128)(2,1)S(1)}, bf16[256,2560]{1,0:T(8,128)(2,1)S(1)}, u32[]{:S(2)}, u32[]{:S(2)}) collective-permute-start(bf16[256,2560]{1,0:T(8,128)(2,1)S(1)} %copy-done.19), channel_id=1, source_target_pairs={{4,0},{8,12},{5,1},{9,13},{6,2},{10,14},{7,3},{11,15},{20,16},{24,... | collective-permute-start | bytes 3932168 | tf_op jit(solution)/shard_map/ppermute | solution.py:275
  246.0 25.0 %collective-permute-start.23 = (bf16[256,2048]{1,0:T(8,128)(2,1)S(1)}, bf16[256,2048]{1,0:T(8,128)(2,1)S(1)}, u32[]{:S(2)}, u32[]{:S(2)}) collective-permute-start(bf16[256,2048]{1,0:T(8,128)(2,1)S(1)} %pad_maximum_fusion.5.refs_1_), channel_id=1, source_target_pairs={{0,4},{12,8},{1,5},{13,9},{2,6},{14,10},{3,7},{15,11},{16,20},{28,... | collective-permute-start | bytes 3145736 | tf_op jit(solution)/shard_map/ppermute | solution.py:275
  251.5 43.6 %collective-permute-start.29 = (bf16[512,2176]{1,0:T(8,128)(2,1)S(1)}, bf16[512,2176]{1,0:T(8,128)(2,1)}, u32[]{:S(2)}, u32[]{:S(2)}) collective-permute-start(bf16[512,2176]{1,0:T(8,128)(2,1)S(1)} %get-tuple-element.194), channel_id=1, source_target_pairs={{3,1},{4,6},{11,9},{12,14},{19,17},{20,22},{27,25},{28,30}} | collective-permute-start | bytes 6684680 | tf_op jit(solution)/shard_map/ppermute | solution.py:143
  255.6 39.6 %copy-start.3 = (bf16[256,2176]{1,0:T(8,128)(2,1)S(1)}, bf16[256,2176]{1,0:T(8,128)(2,1)}, u32[]{:S(2)}) copy-start(bf16[256,2176]{1,0:T(8,128)(2,1)} %copy-done.2) | copy-start | bytes 3342340
  259.1 70.5 %collective-permute-start.34 = (bf16[512,2176]{1,0:T(8,128)(2,1)S(1)}, bf16[512,2176]{1,0:T(8,128)(2,1)}, u32[]{:S(2)}, u32[]{:S(2)}) collective-permute-start(bf16[512,2176]{1,0:T(8,128)(2,1)S(1)} %get-tuple-element.222), channel_id=1, source_target_pairs={{2,0},{7,5},{8,10},{13,15},{18,16},{23,21},{24,26},{29,31}} | collective-permute-start | bytes 6684680 | tf_op jit(solution)/shard_map/ppermute | solution.py:143
  261.1 50.4 %copy-start.1 = (bf16[4608,128]{1,0:T(8,128)(2,1)S(1)}, bf16[4608,128]{1,0:T(8,128)(2,1)}, u32[]{:S(2)}) copy-start(bf16[4608,128]{1,0:T(8,128)(2,1)} %refs_8_.7) | copy-start | bytes 3538948
  261.1 68.5 %collective-permute-start.33 = (bf16[512,2176]{1,0:T(8,128)(2,1)}, bf16[512,2176]{1,0:T(8,128)(2,1)}, u32[]{:S(2)}, u32[]{:S(2)}) collective-permute-start(bf16[512,2176]{1,0:T(8,128)(2,1)} %get-tuple-element.221), channel_id=1, source_target_pairs={{3,1},{4,6},{11,9},{12,14},{19,17},{20,22},{27,25},{28,30}} | collective-permute-start | bytes 6684680 | tf_op jit(solution)/shard_map/ppermute | solution.py:143
  270.9 58.7 %collective-permute-start.35 = (bf16[256,2560]{1,0:T(8,128)(2,1)}, bf16[256,2560]{1,0:T(8,128)(2,1)S(1)}, u32[]{:S(2)}, u32[]{:S(2)}) collective-permute-start(bf16[256,2560]{1,0:T(8,128)(2,1)} %collective-permute-done.28.refs_0_), channel_id=1, source_target_pairs={{4,0},{8,12},{5,1},{9,13},{6,2},{10,14},{7,3},{11,15},{20,16},{24,... | collective-permute-start | bytes 3932168 | tf_op jit(solution)/shard_map/ppermute | solution.py:275
  275.7 54.0 %collective-permute-start.36 = (bf16[256,2048]{1,0:T(8,128)(2,1)S(1)}, bf16[256,2048]{1,0:T(8,128)(2,1)S(1)}, u32[]{:S(2)}, u32[]{:S(2)}) collective-permute-start(bf16[256,2048]{1,0:T(8,128)(2,1)S(1)} %collective-permute-done.23.refs_7_), channel_id=1, source_target_pairs={{4,8},{8,4},{5,9},{9,5},{6,10},{10,6},{7,11},{11,7},{20,24},{24,20... | collective-permute-start | bytes 3145736 | tf_op jit(solution)/shard_map/ppermute | solution.py:275
  356.7 8.4 %collective-permute-start.43 = (bf16[256,2176]{1,0:T(8,128)(2,1)S(1)}, bf16[256,2176]{1,0:T(8,128)(2,1)S(1)}, u32[]{:S(2)}, u32[]{:S(2)}) collective-permute-start(bf16[256,2176]{1,0:T(8,128)(2,1)S(1)} %get-tuple-element.254), channel_id=1, source_target_pairs={{0,1},{2,3},{4,5},{6,7},{9,8},{11,10},{13,12},{15,14},{16,17},{18,... | collective-permute-start | bytes 3342344 | tf_op jit(solution)/shard_map/ppermute | solution.py:138
  358.0 13.7 %collective-permute-start.30 = (bf16[512,2176]{1,0:T(8,128)(2,1)S(1)}, bf16[512,2176]{1,0:T(8,128)(2,1)S(1)}, u32[]{:S(2)}, u32[]{:S(2)}) collective-permute-start(bf16[512,2176]{1,0:T(8,128)(2,1)S(1)} %copy-done.23), channel_id=1, source_target_pairs={{1,0},{3,2},{5,4},{7,6},{8,9},{10,11},{12,13},{14,15},{17,16},{19,... | collective-permute-start | bytes 6684680 | tf_op jit(solution)/shard_map/ppermute | solution.py:138
  361.3 7.3 %collective-permute-start.45 = (bf16[256,2176]{1,0:T(8,128)(2,1)S(1)}, bf16[256,2176]{1,0:T(8,128)(2,1)S(1)}, u32[]{:S(2)}, u32[]{:S(2)}) collective-permute-start(bf16[256,2176]{1,0:T(8,128)(2,1)S(1)} %get-tuple-element.256), channel_id=1, source_target_pairs={{0,1},{2,3},{4,5},{6,7},{9,8},{11,10},{13,12},{15,14},{16,17},{18,... | collective-permute-start | bytes 3342344 | tf_op jit(solution)/shard_map/ppermute | solution.py:138
  362.6 9.1 %collective-permute-start.32 = (bf16[256,2176]{1,0:T(8,128)(2,1)S(1)}, bf16[256,2176]{1,0:T(8,128)(2,1)S(1)}, u32[]{:S(2)}, u32[]{:S(2)}) collective-permute-start(bf16[256,2176]{1,0:T(8,128)(2,1)S(1)} %get-tuple-element.220), channel_id=1, source_target_pairs={{0,1},{2,3},{4,5},{6,7},{9,8},{11,10},{13,12},{15,14},{16,17},{18,... | collective-permute-start | bytes 3342344 | tf_op jit(solution)/shard_map/ppermute | solution.py:138
  363.9 7.8 %collective-permute-start.31 = (bf16[256,2176]{1,0:T(8,128)(2,1)S(1)}, bf16[256,2176]{1,0:T(8,128)(2,1)S(1)}, u32[]{:S(2)}, u32[]{:S(2)}) collective-permute-start(bf16[256,2176]{1,0:T(8,128)(2,1)S(1)} %get-tuple-element.218), channel_id=1, source_target_pairs={{0,1},{2,3},{4,5},{6,7},{9,8},{11,10},{13,12},{15,14},{16,17},{18,... | collective-permute-start | bytes 3342344 | tf_op jit(solution)/shard_map/ppermute | solution.py:138
  366.2 57.8 %collective-permute-start.44 = (bf16[256,2176]{1,0:T(8,128)(2,1)S(1)}, bf16[256,2176]{1,0:T(8,128)(2,1)}, u32[]{:S(2)}, u32[]{:S(2)}) collective-permute-start(bf16[256,2176]{1,0:T(8,128)(2,1)S(1)} %fusion.3), channel_id=1, source_target_pairs={{1,3},{5,7},{10,8},{14,12},{17,19},{21,23},{26,24},{30,28}} | collective-permute-start | bytes 3342344 | tf_op jit(solution)/shard_map/ppermute | solution.py:143
  369.8 27.3 %collective-permute-start.46 = (bf16[256,2176]{1,0:T(8,128)(2,1)}, bf16[256,2176]{1,0:T(8,128)(2,1)S(1)}, u32[]{:S(2)}, u32[]{:S(2)}) collective-permute-start(bf16[256,2176]{1,0:T(8,128)(2,1)} %fusion.4), channel_id=1, source_target_pairs={{1,3},{5,7},{10,8},{14,12},{17,19},{21,23},{26,24},{30,28}} | collective-permute-start | bytes 3342344 | tf_op jit(solution)/shard_map/ppermute | solution.py:143
  377.2 43.6 %collective-permute-start.41 = (bf16[256,2176]{1,0:T(8,128)(2,1)S(1)}, bf16[256,2176]{1,0:T(8,128)(2,1)S(1)}, u32[]{:S(2)}, u32[]{:S(2)}) collective-permute-start(bf16[256,2176]{1,0:T(8,128)(2,1)S(1)} %get-tuple-element.251), channel_id=1, source_target_pairs={{1,3},{5,7},{10,8},{14,12},{17,19},{21,23},{26,24},{30,28}} | collective-permute-start | bytes 3342344 | tf_op jit(solution)/shard_map/ppermute | solution.py:143
  397.5 31.7 %collective-permute-start.47 = (bf16[256,2176]{1,0:T(8,128)(2,1)S(1)}, bf16[256,2176]{1,0:T(8,128)(2,1)}, u32[]{:S(2)}, u32[]{:S(2)}) collective-permute-start(bf16[256,2176]{1,0:T(8,128)(2,1)S(1)} %add_convert_fusion.6), channel_id=1, source_target_pairs={{7,3},{8,12},{23,19},{24,28}} | collective-permute-start | bytes 3342344 | tf_op jit(solution)/shard_map/ppermute | solution.py:148
  399.1 43.8 %collective-permute-start.39 = (bf16[512,2176]{1,0:T(8,128)(2,1)}, bf16[512,2176]{1,0:T(8,128)(2,1)}, u32[]{:S(2)}, u32[]{:S(2)}) collective-permute-start(bf16[512,2176]{1,0:T(8,128)(2,1)} %add_convert_fusion.4), channel_id=1, source_target_pairs={{5,1},{10,14},{21,17},{26,30}} | collective-permute-start | bytes 6684680 | tf_op jit(solution)/shard_map/ppermute | solution.py:148
  400.4 42.6 %collective-permute-start.38 = (bf16[512,2176]{1,0:T(8,128)(2,1)}, bf16[512,2176]{1,0:T(8,128)(2,1)}, u32[]{:S(2)}, u32[]{:S(2)}) collective-permute-start(bf16[512,2176]{1,0:T(8,128)(2,1)} %add_convert_fusion.3), channel_id=1, source_target_pairs={{6,2},{9,13},{22,18},{25,29}} | collective-permute-start | bytes 6684680 | tf_op jit(solution)/shard_map/ppermute | solution.py:148
  420.8 22.2 %collective-permute-start.37 = (bf16[512,2176]{1,0:T(8,128)(2,1)}, bf16[512,2176]{1,0:T(8,128)(2,1)}, u32[]{:S(2)}, u32[]{:S(2)}) collective-permute-start(bf16[512,2176]{1,0:T(8,128)(2,1)} %get-tuple-element.247), channel_id=1, source_target_pairs={{0,2},{6,4},{9,11},{15,13},{16,18},{22,20},{25,27},{31,29}} | collective-permute-start | bytes 6684680 | tf_op jit(solution)/shard_map/ppermute | solution.py:143
  424.0 17.0 %collective-permute-start.40 = (bf16[256,2176]{1,0:T(8,128)(2,1)}, bf16[256,2176]{1,0:T(8,128)(2,1)}, u32[]{:S(2)}, u32[]{:S(2)}) collective-permute-start(bf16[256,2176]{1,0:T(8,128)(2,1)} %get-tuple-element.250), channel_id=1, source_target_pairs={{1,3},{5,7},{10,8},{14,12},{17,19},{21,23},{26,24},{30,28}} | collective-permute-start | bytes 3342344 | tf_op jit(solution)/shard_map/ppermute | solution.py:143
  429.2 11.7 %collective-permute-start.42 = (bf16[256,2176]{1,0:T(8,128)(2,1)}, bf16[256,2176]{1,0:T(8,128)(2,1)}, u32[]{:S(2)}, u32[]{:S(2)}) collective-permute-start(bf16[256,2176]{1,0:T(8,128)(2,1)} %add_convert_fusion.8), channel_id=1, source_target_pairs={{7,3},{8,12},{23,19},{24,28}} | collective-permute-start | bytes 3342344 | tf_op jit(solution)/shard_map/ppermute | solution.py:148
  451.9 5.9 %collective-permute-start.48 = (bf16[512,128]{1,0:T(8,128)(2,1)S(1)}, bf16[512,128]{1,0:T(8,128)(2,1)S(1)}, u32[]{:S(2)}, u32[]{:S(2)}) collective-permute-start(bf16[512,128]{1,0:T(8,128)(2,1)S(1)} %slice.33), channel_id=1, source_target_pairs={{0,12},{4,8},{8,4},{12,0},{1,13},{5,9},{9,5},{13,1},{2,14},{6,10},... | collective-permute-start | bytes 393224 | tf_op jit(solution)/shard_map/ppermute | solution.py:153
  452.0 7.6 %collective-permute-start.49 = (bf16[512,128]{1,0:T(8,128)(2,1)S(1)}, bf16[512,128]{1,0:T(8,128)(2,1)S(1)}, u32[]{:S(2)}, u32[]{:S(2)}) collective-permute-start(bf16[512,128]{1,0:T(8,128)(2,1)S(1)} %slice.33), channel_id=1, source_target_pairs={{0,8},{4,12},{8,0},{12,4},{1,9},{5,13},{9,1},{13,5},{2,10},{6,14},... | collective-permute-start | bytes 393224 | tf_op jit(solution)/shard_map/ppermute | solution.py:153
  452.1 7.5 %collective-permute-start.50 = (bf16[512,128]{1,0:T(8,128)(2,1)S(1)}, bf16[512,128]{1,0:T(8,128)(2,1)S(1)}, u32[]{:S(2)}, u32[]{:S(2)}) collective-permute-start(bf16[512,128]{1,0:T(8,128)(2,1)S(1)} %slice.33), channel_id=1, source_target_pairs={{0,4},{4,0},{8,12},{12,8},{1,5},{5,1},{9,13},{13,9},{2,6},{6,2},{1... | collective-permute-start | bytes 393224 | tf_op jit(solution)/shard_map/ppermute | solution.py:153
  460.5 19.1 %collective-permute-start.51 = (bf16[512,512]{1,0:T(8,128)(2,1)}, bf16[512,512]{1,0:T(8,128)(2,1)S(1)}, u32[]{:S(2)}, u32[]{:S(2)}) collective-permute-start(bf16[512,512]{1,0:T(8,128)(2,1)} %pad_maximum_fusion.7), channel_id=1, source_target_pairs={{0,1},{1,0},{2,3},{3,2},{4,5},{5,4},{6,7},{7,6},{8,9},{9,8},{10,11... | collective-permute-start | bytes 1572872 | tf_op jit(solution)/shard_map/ppermute | solution.py:450
  (20 other events, 130.8 us)

commit v2 on v0

--- a/solution.py
+++ b/solution.py
@@ -1,13 +1,18 @@
+import functools
+
 import jax
 import jax.numpy as jnp
 from jax import lax
+from jax.experimental import pallas as pl
+from jax.experimental.pallas import tpu as pltpu
 from jax.sharding import PartitionSpec as P
 
 HEAD_DIM = 256
 SEQ = 1024
-
-
-def shards(tokens, query_weight, kv_weight):
+F32, BF16 = jnp.float32, jnp.bfloat16
+
+
+def general(tokens, query_weight, kv_weight):
     local_rows = tokens.shape[0]
     total_rows = local_rows * lax.axis_size("ffn")
     query_count = total_rows // lax.axis_size("hid")
@@ -41,9 +46,245 @@
     return mixed.reshape(query_count, heads_here * HEAD_DIM).astype(jnp.bfloat16)
 
 
+def attention_kernel(rows, where_ref, q_ref, kv_ref, o_ref):
+    tile = rows // 2
+    later = where_ref[0]
+    scale = HEAD_DIM ** (-0.5) * 1.4426950408889634
+    row = lax.broadcasted_iota(jnp.int32, (tile, tile), 0)
+    col = lax.broadcasted_iota(jnp.int32, (tile, tile), 1)
+    seen = col <= row
+
+    def strip(first, count):
+        q = q_ref[pl.ds(first * tile, tile), :]
+        keys = kv_ref[: count * tile, :HEAD_DIM]
+        values = kv_ref[: count * tile, HEAD_DIM:]
+        s = lax.dot_general(q, keys, (((1,), (1,)), ((), ())), preferred_element_type=F32)
+        last = jnp.where(seen, s[:, (count - 1) * tile :], -jnp.inf)
+        s = last if count == 1 else jnp.concatenate([s[:, : (count - 1) * tile], last], axis=1)
+        top = jnp.max(s, axis=1, keepdims=True)
+        w = jnp.exp2((s - top) * scale)
+        total = jnp.sum(w, axis=1, keepdims=True)
+        mixed = jnp.dot(w.astype(BF16), values, preferred_element_type=F32)
+        o_ref[pl.ds(first * tile, tile), :] = (mixed / total).astype(BF16)
+
+    @pl.when(later == 0)
+    def _():
+        strip(0, 1)
+        strip(1, 2)
+
+    @pl.when(later == 1)
+    def _():
+        strip(0, 3)
+        strip(1, 4)
+
+
+def attention(later, queries, shared):
+    rows, width = queries.shape
+    return pl.pallas_call(
+        functools.partial(attention_kernel, rows),
+        out_shape=jax.ShapeDtypeStruct(queries.shape, BF16),
+        grid_spec=pltpu.PrefetchScalarGridSpec(
+            num_scalar_prefetch=1,
+            grid=(width // HEAD_DIM,),
+            in_specs=[
+                pl.BlockSpec((rows, HEAD_DIM), lambda i, _: (0, i)),
+                pl.BlockSpec(shared.shape, lambda i, _: (0, 0)),
+            ],
+            out_specs=pl.BlockSpec((rows, HEAD_DIM), lambda i, _: (0, i)),
+        ),
+        compiler_params=pltpu.CompilerParams(vmem_limit_bytes=32 * 2**20),
+        cost_estimate=pl.CostEstimate(flops=6 * 10**9, bytes_accessed=5 * 10**6, transcendentals=3 * 10**6),
+    )(later.reshape(1).astype(jnp.int32), queries, shared)
+
+
+def other_core(x):
+    return lax.ppermute(x, "hid", [(i, i ^ 1) for i in range(4)])
+
+
+def other_chip(x):
+    return lax.ppermute(x, "hid", [(i, i ^ 2) for i in range(4)])
+
+
+def gathered(x):
+    z = lax.axis_index("ffn")
+    got = [x] + [lax.ppermute(x, "ffn", [(i, i ^ k) for i in range(4)]) for k in (1, 2, 3)]
+    columns = []
+    for i in range(4):
+        column = got[0]
+        for k in (1, 2, 3):
+            column = jnp.where((z ^ i) == k, got[k], column)
+        columns.append(column)
+    return jnp.concatenate(columns, 1)
+
+
+TILE = 512
+SHARES = (6, 6, 4)
+
+
+def product_kernel(terms, sums, kinds, heads, based, sp_ref, *refs):
+    refs = list(refs)
+    base = refs.pop(0) if based else None
+    loaded = []
+    for pieces, weights in terms:
+        xs = [[refs.pop(0) for _ in range(n)] for n in pieces]
+        if weights == "help":
+            ws = [refs.pop(0) for _ in range(8)]
+            loaded.append((xs, ws, None))
+        else:
+            ws = [refs.pop(0) for _ in weights]
+            loaded.append((xs, ws, [refs.pop(0) for _ in weights]))
+    outs = [[refs.pop(0) for _ in kinds] for _ in sums]
+    kept = refs
+    j = pl.program_id(0)
+    inner = sp_ref[0] == 1
+
+    @pl.when(j == 0)
+    def _():
+        for (xs, _, _), keep in zip(loaded, kept):
+            if len(xs) == 1 and len(xs[0]) == 1:
+                continue
+            at = 0
+            for piece in xs:
+                m = piece[0].shape[0]
+                x = piece[0][...]
+                if len(piece) == 2:
+                    x = jnp.where(inner, x, piece[1][...])
+                keep[pl.ds(at, m), :] = x
+                at += m
+
+    def total(chosen, part):
+        acc = None
+        if base is not None:
+            acc = base[...] if part == "heads" else base[:, : heads[1]]
+        for i in chosen:
+            xs, ws, kvs = loaded[i]
+            source = xs[0][0] if len(xs) == 1 and len(xs[0]) == 1 else kept[i]
+            at = 0
+            for k, w in enumerate(ws):
+                if part == "heads":
+                    w = w[...]
+                else:
+                    w = w[:, : heads[1]] if kvs is None else kvs[k][...]
+                x = source[:, at : at + w.shape[0]]
+                at += w.shape[0]
+                y = jnp.dot(x, w, preferred_element_type=F32)
+                acc = y if acc is None else acc + y
+        return acc
+
+    @pl.when(j < heads[0])
+    def _():
+        for chosen, out in zip(sums, outs):
+            acc = total(chosen, "heads")
+            for o in out:
+                o[...] = acc.astype(o.dtype)
+
+    @pl.when(j == heads[0])
+    def _():
+        for chosen, out in zip(sums, outs):
+            acc = total(chosen, "kv")
+            for o in out:
+                o[:, : heads[1]] = acc.astype(o.dtype)
+
+
+def product(sp, query_weight, kv_weight, terms, sums, kinds=(F32, BF16), base=None, base_at=0):
+    width, kv_width = query_weight.shape[1], kv_weight.shape[1]
+    tiles = width // TILE
+    args, specs, shape, scratch = [], [], [], []
+
+    def own(at, size, columns, which):
+        def index(j, sp):
+            return (at if isinstance(at, int) else pl.multiple_of(sp[at[0]], 128), jnp.minimum(j, tiles - 1) * TILE if which else 0)
+
+        return pl.BlockSpec((pl.Element(size), pl.Element(columns)), index)
+
+    if base is not None:
+        m = sum(piece[0].shape[0] for piece in terms[0][0])
+        args.append(base)
+        specs.append(pl.BlockSpec((m, TILE), lambda j, sp: (base_at, j)))
+    for pieces, weights in terms:
+        for piece in pieces:
+            for x in piece:
+                args.append(x)
+                specs.append(pl.BlockSpec(x.shape, lambda j, sp: (0, 0)))
+        rows = sum(piece[0].shape[0] for piece in pieces)
+        depth = pieces[0][0].shape[1]
+        scratch.append(pltpu.VMEM((rows, depth), BF16))
+        if isinstance(weights[0], tuple):
+            args += [query_weight] * len(weights) + [kv_weight] * len(weights)
+            specs += [own(at, size, TILE, True) for at, size in weights]
+            specs += [own(at, size, kv_width, False) for at, size in weights]
+            shape.append((tuple(len(p) for p in pieces), tuple(weights)))
+        else:
+            args += list(weights)
+            specs += [pl.BlockSpec((w.shape[0], TILE), lambda j, sp: (0, j)) for w in weights]
+            shape.append((tuple(len(p) for p in pieces), "help"))
+    rows = [scratch[chosen[0]].shape[0] for chosen in sums]
+    out = pl.pallas_call(
+        functools.partial(
+            product_kernel, shape, sums, kinds, (tiles, kv_width), base is not None
+        ),
+        out_shape=[jax.ShapeDtypeStruct((m, width + kv_width), k) for m in rows for k in kinds],
+        grid_spec=pltpu.PrefetchScalarGridSpec(
+            num_scalar_prefetch=1,
+            grid=(tiles + 1,),
+            in_specs=specs,
+            out_specs=[pl.BlockSpec((m, TILE), lambda j, sp: (0, j)) for m in rows for _ in kinds],
+            scratch_shapes=scratch,
+        ),
+        compiler_params=pltpu.CompilerParams(vmem_limit_bytes=48 * 2**20),
+        cost_estimate=pl.CostEstimate(flops=10**10, bytes_accessed=10**6, transcendentals=0),
+    )(sp, *args)
+    out = [tuple(out[i : i + len(kinds)]) for i in range(0, len(out), len(kinds))]
+    return out[0] if len(out) == 1 else out
+
+
+def staged(tokens, query_weight, kv_weight):
+    rows, depth = tokens.shape
+    width = query_weight.shape[1]
+    columns = width + kv_weight.shape[1]
+    hid = lax.axis_index("hid")
+    chip, core = hid // 2, hid % 2
+    sp = jnp.zeros(1, jnp.int32)
+
+    def at(x, i):
+        return lax.dynamic_index_in_dim(x, i, keepdims=False)
+
+    def shared_rows(parts):
+        mine = gathered(jnp.concatenate([x[:, width:] for x in parts], 0))
+        other = other_core(mine)
+        return jnp.where(core == 0, mine, other), jnp.where(core == 0, other, mine)
+
+    blocks, first = [], 0
+    for sixteenths in SHARES:
+        m = rows * sixteenths // 16
+        blocks.append(lax.all_gather(tokens[first : first + m], "ffn", axis=0, tiled=True))
+        first += m
+    parts, early = [], None
+    for block in blocks:
+        if parts:
+            block, _ = lax.optimization_barrier((block, parts[-1]))
+        if len(parts) == len(SHARES) - 1:
+            early = shared_rows(parts)
+            block, early = lax.optimization_barrier((block, early))
+        m = block.shape[0] // 4
+        summed, sent = product(
+            sp, query_weight, kv_weight, [([(block,)], ((0, depth),))], ((0,),)
+        )
+        summed = jnp.swapaxes(summed.reshape(2, 2, m, columns), 0, 1)
+        sent = jnp.swapaxes(sent.reshape(2, 2, m, columns), 0, 1)
+        summed = at(summed, core) + other_core(at(sent, 1 - core)).astype(F32)
+        summed = at(summed, chip) + other_chip(at(summed, 1 - chip).astype(BF16)).astype(F32)
+        parts.append(summed.astype(BF16))
+    queries = jnp.concatenate([x[:, :width] for x in parts], 0)
+    late = shared_rows(parts[-1:])
+    shared = jnp.concatenate([early[0], late[0], early[1], late[1]], 0)
+    return attention(core, queries, shared)
+
+
 def solution(mesh):
+    fits = mesh.shape["ffn"] == 4 and mesh.shape["hid"] == 4 and mesh.shape["grp"] == 2
     return jax.shard_map(
-        shards,
+        staged if fits else general,
         mesh=mesh,
         in_specs=(P(("grp", "ffn"), "hid"), P("hid", "ffn"), P("hid", "ffn")),
         out_specs=P(("grp", "hid"), "ffn"),

time: 639 us -> 431 us (0.67)
  waiting for transfers between devices: 506 us -> 305 us
  matrix products: 84.7 us -> 0 us
  Pallas kernels: 0 us -> 74.2 us
  blocking collectives: 27.5 us -> 0 us
  starting transfers between devices: 0.12 us -> 16.1 us
  other arithmetic: 3.47 us -> 12.1 us
  local copies, waits for them, and re-layouts: 2.38 us -> 9.56 us
    all_gather x3, waiting for transfers between devices: 412 us -> 229 us  [staged(): lax.all_gather(tokens[first:first + m], 'ffn', axis=0, tiled=True)]
    reduce_scatter x1 -> x0, waiting for transfers between devices: 92.5 us -> none  [shards(): lax.psum_scatter(query_partial, 'hid', scatter_dimension=0, tiled=True)]
    dot_general x4 -> x0, matrix products: 84.7 us -> none  [the longest x1 47.8 us: shards(): jnp.dot(lax.all_gather(tokens, 'ffn', axis=0, tiled=True), query_weight,...]
    ppermute x0 -> x14, waiting for transfers between devices: none -> 75.5 us  [the longest x3 47.7 us: other_chip(): return lax.ppermute(x, 'hid', [(i, i ^ 2) for i in range(4)])]
    pallas_call x0 -> x4, Pallas kernels: none -> 74.2 us  [the longest x3 62.6 us: product(): pl.pallas_call(functools.partial(product_kernel, shape, sums, kinds, (til...]
    psum x1 -> x0, blocking collectives: 27.5 us -> none  [shards(): kv_summed = lax.psum(kv_partial, 'hid')]
    ppermute x0 -> x14, starting transfers between devices: none -> 16 us  [the longest x6 7.22 us: gathered(): lax.ppermute(x, 'ffn', [(i, i ^ k) for i in range(4)])]
    add x0 -> x3, other arithmetic: none -> 6.88 us  [staged(): summed = at(summed, core) + other_core(at(sent, 1 - core)).astype(F32)]
  transfers between devices with their start and end apart: 4 -> 17, of which waited for: 4 -> 14; matrix products, arithmetic and copies ran while one was open for 9% -> 3% of each run, Pallas kernels for 0% -> 11%
where the time goes in v2:
time: 431 us
  waiting for transfers between devices  305 us (71%)
  Pallas kernels  74.2 us (17%)
  starting transfers between devices  16.1 us (4%)
  between operations  13.3 us (3%)
  other arithmetic  12.1 us (3%)
  local copies, waits for them, and re-layouts  9.56 us (2%)
    all_gather x3, waiting for transfers between devices, staged(): lax.all_gather(tokens[first:first + m], 'ffn', axis=0, tiled=True)  229 us
    pallas_call x3, Pallas kernels, product(): pl.pallas_call(functools.partial(product_kernel, shape, sums, kinds, (til...  62.6 us
    ppermute x3, waiting for transfers between devices, other_chip(): return lax.ppermute(x, 'hid', [(i, i ^ 2) for i in range(4)])  47.7 us
    ppermute x6, waiting for transfers between devices, gathered(): lax.ppermute(x, 'ffn', [(i, i ^ k) for i in range(4)])  18.1 us
    pallas_call x1, Pallas kernels, attention(): pl.pallas_call(functools.partial(attention_kernel, rows), out_shape=jax.S...  11.6 us
    ppermute x5, waiting for transfers between devices, other_core(): return lax.ppermute(x, 'hid', [(i, i ^ 1) for i in range(4)])  9.69 us
  transfers between devices with their start and end apart: 17, of which 14 were waited for; matrix products, arithmetic and copies ran while one was open for 3% of the time, Pallas kernels for 11%

profile of v2, /device:TPU:1, one launch (start us, length us, event | category | flops | bytes accessed | tf_op | source)
XLA Modules:
  0.0 430.7 jit_solution(4449385913601101893)
XLA Ops:
  6.5 4.0 fusion.6
  10.6 0.0 all-gather.4.cloned.1.call-update
  10.6 0.0 all-gather.6.cloned.1.call-start
  10.7 0.7 all-gather.6.cloned.1.call-update
  11.4 0.0 all-gather.8.cloned.1.call-start
  11.4 129.8 %all-gather.4.cloned.1.call-done.refs_0_ = bf16[768,4608]{1,0:T(8,128)(2,1)} async-done(((bf16[192,4608]{1,0:T(8,128)(2,1)}), bf16[768,4608]{1,0:T(8,128)(2,1)}) %all-gather.4.cloned.1.call-update) | async-done | bytes 7077904 | tf_op jit(solution)/shard_map/all_gather | solution.py:260
  141.3 22.9 %shard_map.37 = (f32[768,2176]{1,0:T(8,128)}, bf16[768,2176]{1,0:T(8,128)(2,1)S(1)}) custom-call(s32[1]{0:T(128)} %constant.71.clone.1.sp_ref, bf16[768,4608]{1,0:T(8,128)(2,1)} %all-gather.4.cloned.1.call-done.refs_0_, bf16[4608,2048]{1,0:T(8,128)(2,1)} %refs_1_.5, bf16[4608,128]{1,0:T(8,128)(2,1)S(1)} %copy-done), custom_call_target="tpu_custom_call" | custom-call | flops 10000000000 | bytes 1000000 | tf_op jit(solution)/shard_map/pallas_call | solution.py:222
  164.2 0.1 dynamic-slice_bitcast_fusion.1
  164.3 0.5 collective-permute-start
  164.8 3.3 collective-permute-done
  168.1 2.8 bitcast_add_fusion.1
  170.9 1.8 copy-done.1
  172.7 0.1 fusion.3
  172.8 1.2 collective-permute-start.1
  174.1 2.4 slice.31
  176.4 0.0 all-gather.8.cloned.1.call-update
  176.5 16.3 %collective-permute-done.1 = bf16[192,2176]{1,0:T(8,128)(2,1)S(1)} collective-permute-done((bf16[192,2176]{1,0:T(8,128)(2,1)S(1)}, bf16[192,2176]{1,0:T(8,128)(2,1)S(1)}, u32[]{:S(2)}, u32[]{:S(2)}) %collective-permute-start.1) | collective-permute-done | bytes 835616 | tf_op jit(solution)/shard_map/ppermute | solution.py:105
  192.8 1.6 fusion.1
  194.4 74.9 %all-gather.6.cloned.1.call-done.refs_0_ = bf16[768,4608]{1,0:T(8,128)(2,1)} async-done(((bf16[192,4608]{1,0:T(8,128)(2,1)}), bf16[768,4608]{1,0:T(8,128)(2,1)}) %all-gather.6.cloned.1.call-update) | async-done | bytes 7077904 | tf_op jit(solution)/shard_map/all_gather | solution.py:260
  269.3 22.9 %shard_map.38 = (f32[768,2176]{1,0:T(8,128)}, bf16[768,2176]{1,0:T(8,128)(2,1)S(1)}) custom-call(s32[1]{0:T(128)} %constant.71.clone.1.sp_ref, bf16[768,4608]{1,0:T(8,128)(2,1)} %all-gather.6.cloned.1.call-done.refs_0_, bf16[4608,2048]{1,0:T(8,128)(2,1)} %refs_1_.5, bf16[4608,128]{1,0:T(8,128)(2,1)S(1)} %copy-done), custom_call_target="tpu_custom_call" | custom-call | flops 10000000000 | bytes 1000000 | tf_op jit(solution)/shard_map/pallas_call | solution.py:222
  292.3 0.1 dynamic-slice_bitcast_fusion
  292.4 0.5 collective-permute-start.2
  292.9 3.2 collective-permute-done.2
  296.1 2.3 bitcast_add_fusion
  298.3 0.1 fusion.4
  298.4 1.3 collective-permute-start.3
  299.7 18.7 %collective-permute-done.3 = bf16[192,2176]{1,0:T(8,128)(2,1)S(1)} collective-permute-done((bf16[192,2176]{1,0:T(8,128)(2,1)S(1)}, bf16[192,2176]{1,0:T(8,128)(2,1)S(1)}, u32[]{:S(2)}, u32[]{:S(2)}) %collective-permute-start.3) | collective-permute-done | bytes 835616 | tf_op jit(solution)/shard_map/ppermute | solution.py:105
  318.4 0.2 fusion
  318.6 0.1 collective-permute-start.4
  318.7 0.4 collective-permute-start.5
  319.1 3.1 collective-permute-start.6
  322.2 4.6 %collective-permute-done.4 = bf16[384,128]{1,0:T(8,128)(2,1)S(1)} collective-permute-done((bf16[384,128]{1,0:T(8,128)(2,1)S(1)}, bf16[384,128]{1,0:T(8,128)(2,1)S(1)}, u32[]{:S(2)}, u32[]{:S(2)}) %collective-permute-start.4) | collective-permute-done | bytes 98336 | tf_op jit(solution)/shard_map/ppermute | solution.py:110
  326.9 12.3 %collective-permute-done.5 = bf16[384,128]{1,0:T(8,128)(2,1)S(1)} collective-permute-done((bf16[384,128]{1,0:T(8,128)(2,1)S(1)}, bf16[384,128]{1,0:T(8,128)(2,1)S(1)}, u32[]{:S(2)}, u32[]{:S(2)}) %collective-permute-start.5) | collective-permute-done | bytes 98336 | tf_op jit(solution)/shard_map/ppermute | solution.py:110
  339.2 0.0 collective-permute-done.6
  339.2 0.6 copy-done.3
  339.8 0.1 select_select_fusion.2
  339.9 1.0 select_select_fusion.3
  340.9 0.8 pad_maximum_fusion.2
  341.6 0.7 collective-permute-start.7
  342.3 24.4 %all-gather.8.cloned.1.call-done.refs_0_ = bf16[512,4608]{1,0:T(8,128)(2,1)} async-done(((bf16[128,4608]{1,0:T(8,128)(2,1)}), bf16[512,4608]{1,0:T(8,128)(2,1)}) %all-gather.8.cloned.1.call-update) | async-done | bytes 4718608 | tf_op jit(solution)/shard_map/all_gather | solution.py:260
  366.7 0.0 collective-permute-done.7
  366.7 1.2 broadcast_select_fusion
  367.9 16.7 %shard_map.39 = (f32[512,2176]{1,0:T(8,128)}, bf16[512,2176]{1,0:T(8,128)(2,1)S(1)}) custom-call(s32[1]{0:T(128)} %constant.71.clone.1.sp_ref, bf16[512,4608]{1,0:T(8,128)(2,1)} %all-gather.8.cloned.1.call-done.refs_0_, bf16[4608,2048]{1,0:T(8,128)(2,1)} %refs_1_.5, bf16[4608,128]{1,0:T(8,128)(2,1)S(1)} %copy-done), custom_call_target="tpu_custom_call" | custom-call | flops 10000000000 | bytes 1000000 | tf_op jit(solution)/shard_map/pallas_call | solution.py:222
  384.7 0.1 dynamic-slice_bitcast_fusion.2
  384.7 0.7 collective-permute-start.8
  385.4 2.4 collective-permute-done.8
  387.8 1.9 bitcast_add_fusion.2
  389.6 0.1 fusion.5
  389.7 1.3 collective-permute-start.9
  391.0 12.7 %collective-permute-done.9 = bf16[128,2176]{1,0:T(8,128)(2,1)S(1)} collective-permute-done((bf16[128,2176]{1,0:T(8,128)(2,1)S(1)}, bf16[128,2176]{1,0:T(8,128)(2,1)S(1)}, u32[]{:S(2)}, u32[]{:S(2)}) %collective-permute-start.9) | collective-permute-done | bytes 557088 | tf_op jit(solution)/shard_map/ppermute | solution.py:105
  403.6 0.1 fusion.2
  403.8 0.3 collective-permute-start.10
  404.1 0.0 collective-permute-start.11
  404.1 3.3 collective-permute-start.12
  407.4 0.1 slice.37
  407.5 0.9 collective-permute-done.10
  408.4 0.0 collective-permute-done.11
  408.4 0.3 collective-permute-done.12
  408.8 2.6 collective-permute-start.13
  411.4 0.2 pad_maximum_fusion.q_ref
  411.6 0.8 collective-permute-done.13
  412.4 0.1 broadcast_select_fusion.3
  412.5 0.1 pad_maximum_fusion.1.kv_ref
  412.5 11.6 %shard_map.40 = bf16[512,2048]{1,0:T(8,128)(2,1)} custom-call(s32[1]{0:T(128)} %bitcast.where_ref, bf16[512,2048]{1,0:T(8,128)(2,1)S(1)} %pad_maximum_fusion.q_ref, bf16[1024,512]{1,0:T(8,128)(2,1)S(1)} %pad_maximum_fusion.1.kv_ref), custom_call_target="tpu_custom_call" | custom-call | flops 6000000000 | bytes 5000000 | tf_op jit(solution)/shard_map/pallas_call | solution.py:83
  (16 shorter events, 0.1 us)
Async XLA Ops:
  6.5 134.7 %all-gather.4.cloned.1.call-start = ((), (), s32[]{:S(2)}) async-start(), calls=%async_computation | async-start | bytes 8847360 | tf_op jit(solution)/shard_map/all_gather | solution.py:260
  10.6 130.7 %copy-start = (bf16[4608,128]{1,0:T(8,128)(2,1)S(1)}, bf16[4608,128]{1,0:T(8,128)(2,1)}, u32[]{:S(2)}) copy-start(bf16[4608,128]{1,0:T(8,128)(2,1)} %refs_2_.5) | copy-start | bytes 3538948
  10.6 258.7 %all-gather.6.cloned.1.call-start = ((), (), s32[]{:S(2)}) async-start(), calls=%async_computation.1 | async-start | bytes 8847360 | tf_op jit(solution)/shard_map/all_gather | solution.py:260
  11.4 355.4 %all-gather.8.cloned.1.call-start = ((), (), s32[]{:S(2)}) async-start(), calls=%async_computation.2 | async-start | bytes 5898240 | tf_op jit(solution)/shard_map/all_gather | solution.py:260
  164.3 3.8 collective-permute-start
  170.9 1.8 copy-start.1
  172.8 20.0 %collective-permute-start.1 = (bf16[192,2176]{1,0:T(8,128)(2,1)S(1)}, bf16[192,2176]{1,0:T(8,128)(2,1)S(1)}, u32[]{:S(2)}, u32[]{:S(2)}) collective-permute-start(bf16[192,2176]{1,0:T(8,128)(2,1)S(1)} %fusion.3), channel_id=1, source_target_pairs={{0,2},{1,3},{2,0},{3,1},{4,6},{5,7},{6,4},{7,5},{8,10},{9,11},{10,... | collective-permute-start | bytes 2506760 | tf_op jit(solution)/shard_map/ppermute | solution.py:105
  194.4 213.0 %copy-start.2 = (bf16[192,2176]{1,0:T(8,128)(2,1)}, bf16[192,2176]{1,0:T(8,128)(2,1)S(1)}, u32[]{:S(2)}) copy-start(bf16[192,2176]{1,0:T(8,128)(2,1)S(1)} %fusion.1) | copy-start | bytes 2506756
  292.4 3.7 collective-permute-start.2
  298.4 20.0 %collective-permute-start.3 = (bf16[192,2176]{1,0:T(8,128)(2,1)S(1)}, bf16[192,2176]{1,0:T(8,128)(2,1)S(1)}, u32[]{:S(2)}, u32[]{:S(2)}) collective-permute-start(bf16[192,2176]{1,0:T(8,128)(2,1)S(1)} %fusion.4), channel_id=1, source_target_pairs={{0,2},{1,3},{2,0},{3,1},{4,6},{5,7},{6,4},{7,5},{8,10},{9,11},{10,... | collective-permute-start | bytes 2506760 | tf_op jit(solution)/shard_map/ppermute | solution.py:105
  318.6 8.2 %collective-permute-start.4 = (bf16[384,128]{1,0:T(8,128)(2,1)S(1)}, bf16[384,128]{1,0:T(8,128)(2,1)S(1)}, u32[]{:S(2)}, u32[]{:S(2)}) collective-permute-start(bf16[384,128]{1,0:T(8,128)(2,1)S(1)} %pad_maximum_fusion.4), channel_id=1, source_target_pairs={{0,12},{4,8},{8,4},{12,0},{1,13},{5,9},{9,5},{13,1},{2,14},{6,10},... | collective-permute-start | bytes 294920 | tf_op jit(solution)/shard_map/ppermute | solution.py:110
  318.7 20.5 %collective-permute-start.5 = (bf16[384,128]{1,0:T(8,128)(2,1)S(1)}, bf16[384,128]{1,0:T(8,128)(2,1)S(1)}, u32[]{:S(2)}, u32[]{:S(2)}) collective-permute-start(bf16[384,128]{1,0:T(8,128)(2,1)S(1)} %pad_maximum_fusion.4), channel_id=1, source_target_pairs={{0,8},{4,12},{8,0},{12,4},{1,9},{5,13},{9,1},{13,5},{2,10},{6,14},... | collective-permute-start | bytes 294920 | tf_op jit(solution)/shard_map/ppermute | solution.py:110
  319.1 20.1 %collective-permute-start.6 = (bf16[384,128]{1,0:T(8,128)(2,1)S(1)}, bf16[384,128]{1,0:T(8,128)(2,1)S(1)}, u32[]{:S(2)}, u32[]{:S(2)}) collective-permute-start(bf16[384,128]{1,0:T(8,128)(2,1)S(1)} %pad_maximum_fusion.4), channel_id=1, source_target_pairs={{0,4},{4,0},{8,12},{12,8},{1,5},{5,1},{9,13},{13,9},{2,6},{6,2},{1... | collective-permute-start | bytes 294920 | tf_op jit(solution)/shard_map/ppermute | solution.py:110
  339.2 0.6 copy-start.3
  341.6 25.1 %collective-permute-start.7 = (bf16[384,512]{1,0:T(8,128)(2,1)}, bf16[384,512]{1,0:T(8,128)(2,1)}, u32[]{:S(2)}, u32[]{:S(2)}) collective-permute-start(bf16[384,512]{1,0:T(8,128)(2,1)} %pad_maximum_fusion.2), channel_id=1, source_target_pairs={{0,1},{1,0},{2,3},{3,2},{4,5},{5,4},{6,7},{7,6},{8,9},{9,8},{10,11... | collective-permute-start | bytes 1179656 | tf_op jit(solution)/shard_map/ppermute | solution.py:101
  384.7 3.0 collective-permute-start.8
  389.7 13.9 %collective-permute-start.9 = (bf16[128,2176]{1,0:T(8,128)(2,1)S(1)}, bf16[128,2176]{1,0:T(8,128)(2,1)S(1)}, u32[]{:S(2)}, u32[]{:S(2)}) collective-permute-start(bf16[128,2176]{1,0:T(8,128)(2,1)S(1)} %fusion.5), channel_id=1, source_target_pairs={{0,2},{1,3},{2,0},{3,1},{4,6},{5,7},{6,4},{7,5},{8,10},{9,11},{10,... | collective-permute-start | bytes 1671176 | tf_op jit(solution)/shard_map/ppermute | solution.py:105
  403.8 4.6 %collective-permute-start.10 = (bf16[128,128]{1,0:T(8,128)(2,1)S(1)}, bf16[128,128]{1,0:T(8,128)(2,1)S(1)}, u32[]{:S(2)}, u32[]{:S(2)}) collective-permute-start(bf16[128,128]{1,0:T(8,128)(2,1)S(1)} %slice.41), channel_id=1, source_target_pairs={{0,12},{4,8},{8,4},{12,0},{1,13},{5,9},{9,5},{13,1},{2,14},{6,10},... | collective-permute-start | bytes 98312 | tf_op jit(solution)/shard_map/ppermute | solution.py:110
  404.1 4.3 collective-permute-start.11
  404.1 4.6 %collective-permute-start.12 = (bf16[128,128]{1,0:T(8,128)(2,1)S(1)}, bf16[128,128]{1,0:T(8,128)(2,1)S(1)}, u32[]{:S(2)}, u32[]{:S(2)}) collective-permute-start(bf16[128,128]{1,0:T(8,128)(2,1)S(1)} %slice.41), channel_id=1, source_target_pairs={{0,4},{4,0},{8,12},{12,8},{1,5},{5,1},{9,13},{13,9},{2,6},{6,2},{1... | collective-permute-start | bytes 98312 | tf_op jit(solution)/shard_map/ppermute | solution.py:110
  407.4 4.1 slice-start
  408.8 3.6 collective-permute-start.13
Sparse Core Ops, SparseCore 0:
  10.7 130.4 all-gather.3
  142.8 126.4 all-gather.5
  270.9 95.7 all-gather.7

commit v3 on v2

--- a/solution.py
+++ b/solution.py
@@ -97,6 +97,42 @@
     )(later.reshape(1).astype(jnp.int32), queries, shared)
 
 
+MID = [(1, 2), (2, 1)]
+INTO = [(0, 1), (3, 2)]
+OUT = [(1, 0), (2, 3)]
+ORDER = ((0, 1, 2, 3), (1, 2, 1, 2), (2, 0, 3, 1), (3, 3, 0, 0))
+
+
+def along(axis, pairs):
+    return lambda x: lax.ppermute(x, axis, pairs)
+
+
+def gate(xs, deps):
+    deps = tuple(x for x in deps if x is not None)
+    return lax.optimization_barrier((tuple(xs), deps))[0]
+
+
+class Steps:
+    def __init__(self):
+        self.last, self.at, self.due = None, 0, {}
+
+    def step(self):
+        self.at += 1
+
+    def start(self, move, x, due=1):
+        (x,) = gate((x,), (self.last,))
+        y = move(x)
+        self.due.setdefault(self.at + due, []).append(y)
+        return y
+
+    def run(self, work, *xs, after=()):
+        arrived = [y for at in list(self.due) if at <= self.at for y in self.due.pop(at)]
+        xs = gate(xs, [self.last, *arrived, *after])
+        out = work(*xs)
+        self.last = jax.tree.leaves(out)[0]
+        return out
+
+
 def other_core(x):
     return lax.ppermute(x, "hid", [(i, i ^ 1) for i in range(4)])
 
@@ -118,7 +154,6 @@
 
 
 TILE = 512
-SHARES = (6, 6, 4)
 
 
 def product_kernel(terms, sums, kinds, heads, based, sp_ref, *refs):
@@ -127,8 +162,8 @@
     loaded = []
     for pieces, weights in terms:
         xs = [[refs.pop(0) for _ in range(n)] for n in pieces]
-        if weights == "help":
-            ws = [refs.pop(0) for _ in range(8)]
+        if isinstance(weights, int):
+            ws = [refs.pop(0) for _ in range(weights)]
             loaded.append((xs, ws, None))
         else:
             ws = [refs.pop(0) for _ in weights]
@@ -217,7 +252,7 @@
         else:
             args += list(weights)
             specs += [pl.BlockSpec((w.shape[0], TILE), lambda j, sp: (0, j)) for w in weights]
-            shape.append((tuple(len(p) for p in pieces), "help"))
+            shape.append((tuple(len(p) for p in pieces), len(weights)))
     rows = [scratch[chosen[0]].shape[0] for chosen in sums]
     out = pl.pallas_call(
         functools.partial(
@@ -231,7 +266,7 @@
             out_specs=[pl.BlockSpec((m, TILE), lambda j, sp: (0, j)) for m in rows for _ in kinds],
             scratch_shapes=scratch,
         ),
-        compiler_params=pltpu.CompilerParams(vmem_limit_bytes=48 * 2**20),
+        compiler_params=pltpu.CompilerParams(vmem_limit_bytes=60 * 2**20),
         cost_estimate=pl.CostEstimate(flops=10**10, bytes_accessed=10**6, transcendentals=0),
     )(sp, *args)
     out = [tuple(out[i : i + len(kinds)]) for i in range(0, len(out), len(kinds))]
@@ -242,41 +277,150 @@
     rows, depth = tokens.shape
     width = query_weight.shape[1]
     columns = width + kv_weight.shape[1]
-    hid = lax.axis_index("hid")
+    z, hid, grp = (lax.axis_index(name) for name in ("ffn", "hid", "grp"))
     chip, core = hid // 2, hid % 2
-    sp = jnp.zeros(1, jnp.int32)
+    part = depth // 6 // 128 * 128
+    first = depth - 2 * part
+    mid, into, out = along("ffn", MID), along("ffn", INTO), along("ffn", OUT)
+    across = along("grp", [(0, 1), (1, 0)])
+    own_at, far_at = first + grp * part, first + (1 - grp) * part
+    inner = (z == 1) | (z == 2)
+    sp = jnp.stack([inner, own_at, far_at]).astype(jnp.int32)
+    weights1 = ((0, first),)
+    weights2 = (((1,), part), ((2,), part))
+    early_rows = rows // 2
+    spans = ((0, early_rows), (early_rows, rows - early_rows))
+    share = part // 2
 
     def at(x, i):
         return lax.dynamic_index_in_dim(x, i, keepdims=False)
+
+    def from_plane(x, block):
+        stage = 0
+        for i, order in enumerate(ORDER):
+            stage += i * (sum(jnp.where(z == k, b, 0) for k, b in enumerate(order)) == block)
+        m = x.shape[0] // 4
+        return lax.dynamic_slice_in_dim(x, stage * m, m, 0)
+
+    def give_core(x):
+        return jnp.stack([from_plane(x, 2 * i + 1 - core) for i in range(2)])
+
+    def over_cores(x, got):
+        keep = from_plane(x, hid) + at(got, chip).astype(F32)
+        give = from_plane(x, hid ^ 2) + at(got, 1 - chip).astype(F32)
+        return keep, give.astype(BF16)
 
     def shared_rows(parts):
         mine = gathered(jnp.concatenate([x[:, width:] for x in parts], 0))
         other = other_core(mine)
         return jnp.where(core == 0, mine, other), jnp.where(core == 0, other, mine)
 
-    blocks, first = [], 0
-    for sixteenths in SHARES:
-        m = rows * sixteenths // 16
-        blocks.append(lax.all_gather(tokens[first : first + m], "ffn", axis=0, tiled=True))
-        first += m
-    parts, early = [], None
-    for block in blocks:
-        if parts:
-            block, _ = lax.optimization_barrier((block, parts[-1]))
-        if len(parts) == len(SHARES) - 1:
-            early = shared_rows(parts)
-            block, early = lax.optimization_barrier((block, early))
-        m = block.shape[0] // 4
-        summed, sent = product(
-            sp, query_weight, kv_weight, [([(block,)], ((0, depth),))], ((0,),)
+    def mark(*xs):
+        return sum(x[:16, :128] for x in xs)
+
+    def weights_at(i):
+        return jnp.concatenate(
+            [
+                lax.dynamic_slice_in_dim(w, own_at + i * share, share, 0)
+                for w in (query_weight, kv_weight)
+            ],
+            1,
         )
-        summed = jnp.swapaxes(summed.reshape(2, 2, m, columns), 0, 1)
-        sent = jnp.swapaxes(sent.reshape(2, 2, m, columns), 0, 1)
-        summed = at(summed, core) + other_core(at(sent, 1 - core)).astype(F32)
-        summed = at(summed, chip) + other_chip(at(summed, 1 - chip).astype(BF16)).astype(F32)
-        parts.append(summed.astype(BF16))
-    queries = jnp.concatenate([x[:, :width] for x in parts], 0)
-    late = shared_rows(parts[-1:])
+
+    def shares(rest, w):
+        return product(
+            sp,
+            query_weight,
+            kv_weight,
+            [([(x,) for x in rest], weights2), ([(x,) for x in rest], w)],
+            ((0,), (1,)),
+        )
+
+    def whole(pieces, base):
+        return product(
+            sp, query_weight, kv_weight, [(pieces, weights1)], ((0,),), base=base
+        )
+
+    t1 = [tokens[a : a + m, :first] for a, m in spans]
+    t2 = [
+        jnp.concatenate(
+            [lax.dynamic_slice(tokens, (a, i), (m, part)) for i in (own_at, far_at)], 1
+        )
+        for a, m in spans
+    ]
+    s = Steps()
+    c2 = [s.start(into, x) for x in t2]
+    b1 = [s.start(mid, t1[0])]
+    e1 = [s.start(out, t1[0])]
+    s.step()
+    s.run(mark, c2[0], b1[0])
+    w_in = [s.start(into, weights_at(0))]
+    d2 = [s.start(mid, x) for x in c2]
+    e1.append(s.start(out, t1[1]))
+    s.step()
+    s.run(mark, w_in[0], d2[0])
+    w_in.append(s.start(into, weights_at(1)))
+    b1.append(s.start(mid, t1[1]))
+    f1 = [s.start(out, b1[0])]
+    w_far = [s.start(across, w_in[0])]
+    s.step()
+    s.run(mark, w_in[1], b1[1])
+    c1 = [s.start(into, t1[0])]
+    b2 = [s.start(mid, x) for x in t2]
+    f1.append(s.start(out, b1[1]))
+    w_far.append(s.start(across, w_in[1]))
+    s.step()
+    s.run(mark, c1[0], b2[0])
+    c1.append(s.start(into, t1[1]))
+    d1 = [s.start(mid, c1[0])]
+    rest = [[jnp.where(inner, x, jnp.zeros_like(x)), *y] for x, *y in zip(t2, b2, c2, d2)]
+    w_help = w_in + w_far
+
+    def complete(x, y):
+        return (x + y.astype(F32)).astype(BF16)
+
+    def finished(q, got, o):
+        return (q + got.astype(F32) + o.astype(F32)).astype(BF16)
+
+    def block(i, after=None):
+        b, e, c, f, d, g = gate([y[i] for y in (b1, e1, c1, f1, d1, g1)], (after,))
+        return [(t1[i],), (b, e), (c, f), (d, g)]
+
+    (p0, _), (h0, h0_16) = s.run(shares, rest[0], w_help)
+    s.step()
+    s.run(mark, c1[1], d1[0])
+    d1.append(s.start(mid, c1[1]))
+    g1 = [s.start(out, d1[0])]
+    (h0_16,) = gate((h0_16,), (s.last,))
+    h0_core = s.start(other_core, give_core(h0_16))
+    h0, h0_give = s.run(over_cores, h0, h0_core)
+    h0_got = s.start(other_chip, h0_give)
+    (p1, _), (h1, h1_16) = s.run(shares, rest[1], w_help)
+    s.step()
+    h0 = s.run(complete, h0, h0_got)
+    g1.append(s.start(out, d1[1]))
+    o0 = s.start(out, h0, 2)
+    (h1_16,) = gate((h1_16,), (s.last,))
+    h1_core = s.start(other_core, give_core(h1_16))
+    h1, h1_give = s.run(over_cores, h1, h1_core)
+    h1_got = s.start(other_chip, h1_give)
+    q0, q0_16 = s.run(whole, block(0, h1_give), p0)
+    s.step()
+    h1 = s.run(complete, h1, h1_got)
+    o1 = s.start(out, h1, 9)
+    q0_core = s.start(other_core, give_core(q0_16))
+    q0, q0_give = s.run(over_cores, q0, q0_core)
+    q0_got = s.start(other_chip, q0_give)
+    q1, q1_16 = s.run(whole, block(1, q0_give), p1)
+    s.step()
+    q0 = s.run(finished, q0, q0_got, o0)
+    q1_core = s.start(other_core, give_core(q1_16))
+    q1, q1_give = s.run(over_cores, q1, q1_core)
+    q1_got = other_chip(q1_give)
+    early = shared_rows([q0])
+    q1 = finished(q1, q1_got, o1)
+    queries = jnp.concatenate([x[:, :width] for x in (q0, q1)], 0)
+    late = shared_rows([q1])
     shared = jnp.concatenate([early[0], late[0], early[1], late[1]], 0)
     return attention(core, queries, shared)
 

time: 431 us -> 398 us (0.923)
  waiting for transfers between devices: 305 us -> 167 us
  starting transfers between devices: 16.1 us -> 73.7 us
  Pallas kernels: 74.2 us -> 112 us
  other arithmetic: 12.1 us -> 24.9 us
  between operations: 13.3 us -> 0.59 us
  local copies, waits for them, and re-layouts: 9.56 us -> 19.5 us
    all_gather x3 -> x0, waiting for transfers between devices: 229 us -> none  [staged(): lax.all_gather(tokens[first:first + m], 'ffn', axis=0, tiled=True)]
    ppermute x0 -> x24, waiting for transfers between devices: none -> 133 us  [along(): return lambda x: lax.ppermute(x, axis, pairs)]
    ppermute x0 -> x24, starting transfers between devices: none -> 51.1 us  [along(): return lambda x: lax.ppermute(x, axis, pairs)]
    ppermute x3 -> x4, waiting for transfers between devices: 47.7 us -> 0.31 us  [other_chip(): return lax.ppermute(x, 'hid', [(i, i ^ 2) for i in range(4)])]
    pallas_call x3 -> x4, Pallas kernels: 62.6 us -> 99.7 us  [product(): pl.pallas_call(functools.partial(product_kernel, shape, sums, kinds, (til...]
    convert_element_type x3 -> x7, other arithmetic: 1.87 us -> 18 us  [the longest x3 9.38 us: over_cores(): return (keep, give.astype(BF16))]
    ppermute x5 -> x6, starting transfers between devices: 5.02 us -> 11.6 us  [other_core(): return lax.ppermute(x, 'hid', [(i, i ^ 1) for i in range(4)])]
    ppermute x6, waiting for transfers between devices: 18.1 us -> 24.6 us  [gathered(): lax.ppermute(x, 'ffn', [(i, i ^ k) for i in range(4)])]
  transfers between devices with their start and end apart: 17 -> 40, of which waited for: 14 -> 19; matrix products, arithmetic and copies ran while one was open for 3% -> 6% of each run, Pallas kernels for 11% -> 25%
where the time goes in v3:
time: 398 us; the launch traced here: 397 us
  waiting for transfers between devices  167 us (42%)
  Pallas kernels  112 us (28%)
  starting transfers between devices  73.7 us (19%)
  other arithmetic  24.9 us (6%)
  local copies, waits for them, and re-layouts  19.5 us (5%)
    ppermute x24, waiting for transfers between devices, along(): return lambda x: lax.ppermute(x, axis, pairs)  133 us
    pallas_call x4, Pallas kernels, product(): pl.pallas_call(functools.partial(product_kernel, shape, sums, kinds, (til...  99.7 us
    ppermute x24, starting transfers between devices, along(): return lambda x: lax.ppermute(x, axis, pairs)  51.1 us
    ppermute x6, waiting for transfers between devices, gathered(): lax.ppermute(x, 'ffn', [(i, i ^ k) for i in range(4)])  24.6 us
    pallas_call x1, Pallas kernels, attention(): pl.pallas_call(functools.partial(attention_kernel, rows), out_shape=jax.S...  11.9 us
    ppermute x6, starting transfers between devices, other_core(): return lax.ppermute(x, 'hid', [(i, i ^ 1) for i in range(4)])  11.6 us
    convert_element_type x3, other arithmetic, over_cores(): return (keep, give.astype(BF16))  9.38 us
    ppermute x6, waiting for transfers between devices, other_core(): return lax.ppermute(x, 'hid', [(i, i ^ 1) for i in range(4)])  9.27 us
  transfers between devices with their start and end apart: 40, of which 19 were waited for; matrix products, arithmetic and copies ran while one was open for 6% of the time, Pallas kernels for 25%

profile of v3, /device:TPU:1, one launch (start us, length us, event | category | flops | bytes accessed | tf_op | source)
XLA Modules:
  0.0 397.2 jit_solution(3556146668377721874)
XLA Ops:
  0.0 2.1 fusion.7
  2.1 2.1 collective-permute-start
  4.2 1.3 collective-permute-start.1
  5.5 1.5 constant_dynamic-slice_fusion.1
  7.0 1.8 pad_maximum_fusion.9
  8.8 7.2 %collective-permute-start.2 = (bf16[256,1536]{1,0:T(8,128)(2,1)}, bf16[256,1536]{1,0:T(8,128)(2,1)}, u32[]{:S(2)}, u32[]{:S(2)}) collective-permute-start(bf16[256,1536]{1,0:T(8,128)(2,1)} %get-tuple-element.128), channel_id=1, source_target_pairs={{0,4},{12,8},{1,5},{13,9},{2,6},{14,10},{3,7},{15,11},{16,20},{28,... | collective-permute-start | bytes 2359304 | tf_op jit(solution)/shard_map/ppermute | solution.py:107
  15.9 2.2 collective-permute-start.3
  19.1 2.1 constant_dynamic-slice_fusion.3
  21.5 9.7 %collective-permute-done.2.refs_2_.refs_10_ = bf16[256,1536]{1,0:T(8,128)(2,1)} collective-permute-done((bf16[256,1536]{1,0:T(8,128)(2,1)}, bf16[256,1536]{1,0:T(8,128)(2,1)}, u32[]{:S(2)}, u32[]{:S(2)}) %collective-permute-start.2) | collective-permute-done | bytes 786464 | tf_op jit(solution)/shard_map/ppermute | solution.py:107
  31.2 16.9 %collective-permute-done.3.refs_2_.refs_10_ = bf16[256,1536]{1,0:T(8,128)(2,1)} collective-permute-done((bf16[256,1536]{1,0:T(8,128)(2,1)}, bf16[256,1536]{1,0:T(8,128)(2,1)}, u32[]{:S(2)}, u32[]{:S(2)}) %collective-permute-start.3) | collective-permute-done | bytes 786464 | tf_op jit(solution)/shard_map/ppermute | solution.py:107
  48.1 4.2 %collective-permute-start.4 = (bf16[384,2176]{1,0:T(8,128)(2,1)S(1)}, bf16[384,2176]{1,0:T(8,128)(2,1)S(1)}, u32[]{:S(2)}, u32[]{:S(2)}) collective-permute-start(bf16[384,2176]{1,0:T(8,128)(2,1)S(1)} %get-tuple-element.115), channel_id=1, source_target_pairs={{0,4},{12,8},{1,5},{13,9},{2,6},{14,10},{3,7},{15,11},{16,20},{28,... | collective-permute-start | bytes 5013512 | tf_op jit(solution)/shard_map/ppermute | solution.py:107
  52.3 1.3 collective-permute-start.7
  55.1 32.9 %collective-permute-done.7.refs_3_ = bf16[256,3072]{1,0:T(8,128)(2,1)S(1)} collective-permute-done((bf16[256,3072]{1,0:T(8,128)(2,1)S(1)}, bf16[256,3072]{1,0:T(8,128)(2,1)S(1)}, u32[]{:S(2)}, u32[]{:S(2)}) %collective-permute-start.7) | collective-permute-done | bytes 1572896 | tf_op jit(solution)/shard_map/ppermute | solution.py:107
  89.1 6.6 %collective-permute-start.8 = (bf16[384,2176]{1,0:T(8,128)(2,1)S(1)}, bf16[384,2176]{1,0:T(8,128)(2,1)S(1)}, u32[]{:S(2)}, u32[]{:S(2)}) collective-permute-start(bf16[384,2176]{1,0:T(8,128)(2,1)S(1)} %get-tuple-element.121), channel_id=1, source_target_pairs={{0,4},{12,8},{1,5},{13,9},{2,6},{14,10},{3,7},{15,11},{16,20},{28,... | collective-permute-start | bytes 5013512 | tf_op jit(solution)/shard_map/ppermute | solution.py:107
  95.7 1.3 collective-permute-start.11
  97.7 1.3 collective-permute-start.10
  99.0 33.0 %collective-permute-done.10.refs_5_ = bf16[256,3072]{1,0:T(8,128)(2,1)S(1)} collective-permute-done((bf16[256,3072]{1,0:T(8,128)(2,1)}, bf16[256,3072]{1,0:T(8,128)(2,1)S(1)}, u32[]{:S(2)}, u32[]{:S(2)}) %collective-permute-start.10) | collective-permute-done | bytes 1572896 | tf_op jit(solution)/shard_map/ppermute | solution.py:107
  134.7 2.5 collective-permute-start.12
  137.1 1.3 collective-permute-start.15
  139.9 24.9 %collective-permute-done.12.refs_4_ = bf16[256,3072]{1,0:T(8,128)(2,1)} collective-permute-done((bf16[256,3072]{1,0:T(8,128)(2,1)S(1)}, bf16[256,3072]{1,0:T(8,128)(2,1)}, u32[]{:S(2)}, u32[]{:S(2)}) %collective-permute-start.12) | collective-permute-done | bytes 1572896 | tf_op jit(solution)/shard_map/ppermute | solution.py:107
  164.8 5.0 %collective-permute-done.15.refs_5_ = bf16[256,3072]{1,0:T(8,128)(2,1)S(1)} collective-permute-done((bf16[256,3072]{1,0:T(8,128)(2,1)S(1)}, bf16[256,3072]{1,0:T(8,128)(2,1)S(1)}, u32[]{:S(2)}, u32[]{:S(2)}) %collective-permute-start.15) | collective-permute-done | bytes 1572896 | tf_op jit(solution)/shard_map/ppermute | solution.py:107
  169.8 6.6 %collective-permute-start.18 = (bf16[256,3072]{1,0:T(8,128)(2,1)S(1)}, bf16[256,3072]{1,0:T(8,128)(2,1)}, u32[]{:S(2)}, u32[]{:S(2)}) collective-permute-start(bf16[256,3072]{1,0:T(8,128)(2,1)S(1)} %get-tuple-element.205.refs_1_), channel_id=1, source_target_pairs={{0,4},{12,8},{1,5},{13,9},{2,6},{14,10},{3,7},{15,11},{16,20},{28,... | collective-permute-start | bytes 4718600 | tf_op jit(solution)/shard_map/ppermute | solution.py:107
  176.4 1.9 collective-permute-start.17
  178.9 25.8 %shard_map.37 = (f32[1024,2176]{1,0:T(8,128)}, bf16[1024,2176]{1,0:T(8,128)(2,1)}, f32[1024,2176]{1,0:T(8,128)}, bf16[1024,2176]{1,0:T(8,128)(2,1)}) custom-call(s32[3]{0:T(128)} %pad_add_fusion.sp_ref, bf16[256,1536]{1,0:T(8,128)(2,1)} %get-tuple-element.136.refs_0_.refs_8_, bf16[256,1536]{1,0:T(8,128)(2,1)} %copy-done.11, ...), custom_call_target="tpu_custom_call" | custom-call | flops 10000000000 | bytes 1000000 | tf_op jit(solution)/shard_map/pallas_call | solution.py:257
  204.7 1.7 dynamic-slice_bitcast_fusion.7
  206.4 1.6 pad_maximum_fusion
  208.0 6.6 %collective-permute-start.20 = (bf16[2,256,2176]{2,1,0:T(8,128)(2,1)}, bf16[2,256,2176]{2,1,0:T(8,128)(2,1)S(1)}, u32[]{:S(2)}, u32[]{:S(2)}) collective-permute-start(bf16[2,256,2176]{2,1,0:T(8,128)(2,1)} %pad_maximum_fusion), channel_id=1, source_target_pairs={{0,1},{1,0},{2,3},{3,2},{4,5},{5,4},{6,7},{7,6},{8,9},{9,8},{10,11... | collective-permute-start | bytes 6684680 | tf_op jit(solution)/shard_map/ppermute | solution.py:137
  214.6 1.9 collective-permute-start.22
  216.5 1.5 collective-permute-start.19
  218.8 1.3 copy-done.12
  220.1 4.4 %fusion.6 = (bf16[256,2176]{1,0:T(8,128)(2,1)}, f32[256,2176]{1,0:T(8,128)S(1)}) fusion(f32[1024,2176]{1,0:T(8,128)} %get-tuple-element.152, s32[]{:T(128)S(6)} %select_n.448, bf16[2,256,2176]{2,1,0:T(8,128)(2,1)} %copy-done.12, s32[]{:T(128)S(6)} %select_n.449, s32[]{:T(128)S(6)} %select_n.447, s32[]{:T(128)S(6)} %select_n.445), kind=kLoop, calls=%fused_computation.17 | loop fusion | flops 2785280 | bytes 10027024 | tf_op jit(solution)/shard_map/convert_element_type | solution.py:311
  224.5 1.2 collective-permute-start.21
  225.7 25.6 %shard_map.38 = (f32[1024,2176]{1,0:T(8,128)}, bf16[1024,2176]{1,0:T(8,128)(2,1)}, f32[1024,2176]{1,0:T(8,128)}, bf16[1024,2176]{1,0:T(8,128)(2,1)}) custom-call(s32[3]{0:T(128)} %pad_add_fusion.sp_ref, bf16[256,1536]{1,0:T(8,128)(2,1)} %get-tuple-element.154.refs_0_.refs_8_, bf16[256,1536]{1,0:T(8,128)(2,1)} %copy-done.9, ...), custom_call_target="tpu_custom_call" | custom-call | flops 10000000000 | bytes 1000000 | tf_op jit(solution)/shard_map/pallas_call | solution.py:257
  251.3 4.8 %collective-permute-done.19.refs_7_ = bf16[256,3072]{1,0:T(8,128)(2,1)} collective-permute-done((bf16[256,3072]{1,0:T(8,128)(2,1)}, bf16[256,3072]{1,0:T(8,128)(2,1)}, u32[]{:S(2)}, u32[]{:S(2)}) %collective-permute-start.19) | collective-permute-done | bytes 1572896 | tf_op jit(solution)/shard_map/ppermute | solution.py:107
  257.3 1.5 copy-done.22
  260.0 1.5 collective-permute-start.25
  261.6 2.4 collective-permute-done.23
  264.0 1.3 fusion.5
  265.3 1.2 collective-permute-start.24
  266.5 24.3 %shard_map.39 = (f32[1024,2176]{1,0:T(8,128)}, bf16[1024,2176]{1,0:T(8,128)(2,1)}) custom-call(s32[3]{0:T(128)} %pad_add_fusion.sp_ref, f32[1024,2176]{1,0:T(8,128)} %get-tuple-element.179.refs_0_, bf16[256,3072]{1,0:T(8,128)(2,1)} %copy-done.5, bf16[256,3072]{1,0:T(8,128)(2,1)} %collective-permute-done.refs_2_, ...), custom_call_target="tpu_custom_call" | custom-call | flops 10000000000 | bytes 1000000 | tf_op jit(solution)/shard_map/pallas_call | solution.py:257
  290.8 1.7 dynamic-slice_bitcast_fusion.3
  292.8 5.6 %collective-permute-done.25.refs_7_ = bf16[256,3072]{1,0:T(8,128)(2,1)S(1)} collective-permute-done((bf16[256,3072]{1,0:T(8,128)(2,1)}, bf16[256,3072]{1,0:T(8,128)(2,1)S(1)}, u32[]{:S(2)}, u32[]{:S(2)}) %collective-permute-start.25) | collective-permute-done | bytes 1572896 | tf_op jit(solution)/shard_map/ppermute | solution.py:107
  298.4 3.0 add_convert_fusion.1
  302.2 1.5 collective-permute-start.28
  303.7 2.5 collective-permute-done.26
  306.2 1.3 convert_add_fusion.3
  307.5 1.2 collective-permute-start.27
  308.7 24.1 %shard_map.40 = (f32[1024,2176]{1,0:T(8,128)}, bf16[1024,2176]{1,0:T(8,128)(2,1)}) custom-call(s32[3]{0:T(128)} %pad_add_fusion.sp_ref, f32[1024,2176]{1,0:T(8,128)} %get-tuple-element.204.refs_0_, bf16[256,3072]{1,0:T(8,128)(2,1)} %copy-done.4, bf16[256,3072]{1,0:T(8,128)(2,1)} %copy-done.18, bf16[256,3072]{1,0:T(8,128)(2,1)} %copy-done.17, ...), custom_call_target="tpu_custom_call" | custom-call | flops 10000000000 | bytes 1000000 | tf_op jit(solution)/shard_map/pallas_call | solution.py:257
  332.7 1.7 dynamic-slice_bitcast_fusion.1
  335.7 1.9 add_convert_fusion
  338.4 1.3 collective-permute-start.31
  339.6 2.7 collective-permute-done.29
  342.3 3.7 fusion
  346.3 1.8 collective-permute-start.32
  348.0 1.8 collective-permute-start.34
  349.8 1.5 collective-permute-done.32
  351.3 3.6 collective-permute-done.33
  354.9 16.1 %collective-permute-done.34 = bf16[256,128]{1,0:T(8,128)(2,1)S(1)} collective-permute-done((bf16[256,128]{1,0:T(8,128)(2,1)S(1)}, bf16[256,128]{1,0:T(8,128)(2,1)S(1)}, u32[]{:S(2)}, u32[]{:S(2)}) %collective-permute-start.34) | collective-permute-done | bytes 65568 | tf_op jit(solution)/shard_map/ppermute | solution.py:146
  372.1 2.5 fusion.3
  374.6 1.8 collective-permute-start.36
  376.4 1.8 collective-permute-start.38
  379.6 2.3 collective-permute-done.37
  382.0 1.9 collective-permute-start.39
  385.3 11.9 %shard_map.41 = bf16[512,2048]{1,0:T(8,128)(2,1)} custom-call(s32[1]{0:T(128)} %bitcast.where_ref, bf16[512,2048]{1,0:T(8,128)(2,1)S(1)} %pad_maximum_fusion.4.q_ref, bf16[1024,512]{1,0:T(8,128)(2,1)S(1)} %pad_maximum_fusion.7.kv_ref), custom_call_target="tpu_custom_call" | custom-call | flops 6000000000 | bytes 5000000 | tf_op jit(solution)/shard_map/pallas_call | solution.py:83
  (105 shorter events, 19.7 us)
Async XLA Ops:
  2.1 6.7 %copy-start.5 = (bf16[256,3072]{1,0:T(8,128)(2,1)}, bf16[256,3072]{1,0:T(8,128)(2,1)S(1)}, u32[]{:S(2)}) copy-start(bf16[256,3072]{1,0:T(8,128)(2,1)S(1)} %get-tuple-element.180.refs_1_) | copy-start | bytes 4718596
  2.1 167.7 %copy-start.4 = (bf16[256,3072]{1,0:T(8,128)(2,1)}, bf16[256,3072]{1,0:T(8,128)(2,1)S(1)}, u32[]{:S(2)}) copy-start(bf16[256,3072]{1,0:T(8,128)(2,1)S(1)} %get-tuple-element.205.refs_1_) | copy-start | bytes 4718596
  2.1 46.0 %collective-permute-start = (bf16[256,3072]{1,0:T(8,128)(2,1)S(1)}, bf16[256,3072]{1,0:T(8,128)(2,1)}, u32[]{:S(2)}, u32[]{:S(2)}) collective-permute-start(bf16[256,3072]{1,0:T(8,128)(2,1)S(1)} %get-tuple-element.180.refs_1_), channel_id=1, source_target_pairs={{4,8},{8,4},{5,9},{9,5},{6,10},{10,6},{7,11},{11,7},{20,24},{24,20... | collective-permute-start | bytes 4718600 | tf_op jit(solution)/shard_map/ppermute | solution.py:107
  4.2 43.9 %collective-permute-start.1 = (bf16[256,3072]{1,0:T(8,128)(2,1)S(1)}, bf16[256,3072]{1,0:T(8,128)(2,1)}, u32[]{:S(2)}, u32[]{:S(2)}) collective-permute-start(bf16[256,3072]{1,0:T(8,128)(2,1)S(1)} %get-tuple-element.180.refs_1_), channel_id=1, source_target_pairs={{4,0},{8,12},{5,1},{9,13},{6,2},{10,14},{7,3},{11,15},{20,16},{24,... | collective-permute-start | bytes 4718600 | tf_op jit(solution)/shard_map/ppermute | solution.py:107
  8.8 22.4 %collective-permute-start.2 = (bf16[256,1536]{1,0:T(8,128)(2,1)}, bf16[256,1536]{1,0:T(8,128)(2,1)}, u32[]{:S(2)}, u32[]{:S(2)}) collective-permute-start(bf16[256,1536]{1,0:T(8,128)(2,1)} %get-tuple-element.128), channel_id=1, source_target_pairs={{0,4},{12,8},{1,5},{13,9},{2,6},{14,10},{3,7},{15,11},{16,20},{28,... | collective-permute-start | bytes 2359304 | tf_op jit(solution)/shard_map/ppermute | solution.py:107
  15.9 32.1 %collective-permute-start.3 = (bf16[256,1536]{1,0:T(8,128)(2,1)}, bf16[256,1536]{1,0:T(8,128)(2,1)}, u32[]{:S(2)}, u32[]{:S(2)}) collective-permute-start(bf16[256,1536]{1,0:T(8,128)(2,1)} %get-tuple-element.129), channel_id=1, source_target_pairs={{0,4},{12,8},{1,5},{13,9},{2,6},{14,10},{3,7},{15,11},{16,20},{28,... | collective-permute-start | bytes 2359304 | tf_op jit(solution)/shard_map/ppermute | solution.py:107
  21.2 113.5 %copy-start.6 = (bf16[256,3072]{1,0:T(8,128)(2,1)S(1)}, bf16[256,3072]{1,0:T(8,128)(2,1)}, u32[]{:S(2)}) copy-start(bf16[256,3072]{1,0:T(8,128)(2,1)} %copy-done.5) | copy-start | bytes 4718596
  48.1 39.9 %collective-permute-start.4 = (bf16[384,2176]{1,0:T(8,128)(2,1)S(1)}, bf16[384,2176]{1,0:T(8,128)(2,1)S(1)}, u32[]{:S(2)}, u32[]{:S(2)}) collective-permute-start(bf16[384,2176]{1,0:T(8,128)(2,1)S(1)} %get-tuple-element.115), channel_id=1, source_target_pairs={{0,4},{12,8},{1,5},{13,9},{2,6},{14,10},{3,7},{15,11},{16,20},{28,... | collective-permute-start | bytes 5013512 | tf_op jit(solution)/shard_map/ppermute | solution.py:107
  52.3 35.6 %collective-permute-start.7 = (bf16[256,3072]{1,0:T(8,128)(2,1)S(1)}, bf16[256,3072]{1,0:T(8,128)(2,1)S(1)}, u32[]{:S(2)}, u32[]{:S(2)}) collective-permute-start(bf16[256,3072]{1,0:T(8,128)(2,1)S(1)} %get-tuple-element.205.refs_1_), channel_id=1, source_target_pairs={{4,0},{8,12},{5,1},{9,13},{6,2},{10,14},{7,3},{11,15},{20,16},{24,... | collective-permute-start | bytes 4718600 | tf_op jit(solution)/shard_map/ppermute | solution.py:107
  53.6 1.4 collective-permute-start.5
  54.3 0.7 collective-permute-start.6
  55.0 32.9 %copy-start.10 = (bf16[256,1536]{1,0:T(8,128)(2,1)}, bf16[256,1536]{1,0:T(8,128)(2,1)S(1)}, u32[]{:S(2)}) copy-start(bf16[256,1536]{1,0:T(8,128)(2,1)S(1)} %collective-permute-done.5.refs_3_.refs_11_) | copy-start | bytes 2359300
  55.0 32.9 %copy-start.8 = (bf16[256,1536]{1,0:T(8,128)(2,1)}, bf16[256,1536]{1,0:T(8,128)(2,1)S(1)}, u32[]{:S(2)}) copy-start(bf16[256,1536]{1,0:T(8,128)(2,1)S(1)} %collective-permute-done.6.refs_3_.refs_11_) | copy-start | bytes 2359300
  87.9 1.2 copy-start.17
  89.1 89.8 %copy-start = (bf16[384,2176]{1,0:T(8,128)(2,1)}, bf16[384,2176]{1,0:T(8,128)(2,1)S(1)}, u32[]{:S(2)}) copy-start(bf16[384,2176]{1,0:T(8,128)(2,1)S(1)} %collective-permute-done.4.refs_12_) | copy-start | bytes 5013508
  89.1 43.0 %collective-permute-start.8 = (bf16[384,2176]{1,0:T(8,128)(2,1)S(1)}, bf16[384,2176]{1,0:T(8,128)(2,1)S(1)}, u32[]{:S(2)}, u32[]{:S(2)}) collective-permute-start(bf16[384,2176]{1,0:T(8,128)(2,1)S(1)} %get-tuple-element.121), channel_id=1, source_target_pairs={{0,4},{12,8},{1,5},{13,9},{2,6},{14,10},{3,7},{15,11},{16,20},{28,... | collective-permute-start | bytes 5013512 | tf_op jit(solution)/shard_map/ppermute | solution.py:107
  95.7 37.6 %collective-permute-start.11 = (bf16[384,2176]{1,0:T(8,128)(2,1)S(1)}, bf16[384,2176]{1,0:T(8,128)(2,1)S(1)}, u32[]{:S(2)}, u32[]{:S(2)}) collective-permute-start(bf16[384,2176]{1,0:T(8,128)(2,1)S(1)} %collective-permute-done.4.refs_12_), channel_id=1, source_target_pairs={{0,16},{16,0},{1,17},{17,1},{2,18},{18,2},{3,19},{19,3},{4,20},{20... | collective-permute-start | bytes 5013512 | tf_op jit(solution)/shard_map/ppermute | solution.py:107
  97.0 2.1 collective-permute-start.9
  97.7 34.4 %collective-permute-start.10 = (bf16[256,3072]{1,0:T(8,128)(2,1)}, bf16[256,3072]{1,0:T(8,128)(2,1)S(1)}, u32[]{:S(2)}, u32[]{:S(2)}) collective-permute-start(bf16[256,3072]{1,0:T(8,128)(2,1)} %collective-permute-done.refs_2_), channel_id=1, source_target_pairs={{4,0},{8,12},{5,1},{9,13},{6,2},{10,14},{7,3},{11,15},{20,16},{24,... | collective-permute-start | bytes 4718600 | tf_op jit(solution)/shard_map/ppermute | solution.py:107
  99.0 77.4 %copy-start.18 = (bf16[256,3072]{1,0:T(8,128)(2,1)}, bf16[256,3072]{1,0:T(8,128)(2,1)S(1)}, u32[]{:S(2)}) copy-start(bf16[256,3072]{1,0:T(8,128)(2,1)S(1)} %collective-permute-done.9.refs_2_) | copy-start | bytes 4718596
  132.1 1.1 copy-start.20
  133.2 1.2 copy-start.1
  134.4 35.4 %copy-start.2 = (bf16[384,2176]{1,0:T(8,128)(2,1)}, bf16[384,2176]{1,0:T(8,128)(2,1)S(1)}, u32[]{:S(2)}) copy-start(bf16[384,2176]{1,0:T(8,128)(2,1)S(1)} %collective-permute-done.11.refs_14_) | copy-start | bytes 5013508
  134.4 35.4 %collective-permute-start.16 = (bf16[384,2176]{1,0:T(8,128)(2,1)S(1)}, bf16[384,2176]{1,0:T(8,128)(2,1)S(1)}, u32[]{:S(2)}, u32[]{:S(2)}) collective-permute-start(bf16[384,2176]{1,0:T(8,128)(2,1)S(1)} %collective-permute-done.8.refs_13_), channel_id=1, source_target_pairs={{0,16},{16,0},{1,17},{17,1},{2,18},{18,2},{3,19},{19,3},{4,20},{20... | collective-permute-start | bytes 5013512 | tf_op jit(solution)/shard_map/ppermute | solution.py:107
  134.7 30.1 %collective-permute-start.12 = (bf16[256,3072]{1,0:T(8,128)(2,1)S(1)}, bf16[256,3072]{1,0:T(8,128)(2,1)}, u32[]{:S(2)}, u32[]{:S(2)}) collective-permute-start(bf16[256,3072]{1,0:T(8,128)(2,1)S(1)} %copy-done.6), channel_id=1, source_target_pairs={{0,4},{12,8},{1,5},{13,9},{2,6},{14,10},{3,7},{15,11},{16,20},{28,... | collective-permute-start | bytes 4718600 | tf_op jit(solution)/shard_map/ppermute | solution.py:107
  137.1 32.7 %collective-permute-start.15 = (bf16[256,3072]{1,0:T(8,128)(2,1)S(1)}, bf16[256,3072]{1,0:T(8,128)(2,1)S(1)}, u32[]{:S(2)}, u32[]{:S(2)}) collective-permute-start(bf16[256,3072]{1,0:T(8,128)(2,1)S(1)} %collective-permute-done.9.refs_2_), channel_id=1, source_target_pairs={{4,0},{8,12},{5,1},{9,13},{6,2},{10,14},{7,3},{11,15},{20,16},{24,... | collective-permute-start | bytes 4718600 | tf_op jit(solution)/shard_map/ppermute | solution.py:107
  138.4 1.4 collective-permute-start.14
  139.1 0.7 collective-permute-start.13
  139.9 36.5 %copy-start.9 = (bf16[256,1536]{1,0:T(8,128)(2,1)}, bf16[256,1536]{1,0:T(8,128)(2,1)S(1)}, u32[]{:S(2)}) copy-start(bf16[256,1536]{1,0:T(8,128)(2,1)S(1)} %collective-permute-done.14.refs_1_.refs_9_) | copy-start | bytes 2359300
  139.9 36.5 %copy-start.11 = (bf16[256,1536]{1,0:T(8,128)(2,1)}, bf16[256,1536]{1,0:T(8,128)(2,1)S(1)}, u32[]{:S(2)}) copy-start(bf16[256,1536]{1,0:T(8,128)(2,1)S(1)} %collective-permute-done.13.refs_1_.refs_9_) | copy-start | bytes 2359300
  169.8 6.6 %copy-start.19 = (bf16[256,3072]{1,0:T(8,128)(2,1)}, bf16[256,3072]{1,0:T(8,128)(2,1)S(1)}, u32[]{:S(2)}) copy-start(bf16[256,3072]{1,0:T(8,128)(2,1)S(1)} %collective-permute-done.15.refs_5_) | copy-start | bytes 4718596
  169.8 6.6 %copy-start.3 = (bf16[384,2176]{1,0:T(8,128)(2,1)}, bf16[384,2176]{1,0:T(8,128)(2,1)S(1)}, u32[]{:S(2)}) copy-start(bf16[384,2176]{1,0:T(8,128)(2,1)S(1)} %collective-permute-done.16.refs_15_) | copy-start | bytes 5013508
  169.8 34.8 %collective-permute-start.18 = (bf16[256,3072]{1,0:T(8,128)(2,1)S(1)}, bf16[256,3072]{1,0:T(8,128)(2,1)}, u32[]{:S(2)}, u32[]{:S(2)}) collective-permute-start(bf16[256,3072]{1,0:T(8,128)(2,1)S(1)} %get-tuple-element.205.refs_1_), channel_id=1, source_target_pairs={{0,4},{12,8},{1,5},{13,9},{2,6},{14,10},{3,7},{15,11},{16,20},{28,... | collective-permute-start | bytes 4718600 | tf_op jit(solution)/shard_map/ppermute | solution.py:107
  176.4 28.3 %collective-permute-start.17 = (bf16[256,3072]{1,0:T(8,128)(2,1)}, bf16[256,3072]{1,0:T(8,128)(2,1)}, u32[]{:S(2)}, u32[]{:S(2)}) collective-permute-start(bf16[256,3072]{1,0:T(8,128)(2,1)} %collective-permute-done.12.refs_4_), channel_id=1, source_target_pairs={{4,8},{8,4},{5,9},{9,5},{6,10},{10,6},{7,11},{11,7},{20,24},{24,20... | collective-permute-start | bytes 4718600 | tf_op jit(solution)/shard_map/ppermute | solution.py:107
  208.0 10.8 %collective-permute-start.20 = (bf16[2,256,2176]{2,1,0:T(8,128)(2,1)}, bf16[2,256,2176]{2,1,0:T(8,128)(2,1)S(1)}, u32[]{:S(2)}, u32[]{:S(2)}) collective-permute-start(bf16[2,256,2176]{2,1,0:T(8,128)(2,1)} %pad_maximum_fusion), channel_id=1, source_target_pairs={{0,1},{1,0},{2,3},{3,2},{4,5},{5,4},{6,7},{7,6},{8,9},{9,8},{10,11... | collective-permute-start | bytes 6684680 | tf_op jit(solution)/shard_map/ppermute | solution.py:137
  214.6 36.7 %collective-permute-start.22 = (bf16[256,3072]{1,0:T(8,128)(2,1)}, bf16[256,3072]{1,0:T(8,128)(2,1)}, u32[]{:S(2)}, u32[]{:S(2)}) collective-permute-start(bf16[256,3072]{1,0:T(8,128)(2,1)} %collective-permute-done.18.refs_4_), channel_id=1, source_target_pairs={{4,8},{8,4},{5,9},{9,5},{6,10},{10,6},{7,11},{11,7},{20,24},{24,20... | collective-permute-start | bytes 4718600 | tf_op jit(solution)/shard_map/ppermute | solution.py:107
  216.5 39.6 %collective-permute-start.19 = (bf16[256,3072]{1,0:T(8,128)(2,1)}, bf16[256,3072]{1,0:T(8,128)(2,1)}, u32[]{:S(2)}, u32[]{:S(2)}) collective-permute-start(bf16[256,3072]{1,0:T(8,128)(2,1)} %collective-permute-done.17.refs_6_), channel_id=1, source_target_pairs={{4,0},{8,12},{5,1},{9,13},{6,2},{10,14},{7,3},{11,15},{20,16},{24,... | collective-permute-start | bytes 4718600 | tf_op jit(solution)/shard_map/ppermute | solution.py:107
  218.8 1.3 copy-start.12
  224.5 31.6 %collective-permute-start.21 = (bf16[256,2176]{1,0:T(8,128)(2,1)}, bf16[256,2176]{1,0:T(8,128)(2,1)S(1)}, u32[]{:S(2)}, u32[]{:S(2)}) collective-permute-start(bf16[256,2176]{1,0:T(8,128)(2,1)} %get-tuple-element.164), channel_id=1, source_target_pairs={{0,2},{1,3},{2,0},{3,1},{4,6},{5,7},{6,4},{7,5},{8,10},{9,11},{10,... | collective-permute-start | bytes 3342344 | tf_op jit(solution)/shard_map/ppermute | solution.py:141
  256.1 2.7 copy-start.22
  258.8 5.2 %copy-start.15 = (f32[1024,2176]{1,0:T(8,128)S(1)}, f32[1024,2176]{1,0:T(8,128)}, u32[]{:S(2)}) copy-start(f32[1024,2176]{1,0:T(8,128)} %get-tuple-element.171) | copy-start | bytes 26738692
  259.2 4.8 %collective-permute-start.23 = (bf16[2,256,2176]{2,1,0:T(8,128)(2,1)S(1)}, bf16[2,256,2176]{2,1,0:T(8,128)(2,1)S(1)}, u32[]{:S(2)}, u32[]{:S(2)}) collective-permute-start(bf16[2,256,2176]{2,1,0:T(8,128)(2,1)S(1)} %pad_maximum_fusion.1), channel_id=1, source_target_pairs={{0,1},{1,0},{2,3},{3,2},{4,5},{5,4},{6,7},{7,6},{8,9},{9,8},{10,11... | collective-permute-start | bytes 6684680 | tf_op jit(solution)/shard_map/ppermute | solution.py:137
  260.0 38.4 %collective-permute-start.25 = (bf16[256,3072]{1,0:T(8,128)(2,1)}, bf16[256,3072]{1,0:T(8,128)(2,1)S(1)}, u32[]{:S(2)}, u32[]{:S(2)}) collective-permute-start(bf16[256,3072]{1,0:T(8,128)(2,1)} %collective-permute-done.22.refs_6_), channel_id=1, source_target_pairs={{4,0},{8,12},{5,1},{9,13},{6,2},{10,14},{7,3},{11,15},{20,16},{24,... | collective-permute-start | bytes 4718600 | tf_op jit(solution)/shard_map/ppermute | solution.py:107
  265.3 33.1 %collective-permute-start.24 = (bf16[256,2176]{1,0:T(8,128)(2,1)}, bf16[256,2176]{1,0:T(8,128)(2,1)}, u32[]{:S(2)}, u32[]{:S(2)}) collective-permute-start(bf16[256,2176]{1,0:T(8,128)(2,1)} %get-tuple-element.189), channel_id=1, source_target_pairs={{0,2},{1,3},{2,0},{3,1},{4,6},{5,7},{6,4},{7,5},{8,10},{9,11},{10,... | collective-permute-start | bytes 3342344 | tf_op jit(solution)/shard_map/ppermute | solution.py:141
  292.5 13.6 %copy-start.16 = (f32[1024,2176]{1,0:T(8,128)S(1)}, f32[1024,2176]{1,0:T(8,128)}, u32[]{:S(2)}) copy-start(f32[1024,2176]{1,0:T(8,128)} %get-tuple-element.194) | copy-start | bytes 26738692
  298.4 3.0 copy-start.21
  301.4 4.8 %collective-permute-start.26 = (bf16[2,256,2176]{2,1,0:T(8,128)(2,1)S(1)}, bf16[2,256,2176]{2,1,0:T(8,128)(2,1)S(1)}, u32[]{:S(2)}, u32[]{:S(2)}) collective-permute-start(bf16[2,256,2176]{2,1,0:T(8,128)(2,1)S(1)} %pad_maximum_fusion.2), channel_id=1, source_target_pairs={{0,1},{1,0},{2,3},{3,2},{4,5},{5,4},{6,7},{7,6},{8,9},{9,8},{10,11... | collective-permute-start | bytes 6684680 | tf_op jit(solution)/shard_map/ppermute | solution.py:137
  302.2 32.5 %collective-permute-start.28 = (bf16[256,2176]{1,0:T(8,128)(2,1)}, bf16[256,2176]{1,0:T(8,128)(2,1)S(1)}, u32[]{:S(2)}, u32[]{:S(2)}) collective-permute-start(bf16[256,2176]{1,0:T(8,128)(2,1)} %add_convert_fusion.2), channel_id=1, source_target_pairs={{4,0},{8,12},{5,1},{9,13},{6,2},{10,14},{7,3},{11,15},{20,16},{24,... | collective-permute-start | bytes 3342344 | tf_op jit(solution)/shard_map/ppermute | solution.py:107
  307.5 27.3 %collective-permute-start.27 = (bf16[256,2176]{1,0:T(8,128)(2,1)}, bf16[256,2176]{1,0:T(8,128)(2,1)}, u32[]{:S(2)}, u32[]{:S(2)}) collective-permute-start(bf16[256,2176]{1,0:T(8,128)(2,1)} %get-tuple-element.196), channel_id=1, source_target_pairs={{0,2},{1,3},{2,0},{3,1},{4,6},{5,7},{6,4},{7,5},{8,10},{9,11},{10,... | collective-permute-start | bytes 3342344 | tf_op jit(solution)/shard_map/ppermute | solution.py:141
  337.6 33.3 %copy-start.7 = (bf16[256,2176]{1,0:T(8,128)(2,1)}, bf16[256,2176]{1,0:T(8,128)(2,1)S(1)}, u32[]{:S(2)}) copy-start(bf16[256,2176]{1,0:T(8,128)(2,1)S(1)} %add_convert_fusion) | copy-start | bytes 3342340
  337.6 4.7 %collective-permute-start.29 = (bf16[2,256,2176]{2,1,0:T(8,128)(2,1)S(1)}, bf16[2,256,2176]{2,1,0:T(8,128)(2,1)S(1)}, u32[]{:S(2)}, u32[]{:S(2)}) collective-permute-start(bf16[2,256,2176]{2,1,0:T(8,128)(2,1)S(1)} %pad_maximum_fusion.3), channel_id=1, source_target_pairs={{0,1},{1,0},{2,3},{3,2},{4,5},{5,4},{6,7},{7,6},{8,9},{9,8},{10,11... | collective-permute-start | bytes 6684680 | tf_op jit(solution)/shard_map/ppermute | solution.py:137
  338.4 33.4 %collective-permute-start.31 = (bf16[256,2176]{1,0:T(8,128)(2,1)}, bf16[256,2176]{1,0:T(8,128)(2,1)S(1)}, u32[]{:S(2)}, u32[]{:S(2)}) collective-permute-start(bf16[256,2176]{1,0:T(8,128)(2,1)} %add_convert_fusion.1), channel_id=1, source_target_pairs={{4,0},{8,12},{5,1},{9,13},{6,2},{10,14},{7,3},{11,15},{20,16},{24,... | collective-permute-start | bytes 3342344 | tf_op jit(solution)/shard_map/ppermute | solution.py:107
  342.3 3.7 copy-start.13
  346.0 26.1 %collective-permute-start.30 = (bf16[256,2176]{1,0:T(8,128)(2,1)}, bf16[256,2176]{1,0:T(8,128)(2,1)}, u32[]{:S(2)}, u32[]{:S(2)}) collective-permute-start(bf16[256,2176]{1,0:T(8,128)(2,1)} %fusion), channel_id=1, source_target_pairs={{0,2},{1,3},{2,0},{3,1},{4,6},{5,7},{6,4},{7,5},{8,10},{9,11},{10,... | collective-permute-start | bytes 3342344 | tf_op jit(solution)/shard_map/ppermute | solution.py:141
  346.3 5.0 %collective-permute-start.32 = (bf16[256,128]{1,0:T(8,128)(2,1)S(1)}, bf16[256,128]{1,0:T(8,128)(2,1)S(1)}, u32[]{:S(2)}, u32[]{:S(2)}) collective-permute-start(bf16[256,128]{1,0:T(8,128)(2,1)S(1)} %slice.66), channel_id=1, source_target_pairs={{0,12},{4,8},{8,4},{12,0},{1,13},{5,9},{9,5},{13,1},{2,14},{6,10},... | collective-permute-start | bytes 196616 | tf_op jit(solution)/shard_map/ppermute | solution.py:146
  348.0 6.9 %collective-permute-start.33 = (bf16[256,128]{1,0:T(8,128)(2,1)S(1)}, bf16[256,128]{1,0:T(8,128)(2,1)S(1)}, u32[]{:S(2)}, u32[]{:S(2)}) collective-permute-start(bf16[256,128]{1,0:T(8,128)(2,1)S(1)} %slice.66), channel_id=1, source_target_pairs={{0,8},{4,12},{8,0},{12,4},{1,9},{5,13},{9,1},{13,5},{2,10},{6,14},... | collective-permute-start | bytes 196616 | tf_op jit(solution)/shard_map/ppermute | solution.py:146
  348.0 22.9 %collective-permute-start.34 = (bf16[256,128]{1,0:T(8,128)(2,1)S(1)}, bf16[256,128]{1,0:T(8,128)(2,1)S(1)}, u32[]{:S(2)}, u32[]{:S(2)}) collective-permute-start(bf16[256,128]{1,0:T(8,128)(2,1)S(1)} %slice.66), channel_id=1, source_target_pairs={{0,4},{4,0},{8,12},{12,8},{1,5},{5,1},{9,13},{13,9},{2,6},{6,2},{1... | collective-permute-start | bytes 196616 | tf_op jit(solution)/shard_map/ppermute | solution.py:146
  349.8 22.3 %copy-start.14 = (bf16[2,256,2176]{2,1,0:T(8,128)(2,1)S(1)}, bf16[2,256,2176]{2,1,0:T(8,128)(2,1)}, u32[]{:S(2)}) copy-start(bf16[2,256,2176]{2,1,0:T(8,128)(2,1)} %copy-done.13) | copy-start | bytes 6684676
  371.0 7.2 %collective-permute-start.35 = (bf16[256,512]{1,0:T(8,128)(2,1)S(1)}, bf16[256,512]{1,0:T(8,128)(2,1)S(1)}, u32[]{:S(2)}, u32[]{:S(2)}) collective-permute-start(bf16[256,512]{1,0:T(8,128)(2,1)S(1)} %pad_maximum_fusion.10), channel_id=1, source_target_pairs={{0,1},{1,0},{2,3},{3,2},{4,5},{5,4},{6,7},{7,6},{8,9},{9,8},{10,11... | collective-permute-start | bytes 786440 | tf_op jit(solution)/shard_map/ppermute | solution.py:137
  374.6 9.3 %slice-start = ((bf16[256,2176]{1,0:T(8,128)(2,1)}), bf16[256,2048]{1,0:T(8,128)(2,1)S(1)}, s32[]{:S(2)}) async-start(bf16[256,2176]{1,0:T(8,128)(2,1)} %copy-done.7), calls=%async_computation | async-start | bytes 2097152 | tf_op jit(solution)/shard_map/slice | solution.py:422
  374.6 5.0 %collective-permute-start.36 = (bf16[256,128]{1,0:T(8,128)(2,1)S(1)}, bf16[256,128]{1,0:T(8,128)(2,1)S(1)}, u32[]{:S(2)}, u32[]{:S(2)}) collective-permute-start(bf16[256,128]{1,0:T(8,128)(2,1)S(1)} %slice.67), channel_id=1, source_target_pairs={{0,12},{4,8},{8,4},{12,0},{1,13},{5,9},{9,5},{13,1},{2,14},{6,10},... | collective-permute-start | bytes 196616 | tf_op jit(solution)/shard_map/ppermute | solution.py:146
  376.4 5.5 %collective-permute-start.37 = (bf16[256,128]{1,0:T(8,128)(2,1)S(1)}, bf16[256,128]{1,0:T(8,128)(2,1)S(1)}, u32[]{:S(2)}, u32[]{:S(2)}) collective-permute-start(bf16[256,128]{1,0:T(8,128)(2,1)S(1)} %slice.67), channel_id=1, source_target_pairs={{0,8},{4,12},{8,0},{12,4},{1,9},{5,13},{9,1},{13,5},{2,10},{6,14},... | collective-permute-start | bytes 196616 | tf_op jit(solution)/shard_map/ppermute | solution.py:146
  376.4 5.5 %collective-permute-start.38 = (bf16[256,128]{1,0:T(8,128)(2,1)S(1)}, bf16[256,128]{1,0:T(8,128)(2,1)S(1)}, u32[]{:S(2)}, u32[]{:S(2)}) collective-permute-start(bf16[256,128]{1,0:T(8,128)(2,1)S(1)} %slice.67), channel_id=1, source_target_pairs={{0,4},{4,0},{8,12},{12,8},{1,5},{5,1},{9,13},{13,9},{2,6},{6,2},{1... | collective-permute-start | bytes 196616 | tf_op jit(solution)/shard_map/ppermute | solution.py:146
  382.0 3.1 collective-permute-start.39
  (1 other events, 1.0 us)

commit v4 on v3

--- a/solution.py
+++ b/solution.py
@@ -288,7 +288,7 @@
     sp = jnp.stack([inner, own_at, far_at]).astype(jnp.int32)
     weights1 = ((0, first),)
     weights2 = (((1,), part), ((2,), part))
-    early_rows = rows // 2
+    early_rows = rows * 15 // 32
     spans = ((0, early_rows), (early_rows, rows - early_rows))
     share = part // 2
 

time: 398 us -> 396 us (level)
  waiting for transfers between devices: 167 us -> 161 us
    ppermute x24, waiting for transfers between devices: 133 us -> 125 us  [along(): return lambda x: lax.ppermute(x, axis, pairs)]
    unnamed x48 -> x42, local copies, waits for them, and re-layouts: 7.33 us -> 2.35 us
  transfers between devices with their start and end apart: 40 -> 40, of which waited for: 19 -> 22; matrix products, arithmetic and copies ran while one was open for 6% -> 7% of each run, Pallas kernels for 25% -> 25%
where the time goes in v4:
time: 396 us; the launch traced here: 395 us
  waiting for transfers between devices  161 us (41%)
  Pallas kernels  112 us (28%)
  starting transfers between devices  76.2 us (19%)
  other arithmetic  27.1 us (7%)
  local copies, waits for them, and re-layouts  18.1 us (5%)
    ppermute x24, waiting for transfers between devices, along(): return lambda x: lax.ppermute(x, axis, pairs)  125 us
    pallas_call x4, Pallas kernels, product(): pl.pallas_call(functools.partial(product_kernel, shape, sums, kinds, (til...  99.9 us
    ppermute x24, starting transfers between devices, along(): return lambda x: lax.ppermute(x, axis, pairs)  52.3 us
    ppermute x6, waiting for transfers between devices, gathered(): lax.ppermute(x, 'ffn', [(i, i ^ k) for i in range(4)])  25.1 us
    ppermute x6, starting transfers between devices, other_core(): return lax.ppermute(x, 'hid', [(i, i ^ 1) for i in range(4)])  12.8 us
    convert_element_type x3, other arithmetic, over_cores(): return (keep, give.astype(BF16))  12.4 us
    pallas_call x1, Pallas kernels, attention(): pl.pallas_call(functools.partial(attention_kernel, rows), out_shape=jax.S...  11.6 us
    ppermute x6, waiting for transfers between devices, other_core(): return lax.ppermute(x, 'hid', [(i, i ^ 1) for i in range(4)])  9.52 us
  transfers between devices with their start and end apart: 40, of which 22 were waited for; matrix products, arithmetic and copies ran while one was open for 7% of the time, Pallas kernels for 25%

profile of v4, /device:TPU:1, one launch (start us, length us, event | category | flops | bytes accessed | tf_op | source)
XLA Modules:
  0.0 394.8 jit_solution(9605738866332334657)
XLA Ops:
  0.0 1.5 slice.48.refs_1_
  1.5 1.8 collective-permute-start
  3.3 1.3 collective-permute-start.1
  5.8 1.2 broadcast_select_fusion.1
  7.0 7.5 %collective-permute-start.2 = (bf16[240,1536]{1,0:T(8,128)(2,1)}, bf16[240,1536]{1,0:T(8,128)(2,1)}, u32[]{:S(2)}, u32[]{:S(2)}) collective-permute-start(bf16[240,1536]{1,0:T(8,128)(2,1)} %get-tuple-element.128), channel_id=1, source_target_pairs={{0,4},{12,8},{1,5},{13,9},{2,6},{14,10},{3,7},{15,11},{16,20},{28,... | collective-permute-start | bytes 2211848 | tf_op jit(solution)/shard_map/ppermute | solution.py:107
  15.7 1.4 pad_maximum_fusion.8
  17.0 2.2 collective-permute-start.3
  19.2 1.5 slice.51.refs_1_
  22.0 2.1 constant_dynamic-slice_fusion.3
  24.4 4.3 %collective-permute-done.2.refs_2_.refs_10_ = bf16[240,1536]{1,0:T(8,128)(2,1)} collective-permute-done((bf16[240,1536]{1,0:T(8,128)(2,1)}, bf16[240,1536]{1,0:T(8,128)(2,1)}, u32[]{:S(2)}, u32[]{:S(2)}) %collective-permute-start.2) | collective-permute-done | bytes 737312 | tf_op jit(solution)/shard_map/ppermute | solution.py:107
  28.7 17.9 %collective-permute-done.3.refs_2_.refs_10_ = bf16[272,1536]{1,0:T(8,128)(2,1)} collective-permute-done((bf16[272,1536]{1,0:T(8,128)(2,1)}, bf16[272,1536]{1,0:T(8,128)(2,1)}, u32[]{:S(2)}, u32[]{:S(2)}) %collective-permute-start.3) | collective-permute-done | bytes 835616 | tf_op jit(solution)/shard_map/ppermute | solution.py:107
  46.6 4.2 %collective-permute-start.4 = (bf16[384,2176]{1,0:T(8,128)(2,1)S(1)}, bf16[384,2176]{1,0:T(8,128)(2,1)S(1)}, u32[]{:S(2)}, u32[]{:S(2)}) collective-permute-start(bf16[384,2176]{1,0:T(8,128)(2,1)S(1)} %get-tuple-element.115), channel_id=1, source_target_pairs={{0,4},{12,8},{1,5},{13,9},{2,6},{14,10},{3,7},{15,11},{16,20},{28,... | collective-permute-start | bytes 5013512 | tf_op jit(solution)/shard_map/ppermute | solution.py:107
  50.8 1.3 collective-permute-start.7
  53.6 31.0 %collective-permute-done.4.refs_12_ = bf16[384,2176]{1,0:T(8,128)(2,1)S(1)} collective-permute-done((bf16[384,2176]{1,0:T(8,128)(2,1)S(1)}, bf16[384,2176]{1,0:T(8,128)(2,1)S(1)}, u32[]{:S(2)}, u32[]{:S(2)}) %collective-permute-start.4) | collective-permute-done | bytes 1671200 | tf_op jit(solution)/shard_map/ppermute | solution.py:107
  84.7 3.9 collective-permute-done.7.refs_3_
  88.6 5.1 %collective-permute-start.8 = (bf16[384,2176]{1,0:T(8,128)(2,1)S(1)}, bf16[384,2176]{1,0:T(8,128)(2,1)S(1)}, u32[]{:S(2)}, u32[]{:S(2)}) collective-permute-start(bf16[384,2176]{1,0:T(8,128)(2,1)S(1)} %get-tuple-element.121), channel_id=1, source_target_pairs={{0,4},{12,8},{1,5},{13,9},{2,6},{14,10},{3,7},{15,11},{16,20},{28,... | collective-permute-start | bytes 5013512 | tf_op jit(solution)/shard_map/ppermute | solution.py:107
  94.5 1.3 collective-permute-start.11
  95.8 1.3 collective-permute-start.10
  97.1 31.0 %collective-permute-done.10.refs_5_ = bf16[240,3072]{1,0:T(8,128)(2,1)S(1)} collective-permute-done((bf16[240,3072]{1,0:T(8,128)(2,1)}, bf16[240,3072]{1,0:T(8,128)(2,1)S(1)}, u32[]{:S(2)}, u32[]{:S(2)}) %collective-permute-start.10) | collective-permute-done | bytes 1474592 | tf_op jit(solution)/shard_map/ppermute | solution.py:107
  129.2 1.2 collective-permute-start.16
  130.4 1.3 collective-permute-start.15
  131.7 5.2 %collective-permute-start.12 = (bf16[240,3072]{1,0:T(8,128)(2,1)S(1)}, bf16[240,3072]{1,0:T(8,128)(2,1)}, u32[]{:S(2)}, u32[]{:S(2)}) collective-permute-start(bf16[240,3072]{1,0:T(8,128)(2,1)S(1)} %copy-done.6), channel_id=1, source_target_pairs={{0,4},{12,8},{1,5},{13,9},{2,6},{14,10},{3,7},{15,11},{16,20},{28,... | collective-permute-start | bytes 4423688 | tf_op jit(solution)/shard_map/ppermute | solution.py:107
  138.4 23.1 %collective-permute-done.12.refs_4_ = bf16[240,3072]{1,0:T(8,128)(2,1)} collective-permute-done((bf16[240,3072]{1,0:T(8,128)(2,1)S(1)}, bf16[240,3072]{1,0:T(8,128)(2,1)}, u32[]{:S(2)}, u32[]{:S(2)}) %collective-permute-start.12) | collective-permute-done | bytes 1474592 | tf_op jit(solution)/shard_map/ppermute | solution.py:107
  161.5 2.7 collective-permute-done.16.refs_15_
  164.7 5.9 %collective-permute-start.18 = (bf16[272,3072]{1,0:T(8,128)(2,1)S(1)}, bf16[272,3072]{1,0:T(8,128)(2,1)}, u32[]{:S(2)}, u32[]{:S(2)}) collective-permute-start(bf16[272,3072]{1,0:T(8,128)(2,1)S(1)} %slice.51.refs_1_), channel_id=1, source_target_pairs={{0,4},{12,8},{1,5},{13,9},{2,6},{14,10},{3,7},{15,11},{16,20},{28,... | collective-permute-start | bytes 5013512 | tf_op jit(solution)/shard_map/ppermute | solution.py:107
  170.7 1.8 collective-permute-start.17
  173.1 24.5 %shard_map.37 = (f32[960,2176]{1,0:T(8,128)}, bf16[960,2176]{1,0:T(8,128)(2,1)}, f32[960,2176]{1,0:T(8,128)}, bf16[960,2176]{1,0:T(8,128)(2,1)}) custom-call(s32[3]{0:T(128)} %pad_add_fusion.sp_ref, bf16[240,1536]{1,0:T(8,128)(2,1)} %get-tuple-element.136.refs_0_.refs_8_, bf16[240,1536]{1,0:T(8,128)(2,1)} %copy-done.11, ...), custom_call_target="tpu_custom_call" | custom-call | flops 10000000000 | bytes 1000000 | tf_op jit(solution)/shard_map/pallas_call | solution.py:257
  198.4 1.7 dynamic-slice_bitcast_fusion.7
  200.1 1.5 pad_maximum_fusion.3
  201.6 7.7 %collective-permute-start.20 = (bf16[2,240,2176]{2,1,0:T(8,128)(2,1)}, bf16[2,240,2176]{2,1,0:T(8,128)(2,1)S(1)}, u32[]{:S(2)}, u32[]{:S(2)}) collective-permute-start(bf16[2,240,2176]{2,1,0:T(8,128)(2,1)} %pad_maximum_fusion.3), channel_id=1, source_target_pairs={{0,1},{1,0},{2,3},{3,2},{4,5},{5,4},{6,7},{7,6},{8,9},{9,8},{10,11... | collective-permute-start | bytes 6266888 | tf_op jit(solution)/shard_map/ppermute | solution.py:137
  209.3 1.9 collective-permute-start.22
  211.2 1.5 collective-permute-start.19
  213.3 1.3 copy-done.14
  214.6 4.1 %fusion.6 = (bf16[240,2176]{1,0:T(8,128)(2,1)}, f32[240,2176]{1,0:T(8,128)S(1)}) fusion(f32[960,2176]{1,0:T(8,128)} %get-tuple-element.152, s32[]{:T(128)S(6)} %select_n.492, bf16[2,240,2176]{2,1,0:T(8,128)(2,1)} %copy-done.14, s32[]{:T(128)S(6)} %select_n.493, s32[]{:T(128)S(6)} %select_n.491, s32[]{:T(128)S(6)} %select_n.489), kind=kLoop, calls=%fused_computation.19 | loop fusion | flops 2611200 | bytes 9400336 | tf_op jit(solution)/shard_map/convert_element_type | solution.py:311
  219.9 26.9 %shard_map.38 = (f32[1088,2176]{1,0:T(8,128)}, bf16[1088,2176]{1,0:T(8,128)(2,1)}, f32[1088,2176]{1,0:T(8,128)}, bf16[1088,2176]{1,0:T(8,128)(2,1)}) custom-call(s32[3]{0:T(128)} %pad_add_fusion.sp_ref, bf16[272,1536]{1,0:T(8,128)(2,1)} %get-tuple-element.154.refs_0_.refs_8_, bf16[272,1536]{1,0:T(8,128)(2,1)} %copy-done.9, ...), custom_call_target="tpu_custom_call" | custom-call | flops 10000000000 | bytes 1000000 | tf_op jit(solution)/shard_map/pallas_call | solution.py:257
  248.0 1.2 add_convert_fusion.2
  249.2 1.8 dynamic-slice_bitcast_fusion.3
  252.1 1.3 collective-permute-start.25
  253.4 3.0 collective-permute-done.23
  256.4 4.4 %fusion.4 = (bf16[272,2176]{1,0:T(8,128)(2,1)}, f32[272,2176]{1,0:T(8,128)S(1)}) fusion(f32[1088,2176]{1,0:T(8,128)} %get-tuple-element.171, s32[]{:T(128)S(6)} %select_n.496, bf16[2,272,2176]{2,1,0:T(8,128)(2,1)} %collective-permute-done.23, s32[]{:T(128)S(6)} %select_n.493, s32[]{:T(128)S(6)} %select_n.491, s32[]{:T(128)S(6)} %select_n.497), kind=kLoop, calls=%fused_computation.10 | loop fusion | flops 2959360 | bytes 10653712 | tf_op jit(solution)/shard_map/convert_element_type | solution.py:311
  262.0 23.0 %shard_map.39 = (f32[960,2176]{1,0:T(8,128)}, bf16[960,2176]{1,0:T(8,128)(2,1)}) custom-call(s32[3]{0:T(128)} %pad_add_fusion.sp_ref, f32[960,2176]{1,0:T(8,128)} %get-tuple-element.179.refs_0_, bf16[240,3072]{1,0:T(8,128)(2,1)} %copy-done.5, bf16[240,3072]{1,0:T(8,128)(2,1)} %collective-permute-done.refs_2_, ...), custom_call_target="tpu_custom_call" | custom-call | flops 10000000000 | bytes 1000000 | tf_op jit(solution)/shard_map/pallas_call | solution.py:257
  285.1 1.7 dynamic-slice_bitcast_fusion.5
  287.0 7.5 %collective-permute-done.25.refs_7_ = bf16[272,3072]{1,0:T(8,128)(2,1)} collective-permute-done((bf16[272,3072]{1,0:T(8,128)(2,1)}, bf16[272,3072]{1,0:T(8,128)(2,1)}, u32[]{:S(2)}, u32[]{:S(2)}) %collective-permute-start.25) | collective-permute-done | bytes 1671200 | tf_op jit(solution)/shard_map/ppermute | solution.py:107
  294.5 1.3 add_convert_fusion
  296.4 1.5 collective-permute-start.28
  297.9 2.3 collective-permute-done.26
  300.2 1.4 convert_add_fusion.5
  301.5 1.2 collective-permute-start.27
  302.8 25.4 %shard_map.40 = (f32[1088,2176]{1,0:T(8,128)}, bf16[1088,2176]{1,0:T(8,128)(2,1)}) custom-call(s32[3]{0:T(128)} %pad_add_fusion.sp_ref, f32[1088,2176]{1,0:T(8,128)} %get-tuple-element.204.refs_0_, bf16[272,3072]{1,0:T(8,128)(2,1)} %copy-done, bf16[272,3072]{1,0:T(8,128)(2,1)} %copy-done.17, bf16[272,3072]{1,0:T(8,128)(2,1)} %copy-done.16, ...), custom_call_target="tpu_custom_call" | custom-call | flops 10000000000 | bytes 1000000 | tf_op jit(solution)/shard_map/pallas_call | solution.py:257
  328.1 1.8 dynamic-slice_bitcast_fusion.1
  331.2 1.8 add_convert_fusion.1
  333.8 1.3 collective-permute-start.31
  335.1 2.9 collective-permute-done.29
  338.0 3.8 fusion
  343.3 2.4 collective-permute-start.34
  345.6 1.5 collective-permute-done.32
  347.1 3.3 collective-permute-done.33
  350.4 17.2 %collective-permute-done.34 = bf16[240,128]{1,0:T(8,128)(2,1)S(1)} collective-permute-done((bf16[240,128]{1,0:T(8,128)(2,1)S(1)}, bf16[240,128]{1,0:T(8,128)(2,1)S(1)}, u32[]{:S(2)}, u32[]{:S(2)}) %collective-permute-start.34) | collective-permute-done | bytes 61472 | tf_op jit(solution)/shard_map/ppermute | solution.py:146
  367.7 1.7 collective-permute-done.30
  369.5 2.6 fusion.3
  373.2 2.4 collective-permute-start.38
  375.7 2.1 collective-permute-start.35
  377.8 3.1 collective-permute-done.37
  383.2 11.6 %shard_map.41 = bf16[512,2048]{1,0:T(8,128)(2,1)} custom-call(s32[1]{0:T(128)} %bitcast.where_ref, bf16[512,2048]{1,0:T(8,128)(2,1)S(1)} %pad_maximum_fusion.2.q_ref, bf16[1024,512]{1,0:T(8,128)(2,1)S(1)} %pad_maximum_fusion.7.kv_ref), custom_call_target="tpu_custom_call" | custom-call | flops 6000000000 | bytes 5000000 | tf_op jit(solution)/shard_map/pallas_call | solution.py:83
  (102 shorter events, 23.6 us)
Async XLA Ops:
  1.5 14.2 %copy-start.5 = (bf16[240,3072]{1,0:T(8,128)(2,1)}, bf16[240,3072]{1,0:T(8,128)(2,1)S(1)}, u32[]{:S(2)}) copy-start(bf16[240,3072]{1,0:T(8,128)(2,1)S(1)} %slice.48.refs_1_) | copy-start | bytes 4423684
  1.5 45.2 %collective-permute-start = (bf16[240,3072]{1,0:T(8,128)(2,1)S(1)}, bf16[240,3072]{1,0:T(8,128)(2,1)}, u32[]{:S(2)}, u32[]{:S(2)}) collective-permute-start(bf16[240,3072]{1,0:T(8,128)(2,1)S(1)} %slice.48.refs_1_), channel_id=1, source_target_pairs={{4,8},{8,4},{5,9},{9,5},{6,10},{10,6},{7,11},{11,7},{20,24},{24,20... | collective-permute-start | bytes 4423688 | tf_op jit(solution)/shard_map/ppermute | solution.py:107
  3.3 43.3 %collective-permute-start.1 = (bf16[240,3072]{1,0:T(8,128)(2,1)S(1)}, bf16[240,3072]{1,0:T(8,128)(2,1)}, u32[]{:S(2)}, u32[]{:S(2)}) collective-permute-start(bf16[240,3072]{1,0:T(8,128)(2,1)S(1)} %slice.48.refs_1_), channel_id=1, source_target_pairs={{4,0},{8,12},{5,1},{9,13},{6,2},{10,14},{7,3},{11,15},{20,16},{24,... | collective-permute-start | bytes 4423688 | tf_op jit(solution)/shard_map/ppermute | solution.py:107
  7.0 21.7 %collective-permute-start.2 = (bf16[240,1536]{1,0:T(8,128)(2,1)}, bf16[240,1536]{1,0:T(8,128)(2,1)}, u32[]{:S(2)}, u32[]{:S(2)}) collective-permute-start(bf16[240,1536]{1,0:T(8,128)(2,1)} %get-tuple-element.128), channel_id=1, source_target_pairs={{0,4},{12,8},{1,5},{13,9},{2,6},{14,10},{3,7},{15,11},{16,20},{28,... | collective-permute-start | bytes 2211848 | tf_op jit(solution)/shard_map/ppermute | solution.py:107
  17.0 29.6 %collective-permute-start.3 = (bf16[272,1536]{1,0:T(8,128)(2,1)}, bf16[272,1536]{1,0:T(8,128)(2,1)}, u32[]{:S(2)}, u32[]{:S(2)}) collective-permute-start(bf16[272,1536]{1,0:T(8,128)(2,1)} %get-tuple-element.129), channel_id=1, source_target_pairs={{0,4},{12,8},{1,5},{13,9},{2,6},{14,10},{3,7},{15,11},{16,20},{28,... | collective-permute-start | bytes 2506760 | tf_op jit(solution)/shard_map/ppermute | solution.py:107
  20.8 143.9 %copy-start = (bf16[272,3072]{1,0:T(8,128)(2,1)}, bf16[272,3072]{1,0:T(8,128)(2,1)S(1)}, u32[]{:S(2)}) copy-start(bf16[272,3072]{1,0:T(8,128)(2,1)S(1)} %slice.51.refs_1_) | copy-start | bytes 5013508
  24.1 107.6 %copy-start.6 = (bf16[240,3072]{1,0:T(8,128)(2,1)S(1)}, bf16[240,3072]{1,0:T(8,128)(2,1)}, u32[]{:S(2)}) copy-start(bf16[240,3072]{1,0:T(8,128)(2,1)} %copy-done.5) | copy-start | bytes 4423684
  46.6 38.0 %collective-permute-start.4 = (bf16[384,2176]{1,0:T(8,128)(2,1)S(1)}, bf16[384,2176]{1,0:T(8,128)(2,1)S(1)}, u32[]{:S(2)}, u32[]{:S(2)}) collective-permute-start(bf16[384,2176]{1,0:T(8,128)(2,1)S(1)} %get-tuple-element.115), channel_id=1, source_target_pairs={{0,4},{12,8},{1,5},{13,9},{2,6},{14,10},{3,7},{15,11},{16,20},{28,... | collective-permute-start | bytes 5013512 | tf_op jit(solution)/shard_map/ppermute | solution.py:107
  50.8 37.7 %collective-permute-start.7 = (bf16[272,3072]{1,0:T(8,128)(2,1)S(1)}, bf16[272,3072]{1,0:T(8,128)(2,1)S(1)}, u32[]{:S(2)}, u32[]{:S(2)}) collective-permute-start(bf16[272,3072]{1,0:T(8,128)(2,1)S(1)} %slice.51.refs_1_), channel_id=1, source_target_pairs={{4,0},{8,12},{5,1},{9,13},{6,2},{10,14},{7,3},{11,15},{20,16},{24,... | collective-permute-start | bytes 5013512 | tf_op jit(solution)/shard_map/ppermute | solution.py:107
  52.1 1.5 collective-permute-start.6
  52.9 0.7 collective-permute-start.5
  53.6 35.0 %copy-start.10 = (bf16[240,1536]{1,0:T(8,128)(2,1)}, bf16[240,1536]{1,0:T(8,128)(2,1)S(1)}, u32[]{:S(2)}) copy-start(bf16[240,1536]{1,0:T(8,128)(2,1)S(1)} %collective-permute-done.5.refs_3_.refs_11_) | copy-start | bytes 2211844
  53.6 35.0 %copy-start.8 = (bf16[272,1536]{1,0:T(8,128)(2,1)}, bf16[272,1536]{1,0:T(8,128)(2,1)S(1)}, u32[]{:S(2)}) copy-start(bf16[272,1536]{1,0:T(8,128)(2,1)S(1)} %collective-permute-done.6.refs_3_.refs_11_) | copy-start | bytes 2506756
  84.7 88.4 %copy-start.1 = (bf16[384,2176]{1,0:T(8,128)(2,1)}, bf16[384,2176]{1,0:T(8,128)(2,1)S(1)}, u32[]{:S(2)}) copy-start(bf16[384,2176]{1,0:T(8,128)(2,1)S(1)} %collective-permute-done.4.refs_12_) | copy-start | bytes 5013508
  88.6 82.0 %copy-start.16 = (bf16[272,3072]{1,0:T(8,128)(2,1)}, bf16[272,3072]{1,0:T(8,128)(2,1)S(1)}, u32[]{:S(2)}) copy-start(bf16[272,3072]{1,0:T(8,128)(2,1)S(1)} %collective-permute-done.7.refs_3_) | copy-start | bytes 5013508
  88.6 39.5 %collective-permute-start.8 = (bf16[384,2176]{1,0:T(8,128)(2,1)S(1)}, bf16[384,2176]{1,0:T(8,128)(2,1)S(1)}, u32[]{:S(2)}, u32[]{:S(2)}) collective-permute-start(bf16[384,2176]{1,0:T(8,128)(2,1)S(1)} %get-tuple-element.121), channel_id=1, source_target_pairs={{0,4},{12,8},{1,5},{13,9},{2,6},{14,10},{3,7},{15,11},{16,20},{28,... | collective-permute-start | bytes 5013512 | tf_op jit(solution)/shard_map/ppermute | solution.py:107
  93.7 34.3 %collective-permute-start.9 = (bf16[272,3072]{1,0:T(8,128)(2,1)S(1)}, bf16[272,3072]{1,0:T(8,128)(2,1)S(1)}, u32[]{:S(2)}, u32[]{:S(2)}) collective-permute-start(bf16[272,3072]{1,0:T(8,128)(2,1)S(1)} %slice.51.refs_1_), channel_id=1, source_target_pairs={{4,8},{8,4},{5,9},{9,5},{6,10},{10,6},{7,11},{11,7},{20,24},{24,20... | collective-permute-start | bytes 5013512 | tf_op jit(solution)/shard_map/ppermute | solution.py:107
  94.5 34.7 %collective-permute-start.11 = (bf16[384,2176]{1,0:T(8,128)(2,1)S(1)}, bf16[384,2176]{1,0:T(8,128)(2,1)S(1)}, u32[]{:S(2)}, u32[]{:S(2)}) collective-permute-start(bf16[384,2176]{1,0:T(8,128)(2,1)S(1)} %collective-permute-done.4.refs_12_), channel_id=1, source_target_pairs={{0,16},{16,0},{1,17},{17,1},{2,18},{18,2},{3,19},{19,3},{4,20},{20... | collective-permute-start | bytes 5013512 | tf_op jit(solution)/shard_map/ppermute | solution.py:107
  95.8 32.2 %collective-permute-start.10 = (bf16[240,3072]{1,0:T(8,128)(2,1)}, bf16[240,3072]{1,0:T(8,128)(2,1)S(1)}, u32[]{:S(2)}, u32[]{:S(2)}) collective-permute-start(bf16[240,3072]{1,0:T(8,128)(2,1)} %collective-permute-done.refs_2_), channel_id=1, source_target_pairs={{4,0},{8,12},{5,1},{9,13},{6,2},{10,14},{7,3},{11,15},{20,16},{24,... | collective-permute-start | bytes 4423688 | tf_op jit(solution)/shard_map/ppermute | solution.py:107
  128.0 42.6 %copy-start.19 = (bf16[240,3072]{1,0:T(8,128)(2,1)}, bf16[240,3072]{1,0:T(8,128)(2,1)S(1)}, u32[]{:S(2)}) copy-start(bf16[240,3072]{1,0:T(8,128)(2,1)S(1)} %collective-permute-done.10.refs_5_) | copy-start | bytes 4423684
  128.0 42.5 %copy-start.2 = (bf16[384,2176]{1,0:T(8,128)(2,1)}, bf16[384,2176]{1,0:T(8,128)(2,1)S(1)}, u32[]{:S(2)}) copy-start(bf16[384,2176]{1,0:T(8,128)(2,1)S(1)} %collective-permute-done.8.refs_13_) | copy-start | bytes 5013508
  128.1 42.5 %copy-start.17 = (bf16[272,3072]{1,0:T(8,128)(2,1)}, bf16[272,3072]{1,0:T(8,128)(2,1)S(1)}, u32[]{:S(2)}) copy-start(bf16[272,3072]{1,0:T(8,128)(2,1)S(1)} %collective-permute-done.9.refs_2_) | copy-start | bytes 5013508
  129.2 41.4 %copy-start.3 = (bf16[384,2176]{1,0:T(8,128)(2,1)}, bf16[384,2176]{1,0:T(8,128)(2,1)S(1)}, u32[]{:S(2)}) copy-start(bf16[384,2176]{1,0:T(8,128)(2,1)S(1)} %collective-permute-done.11.refs_14_) | copy-start | bytes 5013508
  129.2 35.0 %collective-permute-start.16 = (bf16[384,2176]{1,0:T(8,128)(2,1)S(1)}, bf16[384,2176]{1,0:T(8,128)(2,1)S(1)}, u32[]{:S(2)}, u32[]{:S(2)}) collective-permute-start(bf16[384,2176]{1,0:T(8,128)(2,1)S(1)} %collective-permute-done.8.refs_13_), channel_id=1, source_target_pairs={{0,16},{16,0},{1,17},{17,1},{2,18},{18,2},{3,19},{19,3},{4,20},{20... | collective-permute-start | bytes 5013512 | tf_op jit(solution)/shard_map/ppermute | solution.py:107
  130.4 34.2 %collective-permute-start.15 = (bf16[272,3072]{1,0:T(8,128)(2,1)S(1)}, bf16[272,3072]{1,0:T(8,128)(2,1)S(1)}, u32[]{:S(2)}, u32[]{:S(2)}) collective-permute-start(bf16[272,3072]{1,0:T(8,128)(2,1)S(1)} %collective-permute-done.9.refs_2_), channel_id=1, source_target_pairs={{4,0},{8,12},{5,1},{9,13},{6,2},{10,14},{7,3},{11,15},{20,16},{24,... | collective-permute-start | bytes 5013512 | tf_op jit(solution)/shard_map/ppermute | solution.py:107
  131.7 29.7 %collective-permute-start.12 = (bf16[240,3072]{1,0:T(8,128)(2,1)S(1)}, bf16[240,3072]{1,0:T(8,128)(2,1)}, u32[]{:S(2)}, u32[]{:S(2)}) collective-permute-start(bf16[240,3072]{1,0:T(8,128)(2,1)S(1)} %copy-done.6), channel_id=1, source_target_pairs={{0,4},{12,8},{1,5},{13,9},{2,6},{14,10},{3,7},{15,11},{16,20},{28,... | collective-permute-start | bytes 4423688 | tf_op jit(solution)/shard_map/ppermute | solution.py:107
  136.9 1.4 collective-permute-start.14
  137.6 0.7 collective-permute-start.13
  138.4 32.3 %copy-start.11 = (bf16[240,1536]{1,0:T(8,128)(2,1)}, bf16[240,1536]{1,0:T(8,128)(2,1)S(1)}, u32[]{:S(2)}) copy-start(bf16[240,1536]{1,0:T(8,128)(2,1)S(1)} %collective-permute-done.13.refs_1_.refs_9_) | copy-start | bytes 2211844
  138.4 32.2 %copy-start.9 = (bf16[272,1536]{1,0:T(8,128)(2,1)}, bf16[272,1536]{1,0:T(8,128)(2,1)S(1)}, u32[]{:S(2)}) copy-start(bf16[272,1536]{1,0:T(8,128)(2,1)S(1)} %collective-permute-done.14.refs_1_.refs_9_) | copy-start | bytes 2506756
  164.2 6.5 %copy-start.4 = (bf16[384,2176]{1,0:T(8,128)(2,1)}, bf16[384,2176]{1,0:T(8,128)(2,1)S(1)}, u32[]{:S(2)}) copy-start(bf16[384,2176]{1,0:T(8,128)(2,1)S(1)} %collective-permute-done.16.refs_15_) | copy-start | bytes 5013508
  164.7 6.0 %copy-start.18 = (bf16[272,3072]{1,0:T(8,128)(2,1)}, bf16[272,3072]{1,0:T(8,128)(2,1)S(1)}, u32[]{:S(2)}) copy-start(bf16[272,3072]{1,0:T(8,128)(2,1)S(1)} %collective-permute-done.15.refs_5_) | copy-start | bytes 5013508
  164.7 33.7 %collective-permute-start.18 = (bf16[272,3072]{1,0:T(8,128)(2,1)S(1)}, bf16[272,3072]{1,0:T(8,128)(2,1)}, u32[]{:S(2)}, u32[]{:S(2)}) collective-permute-start(bf16[272,3072]{1,0:T(8,128)(2,1)S(1)} %slice.51.refs_1_), channel_id=1, source_target_pairs={{0,4},{12,8},{1,5},{13,9},{2,6},{14,10},{3,7},{15,11},{16,20},{28,... | collective-permute-start | bytes 5013512 | tf_op jit(solution)/shard_map/ppermute | solution.py:107
  170.7 27.0 %collective-permute-start.17 = (bf16[240,3072]{1,0:T(8,128)(2,1)}, bf16[240,3072]{1,0:T(8,128)(2,1)}, u32[]{:S(2)}, u32[]{:S(2)}) collective-permute-start(bf16[240,3072]{1,0:T(8,128)(2,1)} %collective-permute-done.12.refs_4_), channel_id=1, source_target_pairs={{4,8},{8,4},{5,9},{9,5},{6,10},{10,6},{7,11},{11,7},{20,24},{24,20... | collective-permute-start | bytes 4423688 | tf_op jit(solution)/shard_map/ppermute | solution.py:107
  201.6 11.6 %collective-permute-start.20 = (bf16[2,240,2176]{2,1,0:T(8,128)(2,1)}, bf16[2,240,2176]{2,1,0:T(8,128)(2,1)S(1)}, u32[]{:S(2)}, u32[]{:S(2)}) collective-permute-start(bf16[2,240,2176]{2,1,0:T(8,128)(2,1)} %pad_maximum_fusion.3), channel_id=1, source_target_pairs={{0,1},{1,0},{2,3},{3,2},{4,5},{5,4},{6,7},{7,6},{8,9},{9,8},{10,11... | collective-permute-start | bytes 6266888 | tf_op jit(solution)/shard_map/ppermute | solution.py:137
  209.3 38.7 %collective-permute-start.22 = (bf16[272,3072]{1,0:T(8,128)(2,1)}, bf16[272,3072]{1,0:T(8,128)(2,1)}, u32[]{:S(2)}, u32[]{:S(2)}) collective-permute-start(bf16[272,3072]{1,0:T(8,128)(2,1)} %collective-permute-done.18.refs_4_), channel_id=1, source_target_pairs={{4,8},{8,4},{5,9},{9,5},{6,10},{10,6},{7,11},{11,7},{20,24},{24,20... | collective-permute-start | bytes 5013512 | tf_op jit(solution)/shard_map/ppermute | solution.py:107
  211.2 36.8 %collective-permute-start.19 = (bf16[240,3072]{1,0:T(8,128)(2,1)}, bf16[240,3072]{1,0:T(8,128)(2,1)}, u32[]{:S(2)}, u32[]{:S(2)}) collective-permute-start(bf16[240,3072]{1,0:T(8,128)(2,1)} %collective-permute-done.17.refs_6_), channel_id=1, source_target_pairs={{4,0},{8,12},{5,1},{9,13},{6,2},{10,14},{7,3},{11,15},{20,16},{24,... | collective-permute-start | bytes 4423688 | tf_op jit(solution)/shard_map/ppermute | solution.py:107
  213.3 1.3 copy-start.14
  218.7 29.3 %collective-permute-start.21 = (bf16[240,2176]{1,0:T(8,128)(2,1)}, bf16[240,2176]{1,0:T(8,128)(2,1)S(1)}, u32[]{:S(2)}, u32[]{:S(2)}) collective-permute-start(bf16[240,2176]{1,0:T(8,128)(2,1)} %get-tuple-element.164), channel_id=1, source_target_pairs={{0,2},{1,3},{2,0},{3,1},{4,6},{5,7},{6,4},{7,5},{8,10},{9,11},{10,... | collective-permute-start | bytes 3133448 | tf_op jit(solution)/shard_map/ppermute | solution.py:141
  251.2 5.2 %collective-permute-start.23 = (bf16[2,272,2176]{2,1,0:T(8,128)(2,1)S(1)}, bf16[2,272,2176]{2,1,0:T(8,128)(2,1)}, u32[]{:S(2)}, u32[]{:S(2)}) collective-permute-start(bf16[2,272,2176]{2,1,0:T(8,128)(2,1)S(1)} %pad_maximum_fusion), channel_id=1, source_target_pairs={{0,1},{1,0},{2,3},{3,2},{4,5},{5,4},{6,7},{7,6},{8,9},{9,8},{10,11... | collective-permute-start | bytes 7102472 | tf_op jit(solution)/shard_map/ppermute | solution.py:137
  252.1 42.4 %collective-permute-start.25 = (bf16[272,3072]{1,0:T(8,128)(2,1)}, bf16[272,3072]{1,0:T(8,128)(2,1)}, u32[]{:S(2)}, u32[]{:S(2)}) collective-permute-start(bf16[272,3072]{1,0:T(8,128)(2,1)} %collective-permute-done.22.refs_6_), channel_id=1, source_target_pairs={{4,0},{8,12},{5,1},{9,13},{6,2},{10,14},{7,3},{11,15},{20,16},{24,... | collective-permute-start | bytes 5013512 | tf_op jit(solution)/shard_map/ppermute | solution.py:107
  260.8 33.7 %collective-permute-start.24 = (bf16[272,2176]{1,0:T(8,128)(2,1)}, bf16[272,2176]{1,0:T(8,128)(2,1)S(1)}, u32[]{:S(2)}, u32[]{:S(2)}) collective-permute-start(bf16[272,2176]{1,0:T(8,128)(2,1)} %get-tuple-element.189), channel_id=1, source_target_pairs={{0,2},{1,3},{2,0},{3,1},{4,6},{5,7},{6,4},{7,5},{8,10},{9,11},{10,... | collective-permute-start | bytes 3551240 | tf_op jit(solution)/shard_map/ppermute | solution.py:141
  286.8 13.4 %copy-start.15 = (f32[960,2176]{1,0:T(8,128)S(1)}, f32[960,2176]{1,0:T(8,128)}, u32[]{:S(2)}) copy-start(f32[960,2176]{1,0:T(8,128)} %get-tuple-element.194) | copy-start | bytes 25067524
  295.8 4.4 %collective-permute-start.26 = (bf16[2,240,2176]{2,1,0:T(8,128)(2,1)S(1)}, bf16[2,240,2176]{2,1,0:T(8,128)(2,1)S(1)}, u32[]{:S(2)}, u32[]{:S(2)}) collective-permute-start(bf16[2,240,2176]{2,1,0:T(8,128)(2,1)S(1)} %pad_maximum_fusion.4), channel_id=1, source_target_pairs={{0,1},{1,0},{2,3},{3,2},{4,5},{5,4},{6,7},{7,6},{8,9},{9,8},{10,11... | collective-permute-start | bytes 6266888 | tf_op jit(solution)/shard_map/ppermute | solution.py:137
  296.4 33.8 %collective-permute-start.28 = (bf16[240,2176]{1,0:T(8,128)(2,1)}, bf16[240,2176]{1,0:T(8,128)(2,1)S(1)}, u32[]{:S(2)}, u32[]{:S(2)}) collective-permute-start(bf16[240,2176]{1,0:T(8,128)(2,1)} %add_convert_fusion.2), channel_id=1, source_target_pairs={{4,0},{8,12},{5,1},{9,13},{6,2},{10,14},{7,3},{11,15},{20,16},{24,... | collective-permute-start | bytes 3133448 | tf_op jit(solution)/shard_map/ppermute | solution.py:107
  301.5 28.7 %collective-permute-start.27 = (bf16[240,2176]{1,0:T(8,128)(2,1)}, bf16[240,2176]{1,0:T(8,128)(2,1)}, u32[]{:S(2)}, u32[]{:S(2)}) collective-permute-start(bf16[240,2176]{1,0:T(8,128)(2,1)} %get-tuple-element.196), channel_id=1, source_target_pairs={{0,2},{1,3},{2,0},{3,1},{4,6},{5,7},{6,4},{7,5},{8,10},{9,11},{10,... | collective-permute-start | bytes 3133448 | tf_op jit(solution)/shard_map/ppermute | solution.py:141
  330.2 1.0 copy-start.20
  333.0 34.6 %copy-start.7 = (bf16[240,2176]{1,0:T(8,128)(2,1)}, bf16[240,2176]{1,0:T(8,128)(2,1)S(1)}, u32[]{:S(2)}) copy-start(bf16[240,2176]{1,0:T(8,128)(2,1)S(1)} %add_convert_fusion.1) | copy-start | bytes 3133444
  333.0 5.0 %collective-permute-start.29 = (bf16[2,272,2176]{2,1,0:T(8,128)(2,1)S(1)}, bf16[2,272,2176]{2,1,0:T(8,128)(2,1)S(1)}, u32[]{:S(2)}, u32[]{:S(2)}) collective-permute-start(bf16[2,272,2176]{2,1,0:T(8,128)(2,1)S(1)} %pad_maximum_fusion.1), channel_id=1, source_target_pairs={{0,1},{1,0},{2,3},{3,2},{4,5},{5,4},{6,7},{7,6},{8,9},{9,8},{10,11... | collective-permute-start | bytes 7102472 | tf_op jit(solution)/shard_map/ppermute | solution.py:137
  333.8 33.9 %collective-permute-start.31 = (bf16[272,2176]{1,0:T(8,128)(2,1)}, bf16[272,2176]{1,0:T(8,128)(2,1)S(1)}, u32[]{:S(2)}, u32[]{:S(2)}) collective-permute-start(bf16[272,2176]{1,0:T(8,128)(2,1)} %add_convert_fusion), channel_id=1, source_target_pairs={{4,0},{8,12},{5,1},{9,13},{6,2},{10,14},{7,3},{11,15},{20,16},{24,... | collective-permute-start | bytes 3551240 | tf_op jit(solution)/shard_map/ppermute | solution.py:107
  338.0 3.8 copy-start.12
  341.9 27.6 %collective-permute-start.30 = (bf16[272,2176]{1,0:T(8,128)(2,1)}, bf16[272,2176]{1,0:T(8,128)(2,1)}, u32[]{:S(2)}, u32[]{:S(2)}) collective-permute-start(bf16[272,2176]{1,0:T(8,128)(2,1)} %fusion), channel_id=1, source_target_pairs={{0,2},{1,3},{2,0},{3,1},{4,6},{5,7},{6,4},{7,5},{8,10},{9,11},{10,... | collective-permute-start | bytes 3551240 | tf_op jit(solution)/shard_map/ppermute | solution.py:141
  342.1 5.0 %collective-permute-start.32 = (bf16[240,128]{1,0:T(8,128)(2,1)S(1)}, bf16[240,128]{1,0:T(8,128)(2,1)S(1)}, u32[]{:S(2)}, u32[]{:S(2)}) collective-permute-start(bf16[240,128]{1,0:T(8,128)(2,1)S(1)} %slice.66), channel_id=1, source_target_pairs={{0,12},{4,8},{8,4},{12,0},{1,13},{5,9},{9,5},{13,1},{2,14},{6,10},... | collective-permute-start | bytes 184328 | tf_op jit(solution)/shard_map/ppermute | solution.py:146
  343.2 7.2 %collective-permute-start.33 = (bf16[240,128]{1,0:T(8,128)(2,1)S(1)}, bf16[240,128]{1,0:T(8,128)(2,1)S(1)}, u32[]{:S(2)}, u32[]{:S(2)}) collective-permute-start(bf16[240,128]{1,0:T(8,128)(2,1)S(1)} %slice.66), channel_id=1, source_target_pairs={{0,8},{4,12},{8,0},{12,4},{1,9},{5,13},{9,1},{13,5},{2,10},{6,14},... | collective-permute-start | bytes 184328 | tf_op jit(solution)/shard_map/ppermute | solution.py:146
  343.3 24.4 %collective-permute-start.34 = (bf16[240,128]{1,0:T(8,128)(2,1)S(1)}, bf16[240,128]{1,0:T(8,128)(2,1)S(1)}, u32[]{:S(2)}, u32[]{:S(2)}) collective-permute-start(bf16[240,128]{1,0:T(8,128)(2,1)S(1)} %slice.66), channel_id=1, source_target_pairs={{0,4},{4,0},{8,12},{12,8},{1,5},{5,1},{9,13},{13,9},{2,6},{6,2},{1... | collective-permute-start | bytes 184328 | tf_op jit(solution)/shard_map/ppermute | solution.py:146
  345.6 23.8 %copy-start.13 = (bf16[2,272,2176]{2,1,0:T(8,128)(2,1)S(1)}, bf16[2,272,2176]{2,1,0:T(8,128)(2,1)}, u32[]{:S(2)}) copy-start(bf16[2,272,2176]{2,1,0:T(8,128)(2,1)} %copy-done.12) | copy-start | bytes 7102468
  372.0 5.8 %collective-permute-start.36 = (bf16[272,128]{1,0:T(8,128)(2,1)S(1)}, bf16[272,128]{1,0:T(8,128)(2,1)S(1)}, u32[]{:S(2)}, u32[]{:S(2)}) collective-permute-start(bf16[272,128]{1,0:T(8,128)(2,1)S(1)} %slice.67), channel_id=1, source_target_pairs={{0,12},{4,8},{8,4},{12,0},{1,13},{5,9},{9,5},{13,1},{2,14},{6,10},... | collective-permute-start | bytes 208904 | tf_op jit(solution)/shard_map/ppermute | solution.py:146
  373.2 7.7 %collective-permute-start.37 = (bf16[272,128]{1,0:T(8,128)(2,1)S(1)}, bf16[272,128]{1,0:T(8,128)(2,1)S(1)}, u32[]{:S(2)}, u32[]{:S(2)}) collective-permute-start(bf16[272,128]{1,0:T(8,128)(2,1)S(1)} %slice.67), channel_id=1, source_target_pairs={{0,8},{4,12},{8,0},{12,4},{1,9},{5,13},{9,1},{13,5},{2,10},{6,14},... | collective-permute-start | bytes 208904 | tf_op jit(solution)/shard_map/ppermute | solution.py:146
  373.2 7.7 %collective-permute-start.38 = (bf16[272,128]{1,0:T(8,128)(2,1)S(1)}, bf16[272,128]{1,0:T(8,128)(2,1)S(1)}, u32[]{:S(2)}, u32[]{:S(2)}) collective-permute-start(bf16[272,128]{1,0:T(8,128)(2,1)S(1)} %slice.67), channel_id=1, source_target_pairs={{0,4},{4,0},{8,12},{12,8},{1,5},{5,1},{9,13},{13,9},{2,6},{6,2},{1... | collective-permute-start | bytes 208904 | tf_op jit(solution)/shard_map/ppermute | solution.py:146
  375.7 6.4 %slice-start = ((bf16[240,2176]{1,0:T(8,128)(2,1)}), bf16[240,2048]{1,0:T(8,128)(2,1)S(1)}, s32[]{:S(2)}) async-start(bf16[240,2176]{1,0:T(8,128)(2,1)} %copy-done.7), calls=%async_computation | async-start | bytes 1966080 | tf_op jit(solution)/shard_map/slice | solution.py:422
  375.7 6.1 %collective-permute-start.35 = (bf16[240,512]{1,0:T(8,128)(2,1)S(1)}, bf16[240,512]{1,0:T(8,128)(2,1)S(1)}, u32[]{:S(2)}, u32[]{:S(2)}) collective-permute-start(bf16[240,512]{1,0:T(8,128)(2,1)S(1)} %pad_maximum_fusion.11), channel_id=1, source_target_pairs={{0,1},{1,0},{2,3},{3,2},{4,5},{5,4},{6,7},{7,6},{8,9},{9,8},{10,11... | collective-permute-start | bytes 737288 | tf_op jit(solution)/shard_map/ppermute | solution.py:137
  381.0 2.0 collective-permute-start.39

commit v5 on v4

--- a/solution.py
+++ b/solution.py
@@ -279,7 +279,7 @@
     columns = width + kv_weight.shape[1]
     z, hid, grp = (lax.axis_index(name) for name in ("ffn", "hid", "grp"))
     chip, core = hid // 2, hid % 2
-    part = depth // 6 // 128 * 128
+    part = depth * 5 // 36 // 128 * 128
     first = depth - 2 * part
     mid, into, out = along("ffn", MID), along("ffn", INTO), along("ffn", OUT)
     across = along("grp", [(0, 1), (1, 0)])

time: 396 us -> 401 us (1.013)
  waiting for transfers between devices: 161 us -> 172 us
  starting transfers between devices: 76.2 us -> 69.1 us
    ppermute x24, waiting for transfers between devices: 125 us -> 136 us  [along(): return lambda x: lax.ppermute(x, axis, pairs)]
    ppermute x24, starting transfers between devices: 52.3 us -> 48.3 us  [along(): return lambda x: lax.ppermute(x, axis, pairs)]
  transfers between devices with their start and end apart: 40 -> 40, of which waited for: 22 -> 23; matrix products, arithmetic and copies ran while one was open for 7% -> 7% of each run, Pallas kernels for 25% -> 25%
where the time goes in v5:
time: 401 us; the launch traced here: 400 us
  waiting for transfers between devices  172 us (43%)
  Pallas kernels  113 us (28%)
  starting transfers between devices  69.1 us (17%)
  other arithmetic  26.8 us (7%)
  local copies, waits for them, and re-layouts  17.9 us (4%)
    ppermute x24, waiting for transfers between devices, along(): return lambda x: lax.ppermute(x, axis, pairs)  136 us
    pallas_call x4, Pallas kernels, product(): pl.pallas_call(functools.partial(product_kernel, shape, sums, kinds, (til...  101 us
    ppermute x24, starting transfers between devices, along(): return lambda x: lax.ppermute(x, axis, pairs)  48.3 us
    ppermute x6, waiting for transfers between devices, gathered(): lax.ppermute(x, 'ffn', [(i, i ^ k) for i in range(4)])  25 us
    convert_element_type x3, other arithmetic, over_cores(): return (keep, give.astype(BF16))  12.4 us
    pallas_call x1, Pallas kernels, attention(): pl.pallas_call(functools.partial(attention_kernel, rows), out_shape=jax.S...  11.6 us
    ppermute x6, starting transfers between devices, other_core(): return lax.ppermute(x, 'hid', [(i, i ^ 1) for i in range(4)])  9.87 us
    ppermute x6, waiting for transfers between devices, other_core(): return lax.ppermute(x, 'hid', [(i, i ^ 1) for i in range(4)])  9.44 us
  transfers between devices with their start and end apart: 40, of which 23 were waited for; matrix products, arithmetic and copies ran while one was open for 7% of the time, Pallas kernels for 25%

profile of v5, /device:TPU:1, one launch (start us, length us, event | category | flops | bytes accessed | tf_op | source)
XLA Modules:
  0.0 399.5 jit_solution(14231438054184681639)
XLA Ops:
  0.0 1.5 slice.48.refs_1_
  1.5 1.8 collective-permute-start
  3.4 1.3 collective-permute-start.1
  7.0 7.4 %collective-permute-start.3 = (bf16[272,1280]{1,0:T(8,128)(2,1)}, bf16[272,1280]{1,0:T(8,128)(2,1)}, u32[]{:S(2)}, u32[]{:S(2)}) collective-permute-start(bf16[272,1280]{1,0:T(8,128)(2,1)} %get-tuple-element.129), channel_id=1, source_target_pairs={{0,4},{12,8},{1,5},{13,9},{2,6},{14,10},{3,7},{15,11},{16,20},{28,... | collective-permute-start | bytes 2088968 | tf_op jit(solution)/shard_map/ppermute | solution.py:107
  16.7 2.1 collective-permute-start.2
  18.8 1.6 slice.51.refs_1_
  21.6 1.9 constant_dynamic-slice_fusion.3
  23.5 17.5 %collective-permute-done.2.refs_2_.refs_10_ = bf16[240,1280]{1,0:T(8,128)(2,1)} collective-permute-done((bf16[240,1280]{1,0:T(8,128)(2,1)}, bf16[240,1280]{1,0:T(8,128)(2,1)}, u32[]{:S(2)}, u32[]{:S(2)}) %collective-permute-start.2) | collective-permute-done | bytes 614432 | tf_op jit(solution)/shard_map/ppermute | solution.py:107
  41.0 1.6 collective-permute-done.1.refs_3_
  42.6 1.3 collective-permute-start.7
  44.1 4.2 %collective-permute-start.4 = (bf16[320,2176]{1,0:T(8,128)(2,1)S(1)}, bf16[320,2176]{1,0:T(8,128)(2,1)S(1)}, u32[]{:S(2)}, u32[]{:S(2)}) collective-permute-start(bf16[320,2176]{1,0:T(8,128)(2,1)S(1)} %get-tuple-element.115), channel_id=1, source_target_pairs={{0,4},{12,8},{1,5},{13,9},{2,6},{14,10},{3,7},{15,11},{16,20},{28,... | collective-permute-start | bytes 4177928 | tf_op jit(solution)/shard_map/ppermute | solution.py:107
  49.8 26.4 %collective-permute-done.4.refs_12_ = bf16[320,2176]{1,0:T(8,128)(2,1)S(1)} collective-permute-done((bf16[320,2176]{1,0:T(8,128)(2,1)S(1)}, bf16[320,2176]{1,0:T(8,128)(2,1)S(1)}, u32[]{:S(2)}, u32[]{:S(2)}) %collective-permute-start.4) | collective-permute-done | bytes 1392672 | tf_op jit(solution)/shard_map/ppermute | solution.py:107
  76.2 7.7 %collective-permute-done.7.refs_3_ = bf16[272,3328]{1,0:T(8,128)(2,1)S(1)} collective-permute-done((bf16[272,3328]{1,0:T(8,128)(2,1)S(1)}, bf16[272,3328]{1,0:T(8,128)(2,1)S(1)}, u32[]{:S(2)}, u32[]{:S(2)}) %collective-permute-start.7) | collective-permute-done | bytes 1810464 | tf_op jit(solution)/shard_map/ppermute | solution.py:107
  84.7 1.3 collective-permute-start.10
  86.0 4.3 %collective-permute-start.8 = (bf16[320,2176]{1,0:T(8,128)(2,1)S(1)}, bf16[320,2176]{1,0:T(8,128)(2,1)S(1)}, u32[]{:S(2)}, u32[]{:S(2)}) collective-permute-start(bf16[320,2176]{1,0:T(8,128)(2,1)S(1)} %get-tuple-element.121), channel_id=1, source_target_pairs={{0,4},{12,8},{1,5},{13,9},{2,6},{14,10},{3,7},{15,11},{16,20},{28,... | collective-permute-start | bytes 4177928 | tf_op jit(solution)/shard_map/ppermute | solution.py:107
  90.3 1.3 collective-permute-start.11
  91.6 25.7 %collective-permute-done.8.refs_13_ = bf16[320,2176]{1,0:T(8,128)(2,1)S(1)} collective-permute-done((bf16[320,2176]{1,0:T(8,128)(2,1)S(1)}, bf16[320,2176]{1,0:T(8,128)(2,1)S(1)}, u32[]{:S(2)}, u32[]{:S(2)}) %collective-permute-start.8) | collective-permute-done | bytes 1392672 | tf_op jit(solution)/shard_map/ppermute | solution.py:107
  117.3 2.1 collective-permute-done.11.refs_14_
  119.4 1.5 collective-permute-done.10.refs_5_
  120.8 1.3 collective-permute-start.15
  122.2 6.5 %collective-permute-start.12 = (bf16[240,3328]{1,0:T(8,128)(2,1)S(1)}, bf16[240,3328]{1,0:T(8,128)(2,1)}, u32[]{:S(2)}, u32[]{:S(2)}) collective-permute-start(bf16[240,3328]{1,0:T(8,128)(2,1)S(1)} %slice.48.refs_1_), channel_id=1, source_target_pairs={{0,4},{12,8},{1,5},{13,9},{2,6},{14,10},{3,7},{15,11},{16,20},{28,... | collective-permute-start | bytes 4792328 | tf_op jit(solution)/shard_map/ppermute | solution.py:107
  131.4 25.9 %collective-permute-done.16.refs_15_ = bf16[320,2176]{1,0:T(8,128)(2,1)S(1)} collective-permute-done((bf16[320,2176]{1,0:T(8,128)(2,1)S(1)}, bf16[320,2176]{1,0:T(8,128)(2,1)S(1)}, u32[]{:S(2)}, u32[]{:S(2)}) %collective-permute-start.16) | collective-permute-done | bytes 1392672 | tf_op jit(solution)/shard_map/ppermute | solution.py:107
  157.3 1.3 collective-permute-done.12.refs_4_
  158.6 3.5 collective-permute-done.15.refs_5_
  162.1 2.5 collective-permute-start.18
  166.2 23.7 %shard_map.37 = (f32[960,2176]{1,0:T(8,128)}, bf16[960,2176]{1,0:T(8,128)(2,1)}, f32[960,2176]{1,0:T(8,128)}, bf16[960,2176]{1,0:T(8,128)(2,1)}) custom-call(s32[3]{0:T(128)} %pad_add_fusion.sp_ref, bf16[240,1280]{1,0:T(8,128)(2,1)} %get-tuple-element.136.refs_0_.refs_8_, bf16[240,1280]{1,0:T(8,128)(2,1)} %copy-done.10, ...), custom_call_target="tpu_custom_call" | custom-call | flops 10000000000 | bytes 1000000 | tf_op jit(solution)/shard_map/pallas_call | solution.py:257
  189.9 8.7 %collective-permute-done.18.refs_4_ = bf16[272,3328]{1,0:T(8,128)(2,1)} collective-permute-done((bf16[272,3328]{1,0:T(8,128)(2,1)S(1)}, bf16[272,3328]{1,0:T(8,128)(2,1)}, u32[]{:S(2)}, u32[]{:S(2)}) %collective-permute-start.18) | collective-permute-done | bytes 1810464 | tf_op jit(solution)/shard_map/ppermute | solution.py:107
  198.6 1.7 dynamic-slice_bitcast_fusion.7
  200.3 1.5 pad_maximum_fusion.3
  201.8 4.6 %collective-permute-start.20 = (bf16[2,240,2176]{2,1,0:T(8,128)(2,1)}, bf16[2,240,2176]{2,1,0:T(8,128)(2,1)S(1)}, u32[]{:S(2)}, u32[]{:S(2)}) collective-permute-start(bf16[2,240,2176]{2,1,0:T(8,128)(2,1)} %pad_maximum_fusion.3), channel_id=1, source_target_pairs={{0,1},{1,0},{2,3},{3,2},{4,5},{5,4},{6,7},{7,6},{8,9},{9,8},{10,11... | collective-permute-start | bytes 6266888 | tf_op jit(solution)/shard_map/ppermute | solution.py:137
  206.3 1.9 collective-permute-start.22
  208.2 1.5 collective-permute-start.19
  210.3 1.3 copy-done.13
  211.6 4.1 %fusion.6 = (bf16[240,2176]{1,0:T(8,128)(2,1)}, f32[240,2176]{1,0:T(8,128)S(1)}) fusion(f32[960,2176]{1,0:T(8,128)} %get-tuple-element.152, s32[]{:T(128)S(6)} %select_n.492, bf16[2,240,2176]{2,1,0:T(8,128)(2,1)} %copy-done.13, s32[]{:T(128)S(6)} %select_n.493, s32[]{:T(128)S(6)} %select_n.491, s32[]{:T(128)S(6)} %select_n.489), kind=kLoop, calls=%fused_computation.19 | loop fusion | flops 2611200 | bytes 9400336 | tf_op jit(solution)/shard_map/convert_element_type | solution.py:311
  217.0 26.2 %shard_map.38 = (f32[1088,2176]{1,0:T(8,128)}, bf16[1088,2176]{1,0:T(8,128)(2,1)}, f32[1088,2176]{1,0:T(8,128)}, bf16[1088,2176]{1,0:T(8,128)(2,1)}) custom-call(s32[3]{0:T(128)} %pad_add_fusion.sp_ref, bf16[272,1280]{1,0:T(8,128)(2,1)} %get-tuple-element.154.refs_0_.refs_8_, bf16[272,1280]{1,0:T(8,128)(2,1)} %copy-done.8, ...), custom_call_target="tpu_custom_call" | custom-call | flops 10000000000 | bytes 1000000 | tf_op jit(solution)/shard_map/pallas_call | solution.py:257
  243.2 4.9 %collective-permute-done.19.refs_7_ = bf16[240,3328]{1,0:T(8,128)(2,1)} collective-permute-done((bf16[240,3328]{1,0:T(8,128)(2,1)}, bf16[240,3328]{1,0:T(8,128)(2,1)}, u32[]{:S(2)}, u32[]{:S(2)}) %collective-permute-start.19) | collective-permute-done | bytes 1597472 | tf_op jit(solution)/shard_map/ppermute | solution.py:107
  249.4 1.8 dynamic-slice_bitcast_fusion.3
  252.3 1.3 collective-permute-start.25
  253.6 3.0 collective-permute-done.23
  256.6 4.4 %fusion.4 = (bf16[272,2176]{1,0:T(8,128)(2,1)}, f32[272,2176]{1,0:T(8,128)S(1)}) fusion(f32[1088,2176]{1,0:T(8,128)} %get-tuple-element.171, s32[]{:T(128)S(6)} %select_n.496, bf16[2,272,2176]{2,1,0:T(8,128)(2,1)} %collective-permute-done.23, s32[]{:T(128)S(6)} %select_n.493, s32[]{:T(128)S(6)} %select_n.491, s32[]{:T(128)S(6)} %select_n.497), kind=kLoop, calls=%fused_computation.10 | loop fusion | flops 2959360 | bytes 10653712 | tf_op jit(solution)/shard_map/convert_element_type | solution.py:311
  262.2 24.3 %shard_map.39 = (f32[960,2176]{1,0:T(8,128)}, bf16[960,2176]{1,0:T(8,128)(2,1)}) custom-call(s32[3]{0:T(128)} %pad_add_fusion.sp_ref, f32[960,2176]{1,0:T(8,128)} %get-tuple-element.179.refs_0_, bf16[240,3328]{1,0:T(8,128)(2,1)} %copy-done.1, bf16[240,3328]{1,0:T(8,128)(2,1)} %collective-permute-done.refs_2_, ...), custom_call_target="tpu_custom_call" | custom-call | flops 10000000000 | bytes 1000000 | tf_op jit(solution)/shard_map/pallas_call | solution.py:257
  286.5 1.7 dynamic-slice_bitcast_fusion.5
  288.4 9.1 %collective-permute-done.25.refs_7_ = bf16[272,3328]{1,0:T(8,128)(2,1)} collective-permute-done((bf16[272,3328]{1,0:T(8,128)(2,1)}, bf16[272,3328]{1,0:T(8,128)(2,1)}, u32[]{:S(2)}, u32[]{:S(2)}) %collective-permute-start.25) | collective-permute-done | bytes 1810464 | tf_op jit(solution)/shard_map/ppermute | solution.py:107
  297.5 1.3 add_convert_fusion
  299.4 1.5 collective-permute-start.28
  300.9 2.3 collective-permute-done.26
  303.2 1.4 convert_add_fusion.5
  305.8 27.0 %shard_map.40 = (f32[1088,2176]{1,0:T(8,128)}, bf16[1088,2176]{1,0:T(8,128)(2,1)}) custom-call(s32[3]{0:T(128)} %pad_add_fusion.sp_ref, f32[1088,2176]{1,0:T(8,128)} %get-tuple-element.204.refs_0_, bf16[272,3328]{1,0:T(8,128)(2,1)} %copy-done, bf16[272,3328]{1,0:T(8,128)(2,1)} %copy-done.16, bf16[272,3328]{1,0:T(8,128)(2,1)} %copy-done.15, ...), custom_call_target="tpu_custom_call" | custom-call | flops 10000000000 | bytes 1000000 | tf_op jit(solution)/shard_map/pallas_call | solution.py:257
  332.8 1.8 dynamic-slice_bitcast_fusion.1
  335.9 1.8 add_convert_fusion.1
  339.8 2.9 collective-permute-done.29
  342.7 3.8 fusion
  346.8 1.7 collective-permute-start.32
  348.5 1.8 collective-permute-start.34
  350.3 1.4 collective-permute-done.32
  351.8 3.4 collective-permute-done.33
  355.1 17.2 %collective-permute-done.34 = bf16[240,128]{1,0:T(8,128)(2,1)S(1)} collective-permute-done((bf16[240,128]{1,0:T(8,128)(2,1)S(1)}, bf16[240,128]{1,0:T(8,128)(2,1)S(1)}, u32[]{:S(2)}, u32[]{:S(2)}) %collective-permute-start.34) | collective-permute-done | bytes 61472 | tf_op jit(solution)/shard_map/ppermute | solution.py:146
  372.4 1.7 collective-permute-done.30
  374.2 2.6 fusion.3
  376.7 1.8 collective-permute-start.36
  378.5 1.9 collective-permute-start.38
  380.4 2.1 collective-permute-start.35
  382.5 2.9 collective-permute-done.37
  387.9 11.6 %shard_map.41 = bf16[512,2048]{1,0:T(8,128)(2,1)} custom-call(s32[1]{0:T(128)} %bitcast.where_ref, bf16[512,2048]{1,0:T(8,128)(2,1)S(1)} %pad_maximum_fusion.2.q_ref, bf16[1024,512]{1,0:T(8,128)(2,1)S(1)} %pad_maximum_fusion.7.kv_ref), custom_call_target="tpu_custom_call" | custom-call | flops 6000000000 | bytes 5000000 | tf_op jit(solution)/shard_map/pallas_call | solution.py:83
  (102 shorter events, 25.7 us)
Async XLA Ops:
  1.5 120.6 %copy-start.1 = (bf16[240,3328]{1,0:T(8,128)(2,1)}, bf16[240,3328]{1,0:T(8,128)(2,1)S(1)}, u32[]{:S(2)}) copy-start(bf16[240,3328]{1,0:T(8,128)(2,1)S(1)} %slice.48.refs_1_) | copy-start | bytes 4792324
  1.5 39.5 %collective-permute-start = (bf16[240,3328]{1,0:T(8,128)(2,1)S(1)}, bf16[240,3328]{1,0:T(8,128)(2,1)}, u32[]{:S(2)}, u32[]{:S(2)}) collective-permute-start(bf16[240,3328]{1,0:T(8,128)(2,1)S(1)} %slice.48.refs_1_), channel_id=1, source_target_pairs={{4,8},{8,4},{5,9},{9,5},{6,10},{10,6},{7,11},{11,7},{20,24},{24,20... | collective-permute-start | bytes 4792328 | tf_op jit(solution)/shard_map/ppermute | solution.py:107
  3.4 39.2 %collective-permute-start.1 = (bf16[240,3328]{1,0:T(8,128)(2,1)S(1)}, bf16[240,3328]{1,0:T(8,128)(2,1)}, u32[]{:S(2)}, u32[]{:S(2)}) collective-permute-start(bf16[240,3328]{1,0:T(8,128)(2,1)S(1)} %slice.48.refs_1_), channel_id=1, source_target_pairs={{4,0},{8,12},{5,1},{9,13},{6,2},{10,14},{7,3},{11,15},{20,16},{24,... | collective-permute-start | bytes 4792328 | tf_op jit(solution)/shard_map/ppermute | solution.py:107
  7.0 34.0 %collective-permute-start.3 = (bf16[272,1280]{1,0:T(8,128)(2,1)}, bf16[272,1280]{1,0:T(8,128)(2,1)}, u32[]{:S(2)}, u32[]{:S(2)}) collective-permute-start(bf16[272,1280]{1,0:T(8,128)(2,1)} %get-tuple-element.129), channel_id=1, source_target_pairs={{0,4},{12,8},{1,5},{13,9},{2,6},{14,10},{3,7},{15,11},{16,20},{28,... | collective-permute-start | bytes 2088968 | tf_op jit(solution)/shard_map/ppermute | solution.py:107
  16.7 24.3 %collective-permute-start.2 = (bf16[240,1280]{1,0:T(8,128)(2,1)}, bf16[240,1280]{1,0:T(8,128)(2,1)}, u32[]{:S(2)}, u32[]{:S(2)}) collective-permute-start(bf16[240,1280]{1,0:T(8,128)(2,1)} %get-tuple-element.128), channel_id=1, source_target_pairs={{0,4},{12,8},{1,5},{13,9},{2,6},{14,10},{3,7},{15,11},{16,20},{28,... | collective-permute-start | bytes 1843208 | tf_op jit(solution)/shard_map/ppermute | solution.py:107
  20.4 141.7 %copy-start = (bf16[272,3328]{1,0:T(8,128)(2,1)}, bf16[272,3328]{1,0:T(8,128)(2,1)S(1)}, u32[]{:S(2)}) copy-start(bf16[272,3328]{1,0:T(8,128)(2,1)S(1)} %slice.51.refs_1_) | copy-start | bytes 5431300
  42.6 41.3 %collective-permute-start.7 = (bf16[272,3328]{1,0:T(8,128)(2,1)S(1)}, bf16[272,3328]{1,0:T(8,128)(2,1)S(1)}, u32[]{:S(2)}, u32[]{:S(2)}) collective-permute-start(bf16[272,3328]{1,0:T(8,128)(2,1)S(1)} %slice.51.refs_1_), channel_id=1, source_target_pairs={{4,0},{8,12},{5,1},{9,13},{6,2},{10,14},{7,3},{11,15},{20,16},{24,... | collective-permute-start | bytes 5431304 | tf_op jit(solution)/shard_map/ppermute | solution.py:107
  44.1 32.1 %collective-permute-start.4 = (bf16[320,2176]{1,0:T(8,128)(2,1)S(1)}, bf16[320,2176]{1,0:T(8,128)(2,1)S(1)}, u32[]{:S(2)}, u32[]{:S(2)}) collective-permute-start(bf16[320,2176]{1,0:T(8,128)(2,1)S(1)} %get-tuple-element.115), channel_id=1, source_target_pairs={{0,4},{12,8},{1,5},{13,9},{2,6},{14,10},{3,7},{15,11},{16,20},{28,... | collective-permute-start | bytes 4177928 | tf_op jit(solution)/shard_map/ppermute | solution.py:107
  48.3 1.4 collective-permute-start.6
  49.0 0.7 collective-permute-start.5
  49.8 36.2 %copy-start.9 = (bf16[240,1280]{1,0:T(8,128)(2,1)}, bf16[240,1280]{1,0:T(8,128)(2,1)S(1)}, u32[]{:S(2)}) copy-start(bf16[240,1280]{1,0:T(8,128)(2,1)S(1)} %collective-permute-done.5.refs_3_.refs_11_) | copy-start | bytes 1843204
  49.8 36.2 %copy-start.7 = (bf16[272,1280]{1,0:T(8,128)(2,1)}, bf16[272,1280]{1,0:T(8,128)(2,1)S(1)}, u32[]{:S(2)}) copy-start(bf16[272,1280]{1,0:T(8,128)(2,1)S(1)} %collective-permute-done.6.refs_3_.refs_11_) | copy-start | bytes 2088964
  76.2 88.4 %copy-start.2 = (bf16[320,2176]{1,0:T(8,128)(2,1)}, bf16[320,2176]{1,0:T(8,128)(2,1)S(1)}, u32[]{:S(2)}) copy-start(bf16[320,2176]{1,0:T(8,128)(2,1)S(1)} %collective-permute-done.4.refs_12_) | copy-start | bytes 4177924
  83.9 80.7 %copy-start.15 = (bf16[272,3328]{1,0:T(8,128)(2,1)}, bf16[272,3328]{1,0:T(8,128)(2,1)S(1)}, u32[]{:S(2)}) copy-start(bf16[272,3328]{1,0:T(8,128)(2,1)S(1)} %collective-permute-done.7.refs_3_) | copy-start | bytes 5431300
  83.9 36.9 %collective-permute-start.9 = (bf16[272,3328]{1,0:T(8,128)(2,1)S(1)}, bf16[272,3328]{1,0:T(8,128)(2,1)S(1)}, u32[]{:S(2)}, u32[]{:S(2)}) collective-permute-start(bf16[272,3328]{1,0:T(8,128)(2,1)S(1)} %slice.51.refs_1_), channel_id=1, source_target_pairs={{4,8},{8,4},{5,9},{9,5},{6,10},{10,6},{7,11},{11,7},{20,24},{24,20... | collective-permute-start | bytes 5431304 | tf_op jit(solution)/shard_map/ppermute | solution.py:107
  84.7 36.2 %collective-permute-start.10 = (bf16[240,3328]{1,0:T(8,128)(2,1)}, bf16[240,3328]{1,0:T(8,128)(2,1)S(1)}, u32[]{:S(2)}, u32[]{:S(2)}) collective-permute-start(bf16[240,3328]{1,0:T(8,128)(2,1)} %collective-permute-done.refs_2_), channel_id=1, source_target_pairs={{4,0},{8,12},{5,1},{9,13},{6,2},{10,14},{7,3},{11,15},{20,16},{24,... | collective-permute-start | bytes 4792328 | tf_op jit(solution)/shard_map/ppermute | solution.py:107
  86.0 31.3 %collective-permute-start.8 = (bf16[320,2176]{1,0:T(8,128)(2,1)S(1)}, bf16[320,2176]{1,0:T(8,128)(2,1)S(1)}, u32[]{:S(2)}, u32[]{:S(2)}) collective-permute-start(bf16[320,2176]{1,0:T(8,128)(2,1)S(1)} %get-tuple-element.121), channel_id=1, source_target_pairs={{0,4},{12,8},{1,5},{13,9},{2,6},{14,10},{3,7},{15,11},{16,20},{28,... | collective-permute-start | bytes 4177928 | tf_op jit(solution)/shard_map/ppermute | solution.py:107
  90.3 29.1 %collective-permute-start.11 = (bf16[320,2176]{1,0:T(8,128)(2,1)S(1)}, bf16[320,2176]{1,0:T(8,128)(2,1)S(1)}, u32[]{:S(2)}, u32[]{:S(2)}) collective-permute-start(bf16[320,2176]{1,0:T(8,128)(2,1)S(1)} %collective-permute-done.4.refs_12_), channel_id=1, source_target_pairs={{0,16},{16,0},{1,17},{17,1},{2,18},{18,2},{3,19},{19,3},{4,20},{20... | collective-permute-start | bytes 4177928 | tf_op jit(solution)/shard_map/ppermute | solution.py:107
  117.3 47.4 %copy-start.3 = (bf16[320,2176]{1,0:T(8,128)(2,1)}, bf16[320,2176]{1,0:T(8,128)(2,1)S(1)}, u32[]{:S(2)}) copy-start(bf16[320,2176]{1,0:T(8,128)(2,1)S(1)} %collective-permute-done.8.refs_13_) | copy-start | bytes 4177924
  119.4 45.3 %copy-start.4 = (bf16[320,2176]{1,0:T(8,128)(2,1)}, bf16[320,2176]{1,0:T(8,128)(2,1)S(1)}, u32[]{:S(2)}) copy-start(bf16[320,2176]{1,0:T(8,128)(2,1)S(1)} %collective-permute-done.11.refs_14_) | copy-start | bytes 4177924
  120.8 1.3 copy-start.18
  120.8 43.8 %copy-start.16 = (bf16[272,3328]{1,0:T(8,128)(2,1)}, bf16[272,3328]{1,0:T(8,128)(2,1)S(1)}, u32[]{:S(2)}) copy-start(bf16[272,3328]{1,0:T(8,128)(2,1)S(1)} %collective-permute-done.9.refs_2_) | copy-start | bytes 5431300
  120.8 41.3 %collective-permute-start.15 = (bf16[272,3328]{1,0:T(8,128)(2,1)S(1)}, bf16[272,3328]{1,0:T(8,128)(2,1)S(1)}, u32[]{:S(2)}, u32[]{:S(2)}) collective-permute-start(bf16[272,3328]{1,0:T(8,128)(2,1)S(1)} %collective-permute-done.9.refs_2_), channel_id=1, source_target_pairs={{4,0},{8,12},{5,1},{9,13},{6,2},{10,14},{7,3},{11,15},{20,16},{24,... | collective-permute-start | bytes 5431304 | tf_op jit(solution)/shard_map/ppermute | solution.py:107
  122.2 36.4 %collective-permute-start.12 = (bf16[240,3328]{1,0:T(8,128)(2,1)S(1)}, bf16[240,3328]{1,0:T(8,128)(2,1)}, u32[]{:S(2)}, u32[]{:S(2)}) collective-permute-start(bf16[240,3328]{1,0:T(8,128)(2,1)S(1)} %slice.48.refs_1_), channel_id=1, source_target_pairs={{0,4},{12,8},{1,5},{13,9},{2,6},{14,10},{3,7},{15,11},{16,20},{28,... | collective-permute-start | bytes 4792328 | tf_op jit(solution)/shard_map/ppermute | solution.py:107
  128.7 28.6 %collective-permute-start.16 = (bf16[320,2176]{1,0:T(8,128)(2,1)S(1)}, bf16[320,2176]{1,0:T(8,128)(2,1)S(1)}, u32[]{:S(2)}, u32[]{:S(2)}) collective-permute-start(bf16[320,2176]{1,0:T(8,128)(2,1)S(1)} %collective-permute-done.8.refs_13_), channel_id=1, source_target_pairs={{0,16},{16,0},{1,17},{17,1},{2,18},{18,2},{3,19},{19,3},{4,20},{20... | collective-permute-start | bytes 4177928 | tf_op jit(solution)/shard_map/ppermute | solution.py:107
  129.9 1.4 collective-permute-start.14
  130.6 0.7 collective-permute-start.13
  131.3 33.3 %copy-start.10 = (bf16[240,1280]{1,0:T(8,128)(2,1)}, bf16[240,1280]{1,0:T(8,128)(2,1)S(1)}, u32[]{:S(2)}) copy-start(bf16[240,1280]{1,0:T(8,128)(2,1)S(1)} %collective-permute-done.13.refs_1_.refs_9_) | copy-start | bytes 1843204
  131.3 33.3 %copy-start.8 = (bf16[272,1280]{1,0:T(8,128)(2,1)}, bf16[272,1280]{1,0:T(8,128)(2,1)S(1)}, u32[]{:S(2)}) copy-start(bf16[272,1280]{1,0:T(8,128)(2,1)S(1)} %collective-permute-done.14.refs_1_.refs_9_) | copy-start | bytes 2088964
  157.3 7.4 %copy-start.5 = (bf16[320,2176]{1,0:T(8,128)(2,1)}, bf16[320,2176]{1,0:T(8,128)(2,1)S(1)}, u32[]{:S(2)}) copy-start(bf16[320,2176]{1,0:T(8,128)(2,1)S(1)} %collective-permute-done.16.refs_15_) | copy-start | bytes 4177924
  162.1 2.6 copy-start.17
  162.1 36.4 %collective-permute-start.18 = (bf16[272,3328]{1,0:T(8,128)(2,1)S(1)}, bf16[272,3328]{1,0:T(8,128)(2,1)}, u32[]{:S(2)}, u32[]{:S(2)}) collective-permute-start(bf16[272,3328]{1,0:T(8,128)(2,1)S(1)} %slice.51.refs_1_), channel_id=1, source_target_pairs={{0,4},{12,8},{1,5},{13,9},{2,6},{14,10},{3,7},{15,11},{16,20},{28,... | collective-permute-start | bytes 5431304 | tf_op jit(solution)/shard_map/ppermute | solution.py:107
  164.7 25.2 %collective-permute-start.17 = (bf16[240,3328]{1,0:T(8,128)(2,1)}, bf16[240,3328]{1,0:T(8,128)(2,1)S(1)}, u32[]{:S(2)}, u32[]{:S(2)}) collective-permute-start(bf16[240,3328]{1,0:T(8,128)(2,1)} %collective-permute-done.12.refs_4_), channel_id=1, source_target_pairs={{4,8},{8,4},{5,9},{9,5},{6,10},{10,6},{7,11},{11,7},{20,24},{24,20... | collective-permute-start | bytes 4792328 | tf_op jit(solution)/shard_map/ppermute | solution.py:107
  189.9 10.4 %copy-start.19 = (bf16[240,3328]{1,0:T(8,128)(2,1)}, bf16[240,3328]{1,0:T(8,128)(2,1)S(1)}, u32[]{:S(2)}) copy-start(bf16[240,3328]{1,0:T(8,128)(2,1)S(1)} %collective-permute-done.17.refs_6_) | copy-start | bytes 4792324
  201.8 8.5 %collective-permute-start.20 = (bf16[2,240,2176]{2,1,0:T(8,128)(2,1)}, bf16[2,240,2176]{2,1,0:T(8,128)(2,1)S(1)}, u32[]{:S(2)}, u32[]{:S(2)}) collective-permute-start(bf16[2,240,2176]{2,1,0:T(8,128)(2,1)} %pad_maximum_fusion.3), channel_id=1, source_target_pairs={{0,1},{1,0},{2,3},{3,2},{4,5},{5,4},{6,7},{7,6},{8,9},{9,8},{10,11... | collective-permute-start | bytes 6266888 | tf_op jit(solution)/shard_map/ppermute | solution.py:137
  206.3 41.8 %collective-permute-start.22 = (bf16[272,3328]{1,0:T(8,128)(2,1)}, bf16[272,3328]{1,0:T(8,128)(2,1)}, u32[]{:S(2)}, u32[]{:S(2)}) collective-permute-start(bf16[272,3328]{1,0:T(8,128)(2,1)} %collective-permute-done.18.refs_4_), channel_id=1, source_target_pairs={{4,8},{8,4},{5,9},{9,5},{6,10},{10,6},{7,11},{11,7},{20,24},{24,20... | collective-permute-start | bytes 5431304 | tf_op jit(solution)/shard_map/ppermute | solution.py:107
  208.2 39.9 %collective-permute-start.19 = (bf16[240,3328]{1,0:T(8,128)(2,1)}, bf16[240,3328]{1,0:T(8,128)(2,1)}, u32[]{:S(2)}, u32[]{:S(2)}) collective-permute-start(bf16[240,3328]{1,0:T(8,128)(2,1)} %copy-done.19), channel_id=1, source_target_pairs={{4,0},{8,12},{5,1},{9,13},{6,2},{10,14},{7,3},{11,15},{20,16},{24,... | collective-permute-start | bytes 4792328 | tf_op jit(solution)/shard_map/ppermute | solution.py:107
  210.3 1.3 copy-start.13
  215.7 32.4 %collective-permute-start.21 = (bf16[240,2176]{1,0:T(8,128)(2,1)}, bf16[240,2176]{1,0:T(8,128)(2,1)S(1)}, u32[]{:S(2)}, u32[]{:S(2)}) collective-permute-start(bf16[240,2176]{1,0:T(8,128)(2,1)} %get-tuple-element.164), channel_id=1, source_target_pairs={{0,2},{1,3},{2,0},{3,1},{4,6},{5,7},{6,4},{7,5},{8,10},{9,11},{10,... | collective-permute-start | bytes 3133448 | tf_op jit(solution)/shard_map/ppermute | solution.py:141
  251.4 5.2 %collective-permute-start.23 = (bf16[2,272,2176]{2,1,0:T(8,128)(2,1)S(1)}, bf16[2,272,2176]{2,1,0:T(8,128)(2,1)}, u32[]{:S(2)}, u32[]{:S(2)}) collective-permute-start(bf16[2,272,2176]{2,1,0:T(8,128)(2,1)S(1)} %pad_maximum_fusion), channel_id=1, source_target_pairs={{0,1},{1,0},{2,3},{3,2},{4,5},{5,4},{6,7},{7,6},{8,9},{9,8},{10,11... | collective-permute-start | bytes 7102472 | tf_op jit(solution)/shard_map/ppermute | solution.py:137
  252.3 45.2 %collective-permute-start.25 = (bf16[272,3328]{1,0:T(8,128)(2,1)}, bf16[272,3328]{1,0:T(8,128)(2,1)}, u32[]{:S(2)}, u32[]{:S(2)}) collective-permute-start(bf16[272,3328]{1,0:T(8,128)(2,1)} %collective-permute-done.22.refs_6_), channel_id=1, source_target_pairs={{4,0},{8,12},{5,1},{9,13},{6,2},{10,14},{7,3},{11,15},{20,16},{24,... | collective-permute-start | bytes 5431304 | tf_op jit(solution)/shard_map/ppermute | solution.py:107
  261.0 36.5 %collective-permute-start.24 = (bf16[272,2176]{1,0:T(8,128)(2,1)}, bf16[272,2176]{1,0:T(8,128)(2,1)S(1)}, u32[]{:S(2)}, u32[]{:S(2)}) collective-permute-start(bf16[272,2176]{1,0:T(8,128)(2,1)} %get-tuple-element.189), channel_id=1, source_target_pairs={{0,2},{1,3},{2,0},{3,1},{4,6},{5,7},{6,4},{7,5},{8,10},{9,11},{10,... | collective-permute-start | bytes 3551240 | tf_op jit(solution)/shard_map/ppermute | solution.py:141
  288.2 15.0 %copy-start.14 = (f32[960,2176]{1,0:T(8,128)S(1)}, f32[960,2176]{1,0:T(8,128)}, u32[]{:S(2)}) copy-start(f32[960,2176]{1,0:T(8,128)} %get-tuple-element.194) | copy-start | bytes 25067524
  298.8 4.4 %collective-permute-start.26 = (bf16[2,240,2176]{2,1,0:T(8,128)(2,1)S(1)}, bf16[2,240,2176]{2,1,0:T(8,128)(2,1)S(1)}, u32[]{:S(2)}, u32[]{:S(2)}) collective-permute-start(bf16[2,240,2176]{2,1,0:T(8,128)(2,1)S(1)} %pad_maximum_fusion.4), channel_id=1, source_target_pairs={{0,1},{1,0},{2,3},{3,2},{4,5},{5,4},{6,7},{7,6},{8,9},{9,8},{10,11... | collective-permute-start | bytes 6266888 | tf_op jit(solution)/shard_map/ppermute | solution.py:137
  299.4 35.5 %collective-permute-start.28 = (bf16[240,2176]{1,0:T(8,128)(2,1)}, bf16[240,2176]{1,0:T(8,128)(2,1)S(1)}, u32[]{:S(2)}, u32[]{:S(2)}) collective-permute-start(bf16[240,2176]{1,0:T(8,128)(2,1)} %add_convert_fusion.2), channel_id=1, source_target_pairs={{4,0},{8,12},{5,1},{9,13},{6,2},{10,14},{7,3},{11,15},{20,16},{24,... | collective-permute-start | bytes 3133448 | tf_op jit(solution)/shard_map/ppermute | solution.py:107
  304.6 30.3 %collective-permute-start.27 = (bf16[240,2176]{1,0:T(8,128)(2,1)}, bf16[240,2176]{1,0:T(8,128)(2,1)}, u32[]{:S(2)}, u32[]{:S(2)}) collective-permute-start(bf16[240,2176]{1,0:T(8,128)(2,1)} %get-tuple-element.196), channel_id=1, source_target_pairs={{0,2},{1,3},{2,0},{3,1},{4,6},{5,7},{6,4},{7,5},{8,10},{9,11},{10,... | collective-permute-start | bytes 3133448 | tf_op jit(solution)/shard_map/ppermute | solution.py:141
  334.9 1.0 copy-start.20
  337.7 34.6 %copy-start.6 = (bf16[240,2176]{1,0:T(8,128)(2,1)}, bf16[240,2176]{1,0:T(8,128)(2,1)S(1)}, u32[]{:S(2)}) copy-start(bf16[240,2176]{1,0:T(8,128)(2,1)S(1)} %add_convert_fusion.1) | copy-start | bytes 3133444
  337.7 5.0 %collective-permute-start.29 = (bf16[2,272,2176]{2,1,0:T(8,128)(2,1)S(1)}, bf16[2,272,2176]{2,1,0:T(8,128)(2,1)S(1)}, u32[]{:S(2)}, u32[]{:S(2)}) collective-permute-start(bf16[2,272,2176]{2,1,0:T(8,128)(2,1)S(1)} %pad_maximum_fusion.1), channel_id=1, source_target_pairs={{0,1},{1,0},{2,3},{3,2},{4,5},{5,4},{6,7},{7,6},{8,9},{9,8},{10,11... | collective-permute-start | bytes 7102472 | tf_op jit(solution)/shard_map/ppermute | solution.py:137
  338.6 33.9 %collective-permute-start.31 = (bf16[272,2176]{1,0:T(8,128)(2,1)}, bf16[272,2176]{1,0:T(8,128)(2,1)S(1)}, u32[]{:S(2)}, u32[]{:S(2)}) collective-permute-start(bf16[272,2176]{1,0:T(8,128)(2,1)} %add_convert_fusion), channel_id=1, source_target_pairs={{4,0},{8,12},{5,1},{9,13},{6,2},{10,14},{7,3},{11,15},{20,16},{24,... | collective-permute-start | bytes 3551240 | tf_op jit(solution)/shard_map/ppermute | solution.py:107
  342.7 3.8 copy-start.11
  346.6 27.6 %collective-permute-start.30 = (bf16[272,2176]{1,0:T(8,128)(2,1)}, bf16[272,2176]{1,0:T(8,128)(2,1)}, u32[]{:S(2)}, u32[]{:S(2)}) collective-permute-start(bf16[272,2176]{1,0:T(8,128)(2,1)} %fusion), channel_id=1, source_target_pairs={{0,2},{1,3},{2,0},{3,1},{4,6},{5,7},{6,4},{7,5},{8,10},{9,11},{10,... | collective-permute-start | bytes 3551240 | tf_op jit(solution)/shard_map/ppermute | solution.py:141
  346.8 5.0 %collective-permute-start.32 = (bf16[240,128]{1,0:T(8,128)(2,1)S(1)}, bf16[240,128]{1,0:T(8,128)(2,1)S(1)}, u32[]{:S(2)}, u32[]{:S(2)}) collective-permute-start(bf16[240,128]{1,0:T(8,128)(2,1)S(1)} %slice.66), channel_id=1, source_target_pairs={{0,12},{4,8},{8,4},{12,0},{1,13},{5,9},{9,5},{13,1},{2,14},{6,10},... | collective-permute-start | bytes 184328 | tf_op jit(solution)/shard_map/ppermute | solution.py:146
  348.5 6.6 %collective-permute-start.33 = (bf16[240,128]{1,0:T(8,128)(2,1)S(1)}, bf16[240,128]{1,0:T(8,128)(2,1)S(1)}, u32[]{:S(2)}, u32[]{:S(2)}) collective-permute-start(bf16[240,128]{1,0:T(8,128)(2,1)S(1)} %slice.66), channel_id=1, source_target_pairs={{0,8},{4,12},{8,0},{12,4},{1,9},{5,13},{9,1},{13,5},{2,10},{6,14},... | collective-permute-start | bytes 184328 | tf_op jit(solution)/shard_map/ppermute | solution.py:146
  348.5 23.8 %collective-permute-start.34 = (bf16[240,128]{1,0:T(8,128)(2,1)S(1)}, bf16[240,128]{1,0:T(8,128)(2,1)S(1)}, u32[]{:S(2)}, u32[]{:S(2)}) collective-permute-start(bf16[240,128]{1,0:T(8,128)(2,1)S(1)} %slice.66), channel_id=1, source_target_pairs={{0,4},{4,0},{8,12},{12,8},{1,5},{5,1},{9,13},{13,9},{2,6},{6,2},{1... | collective-permute-start | bytes 184328 | tf_op jit(solution)/shard_map/ppermute | solution.py:146
  350.3 23.8 %copy-start.12 = (bf16[2,272,2176]{2,1,0:T(8,128)(2,1)S(1)}, bf16[2,272,2176]{2,1,0:T(8,128)(2,1)}, u32[]{:S(2)}) copy-start(bf16[2,272,2176]{2,1,0:T(8,128)(2,1)} %copy-done.11) | copy-start | bytes 7102468
  376.7 5.8 %collective-permute-start.36 = (bf16[272,128]{1,0:T(8,128)(2,1)S(1)}, bf16[272,128]{1,0:T(8,128)(2,1)S(1)}, u32[]{:S(2)}, u32[]{:S(2)}) collective-permute-start(bf16[272,128]{1,0:T(8,128)(2,1)S(1)} %slice.67), channel_id=1, source_target_pairs={{0,12},{4,8},{8,4},{12,0},{1,13},{5,9},{9,5},{13,1},{2,14},{6,10},... | collective-permute-start | bytes 208904 | tf_op jit(solution)/shard_map/ppermute | solution.py:146
  378.5 7.0 %collective-permute-start.37 = (bf16[272,128]{1,0:T(8,128)(2,1)S(1)}, bf16[272,128]{1,0:T(8,128)(2,1)S(1)}, u32[]{:S(2)}, u32[]{:S(2)}) collective-permute-start(bf16[272,128]{1,0:T(8,128)(2,1)S(1)} %slice.67), channel_id=1, source_target_pairs={{0,8},{4,12},{8,0},{12,4},{1,9},{5,13},{9,1},{13,5},{2,10},{6,14},... | collective-permute-start | bytes 208904 | tf_op jit(solution)/shard_map/ppermute | solution.py:146
  378.5 7.0 %collective-permute-start.38 = (bf16[272,128]{1,0:T(8,128)(2,1)S(1)}, bf16[272,128]{1,0:T(8,128)(2,1)S(1)}, u32[]{:S(2)}, u32[]{:S(2)}) collective-permute-start(bf16[272,128]{1,0:T(8,128)(2,1)S(1)} %slice.67), channel_id=1, source_target_pairs={{0,4},{4,0},{8,12},{12,8},{1,5},{5,1},{9,13},{13,9},{2,6},{6,2},{1... | collective-permute-start | bytes 208904 | tf_op jit(solution)/shard_map/ppermute | solution.py:146
  380.4 6.4 %slice-start = ((bf16[240,2176]{1,0:T(8,128)(2,1)}), bf16[240,2048]{1,0:T(8,128)(2,1)S(1)}, s32[]{:S(2)}) async-start(bf16[240,2176]{1,0:T(8,128)(2,1)} %copy-done.6), calls=%async_computation | async-start | bytes 1966080 | tf_op jit(solution)/shard_map/slice | solution.py:422
  380.4 6.1 %collective-permute-start.35 = (bf16[240,512]{1,0:T(8,128)(2,1)S(1)}, bf16[240,512]{1,0:T(8,128)(2,1)S(1)}, u32[]{:S(2)}, u32[]{:S(2)}) collective-permute-start(bf16[240,512]{1,0:T(8,128)(2,1)S(1)} %pad_maximum_fusion.11), channel_id=1, source_target_pairs={{0,1},{1,0},{2,3},{3,2},{4,5},{5,4},{6,7},{7,6},{8,9},{9,8},{10,11... | collective-permute-start | bytes 737288 | tf_op jit(solution)/shard_map/ppermute | solution.py:137
  385.5 2.1 collective-permute-start.39
